TPU v7x, 32 devices: a whole 2x2x4 slice. The times are simulated.
32 devices in a mesh: dp: 4 (over x, core), seq: 4 (over z), rep: 2 (over y).
Axes of the slice: x: 2, y: 2, z: 4, core: 2. Of those that a mesh axis runs over, the one named last changes fastest.
Arguments:
- tokens: bfloat16 [4, 1024, 2048], P('dp', ('seq', 'rep')), may hold values from -6 to 6
- segments: int32 [4, 1024], P('dp'), may hold values from 0 to 20, as said below
- routes: int32 [4, 1024, 8], P('dp', ('seq', 'rep')), may hold values from 0 to 31, all different within a row
- priority: int32 [4, 1024], P('dp', ('seq', 'rep')), may hold values from 0 to 127, as said below
- w_query: bfloat16 [2048, 4096], P(('dp', 'seq', 'rep')), may hold values from -0.125 to 0.125
- key_matrix: bfloat16 [2048, 512], P(('dp', 'seq', 'rep')), may hold values from -0.125 to 0.125
- value_matrix: bfloat16 [2048, 512], P(('dp', 'seq', 'rep')), may hold values from -0.125 to 0.125
- w_out: bfloat16 [4096, 2048], P(('dp', 'seq', 'rep')), may hold values from -1.5 to 1.5
- w_router: bfloat16 [2048, 32], P(('dp', 'seq', 'rep')), may hold values from -0.0625 to 0.0625
- attn_gain: bfloat16 [2048], P(('dp', 'seq', 'rep')), may hold values from 0.5 to 1.5
- moe_gain: bfloat16 [2048], P(('dp', 'seq', 'rep')), may hold values from 0.5 to 1.5
- query_gain: bfloat16 [128], P(('dp', 'seq', 'rep')), may hold values from 0.5 to 1.5
- key_norm_weight: bfloat16 [128], P(('dp', 'seq', 'rep')), may hold values from 0.5 to 1.5
- w_gate_up: bfloat16 [32, 2048, 1536], P(('dp', 'seq', 'rep')), may hold values from -0.125 to 0.125
- w_down: bfloat16 [32, 768, 2048], P(('dp', 'seq', 'rep')), may hold values from -0.875 to 0.875
- cotangent: bfloat16 [4, 1024, 2048], P('dp', ('seq', 'rep')), may hold values from -6 to 6
Outputs:
- mixed: bfloat16 [4, 1024, 2048], P('dp', ('seq', 'rep'))
- input_grad: float32 [4, 1024, 2048], P('dp', ('seq', 'rep'))
- grad_query: float32 [2048, 4096], P(('dp', 'seq', 'rep'))
- grad_key: float32 [2048, 512], P(('dp', 'seq', 'rep'))
- grad_value: float32 [2048, 512], P(('dp', 'seq', 'rep'))
- grad_out: float32 [4096, 2048], P(('dp', 'seq', 'rep'))
- grad_router: float32 [2048, 32], P(('dp', 'seq', 'rep'))
- grad_attn_gain: float32 [2048], P(('dp', 'seq', 'rep'))
- grad_moe_gain: float32 [2048], P(('dp', 'seq', 'rep'))
- grad_query_gain: float32 [128], P(('dp', 'seq', 'rep'))
- grad_key_gain: float32 [128], P(('dp', 'seq', 'rep'))
- grad_gate_up: float32 [32, 2048, 1536], P(('dp', 'seq', 'rep'))
- grad_down: float32 [32, 768, 2048], P(('dp', 'seq', 'rep'))
Inputs may be any that keep to these rules, and one draw needn't show every extreme that they name: `segments`: along each sequence the document numbers start at 0 and never fall; documents hold 1024 * 200 / 4096 (rounded up) to 500 tokens, except that one sequence is a single document and a sequence's last document may be shorter. `priority`: within each aligned block of 128 tokens the values are a permutation.
All inputs are finite; a program needn't handle non-finite values.
Results may differ from a plain program's by a relative error of at most 0.02.
Values may be sent and summed in bfloat16 or wider, within the bound.
No kernel may reach another device: no remote copies, remote signals or barrier semaphores. Data moves between devices by JAX's collectives and lax.ppermute only.
A program may use at most 320 MiB of HBM per device.

v0:
```python
import jax
import jax.numpy as jnp
from jax import lax
from jax.sharding import PartitionSpec as P

QUERY_HEADS = 32
KEY_VALUE_HEADS = 4
HEAD_DIM = 128
FFE = 768
TOPK = 8


EPS = 1e-06
THETA = 1000000.0
BIG_NEG = -1e30


def norm_rows(values, gain_vector):
    return values * lax.rsqrt(jnp.mean(values * values, axis=-1, keepdims=True) + EPS) * gain_vector


def rotary_angles(positions):
    half_width = HEAD_DIM // 2
    frequency = THETA ** (-2.0 * jnp.arange(half_width, dtype=jnp.float32) / HEAD_DIM)
    angles = positions.astype(jnp.float32)[:, None] * frequency[None, :]
    return (jnp.cos(angles), jnp.sin(angles))


def rotate_heads(values, cosine_table, sine_values):
    half_width = HEAD_DIM // 2
    first_half = values[..., :half_width]
    second_half = values[..., half_width:]
    cosine_table = cosine_table[:, None, :]
    sine_values = sine_values[:, None, :]
    return jnp.concatenate(
        [
            first_half * cosine_table - second_half * sine_values,
            second_half * cosine_table + first_half * sine_values,
        ],
        axis=-1,
    )


def build_head_tensors(projected, gain_vector, head_count, cosine_table, sine_values):
    shaped = projected.reshape(projected.shape[0], head_count, HEAD_DIM)
    return rotate_heads(norm_rows(shaped, gain_vector), cosine_table, sine_values)


def swiglu(gate_in, up_in):
    return jax.nn.silu(gate_in) * up_in


def block_at(blocks, index):
    return tuple((lax.dynamic_index_in_dim(member, index, 0, keepdims=False) for member in blocks))


def masked_scores(grouped_queries, key_block, query_doc, query_pos, key_doc, key_pos):
    allowed = (query_doc[:, None] == key_doc[None, :]) & (key_pos[None, :] <= query_pos[:, None])
    scores = jnp.einsum(
        "hgid,khd->hgik", grouped_queries, key_block, preferred_element_type=jnp.float32
    ) * HEAD_DIM ** (-0.5)
    return (jnp.where(allowed[None, None], scores, BIG_NEG), allowed[None, None])


def softmax_logsum(grouped_queries, blocks, query_doc, query_pos, first_block, end_block):

    def advance(index, state_pair):
        running_max, running_sum = state_pair
        key_block, value_block, key_doc, key_pos = block_at(blocks, index)
        scores, allowed = masked_scores(
            grouped_queries, key_block, query_doc, query_pos, key_doc, key_pos
        )
        new_max = jnp.maximum(running_max, jnp.max(scores, axis=-1))
        exponent = jnp.where(allowed, jnp.exp(scores - new_max[..., None]), 0.0)
        return (new_max, running_sum * jnp.exp(running_max - new_max) + jnp.sum(exponent, axis=-1))

    begin_max = jnp.full(grouped_queries.shape[:3], BIG_NEG, jnp.float32)
    begin_sum = jnp.zeros(grouped_queries.shape[:3], jnp.float32)
    final_max, final_sum = lax.fori_loop(first_block, end_block, advance, (begin_max, begin_sum))
    return final_max + jnp.log(final_sum)


def attention_output(
    grouped_queries, blocks, query_doc, query_pos, log_total, first_block, end_block
):

    def advance(index, running):
        key_block, value_block, key_doc, key_pos = block_at(blocks, index)
        scores, allowed = masked_scores(
            grouped_queries, key_block, query_doc, query_pos, key_doc, key_pos
        )
        attend_probs = jnp.where(allowed, jnp.exp(scores - log_total[..., None]), 0.0).astype(
            jnp.bfloat16
        )
        return running + jnp.einsum(
            "hgik,khd->hgid", attend_probs, value_block, preferred_element_type=jnp.float32
        )

    return lax.fori_loop(
        first_block, end_block, advance, jnp.zeros(grouped_queries.shape, jnp.float32)
    )


def attention_grads(
    grouped_queries,
    grouped_gradient,
    blocks,
    query_doc,
    query_pos,
    log_total,
    delta_rows,
    first_block,
    end_block,
):

    def advance(index, running):
        query_acc, key_store, value_store = running
        key_block, value_block, key_doc, key_pos = block_at(blocks, index)
        scores, allowed = masked_scores(
            grouped_queries, key_block, query_doc, query_pos, key_doc, key_pos
        )
        attend_probs = jnp.where(allowed, jnp.exp(scores - log_total[..., None]), 0.0)
        grad_probs = jnp.einsum(
            "hgid,khd->hgik", grouped_gradient, value_block, preferred_element_type=jnp.float32
        )
        grad_scores = (attend_probs * (grad_probs - delta_rows[..., None])).astype(jnp.bfloat16)
        query_acc = query_acc + jnp.einsum(
            "hgik,khd->hgid", grad_scores, key_block, preferred_element_type=jnp.float32
        )
        grad_key_block = jnp.einsum(
            "hgik,hgid->khd", grad_scores, grouped_queries, preferred_element_type=jnp.float32
        )
        grad_value_block = jnp.einsum(
            "hgik,hgid->khd",
            attend_probs.astype(jnp.bfloat16),
            grouped_gradient,
            preferred_element_type=jnp.float32,
        )
        key_store = lax.dynamic_update_index_in_dim(key_store, grad_key_block, index, 0)
        value_store = lax.dynamic_update_index_in_dim(value_store, grad_value_block, index, 0)
        return (query_acc, key_store, value_store)

    store_shape = blocks[0].shape
    begin = (
        jnp.zeros(grouped_queries.shape, jnp.float32),
        jnp.zeros(store_shape, jnp.float32),
        jnp.zeros(store_shape, jnp.float32),
    )
    return lax.fori_loop(first_block, end_block, advance, begin)


def key_blocks(gathered_keys, gathered_values, documents, sequence_length):
    rows_per_block = min(512, sequence_length)
    count_of_blocks = sequence_length // rows_per_block
    key_pos = jnp.arange(sequence_length, dtype=jnp.int32).reshape(count_of_blocks, rows_per_block)
    return (
        gathered_keys.reshape(count_of_blocks, rows_per_block, KEY_VALUE_HEADS, HEAD_DIM),
        gathered_values.reshape(count_of_blocks, rows_per_block, KEY_VALUE_HEADS, HEAD_DIM),
        documents.reshape(count_of_blocks, rows_per_block),
        key_pos,
    )


def body(
    tokens,
    segments,
    routes,
    priority,
    w_query,
    key_matrix,
    value_matrix,
    w_out,
    w_router,
    attn_gain,
    moe_gain,
    query_gain,
    key_norm_weight,
    w_gate_up,
    w_down,
    cotangent,
):
    resident_rows = tokens.shape[1]
    model_width = tokens.shape[2]
    sequence_length = segments.shape[1]
    heads_per_group = QUERY_HEADS // KEY_VALUE_HEADS
    devices = lax.axis_size(("dp", "seq", "rep"))
    local_experts = w_gate_up.shape[0]
    experts_total = devices * local_experts
    capacity = resident_rows * TOPK // experts_total
    attention_scale = HEAD_DIM ** (-0.5)
    rows_per_block = min(512, sequence_length)
    gathered = (
        lax.all_gather(w_query, ("dp", "seq", "rep"), axis=0, tiled=True),
        lax.all_gather(key_matrix, ("dp", "seq", "rep"), axis=0, tiled=True),
        lax.all_gather(value_matrix, ("dp", "seq", "rep"), axis=0, tiled=True),
        lax.all_gather(w_out, ("dp", "seq", "rep"), axis=0, tiled=True),
        lax.all_gather(w_router, ("dp", "seq", "rep"), axis=0, tiled=True),
        lax.all_gather(attn_gain, ("dp", "seq", "rep"), axis=0, tiled=True),
        lax.all_gather(moe_gain, ("dp", "seq", "rep"), axis=0, tiled=True),
        lax.all_gather(query_gain, ("dp", "seq", "rep"), axis=0, tiled=True),
        lax.all_gather(key_norm_weight, ("dp", "seq", "rep"), axis=0, tiled=True),
    )
    query_weights, key_weights, value_weights, out_weights, router_weights = (
        gathered[0],
        gathered[1],
        gathered[2],
        gathered[3],
        gathered[4],
    )
    first_gain = gathered[5].astype(jnp.float32)
    second_gain = gathered[6].astype(jnp.float32)
    query_norm_gain = gathered[7].astype(jnp.float32)
    key_norm_gain = gathered[8].astype(jnp.float32)
    inputs = tokens[0].astype(jnp.float32)
    normed_f, first_pull = jax.vjp(norm_rows, inputs, first_gain)
    normed = normed_f.astype(jnp.bfloat16)
    query_proj = jnp.dot(normed, query_weights, preferred_element_type=jnp.float32)
    projected_keys = jnp.dot(normed, key_weights, preferred_element_type=jnp.float32)
    value_head_rows = jnp.dot(normed, value_weights, preferred_element_type=jnp.float32).astype(
        jnp.bfloat16
    )
    start_row = lax.axis_index(("seq", "rep")) * resident_rows
    positions = start_row + jnp.arange(resident_rows, dtype=jnp.int32)
    cosine_table, sine_values = rotary_angles(positions)

    def prepare_both(query_in, incoming_keys, query_gain_in, incoming_key_weight):
        return (
            build_head_tensors(query_in, query_gain_in, QUERY_HEADS, cosine_table, sine_values),
            build_head_tensors(
                incoming_keys, incoming_key_weight, KEY_VALUE_HEADS, cosine_table, sine_values
            ),
        )

    (query_rot, rotated_keys), heads_pull = jax.vjp(
        prepare_both, query_proj, projected_keys, query_norm_gain, key_norm_gain
    )
    query_head_rows = query_rot.astype(jnp.bfloat16)
    flattened_keys = rotated_keys.astype(jnp.bfloat16).reshape(
        resident_rows, KEY_VALUE_HEADS * HEAD_DIM
    )
    gathered_keys, gathered_values = (
        lax.all_gather(flattened_keys, ("seq", "rep"), axis=0, tiled=True),
        lax.all_gather(value_head_rows, ("seq", "rep"), axis=0, tiled=True),
    )
    documents = segments[0]
    query_doc = lax.dynamic_slice_in_dim(documents, start_row, resident_rows)
    doc_start = jnp.sum((documents < query_doc[0]).astype(jnp.int32))
    first_block = doc_start // rows_per_block
    end_block = (start_row + resident_rows - 1) // rows_per_block + 1
    grouped_queries = query_head_rows.reshape(
        resident_rows, KEY_VALUE_HEADS, heads_per_group, HEAD_DIM
    ).transpose(1, 2, 0, 3)
    blocks = key_blocks(gathered_keys, gathered_values, documents, sequence_length)
    log_total = softmax_logsum(
        grouped_queries, blocks, query_doc, positions, first_block, end_block
    )
    attended_f = attention_output(
        grouped_queries, blocks, query_doc, positions, log_total, first_block, end_block
    )
    attended = (
        attended_f.transpose(2, 0, 1, 3)
        .reshape(resident_rows, QUERY_HEADS * HEAD_DIM)
        .astype(jnp.bfloat16)
    )
    middle = inputs + jnp.dot(attended, out_weights, preferred_element_type=jnp.float32)
    routed_f, second_pull = jax.vjp(norm_rows, middle, second_gain)
    routed = routed_f.astype(jnp.bfloat16)
    logits = jnp.dot(routed, router_weights, preferred_element_type=jnp.float32)
    choice_ids = routes[0]
    expert_ids = jnp.arange(experts_total, dtype=jnp.int32)
    pick_table = choice_ids[:, :, None] == expert_ids[None, None, :]
    chosen = jnp.sum(jnp.where(pick_table, logits[:, None, :], 0.0), axis=-1)
    gate_values = jax.nn.softmax(chosen, axis=-1)
    priority_rank = priority[0]
    earlier = (priority_rank[None, :] < priority_rank[:, None]).astype(jnp.bfloat16)
    counts = jnp.sum(pick_table, axis=1).astype(jnp.bfloat16)
    rank_table = jnp.dot(earlier, counts, preferred_element_type=jnp.float32)
    slot_index = jnp.sum(jnp.where(pick_table, rank_table[:, None, :], 0.0), axis=-1).astype(
        jnp.int32
    )
    kept_pairs = slot_index < capacity
    targets = jnp.where(kept_pairs, choice_ids * capacity + slot_index, experts_total * capacity)
    pair_count = resident_rows * TOPK
    sources = (
        jnp.full((experts_total * capacity,), pair_count, jnp.int32)
        .at[targets.reshape(-1)]
        .set(jnp.arange(pair_count, dtype=jnp.int32), mode="drop")
    )
    padded = jnp.concatenate([routed, jnp.zeros((1, model_width), jnp.bfloat16)], axis=0)
    outgoing = padded[sources // TOPK].reshape(devices, local_experts, capacity, model_width)
    arrived_rows = lax.all_to_all(
        outgoing, ("dp", "seq", "rep"), split_axis=0, concat_axis=0, tiled=True
    )
    gate_up_rows = jnp.einsum(
        "sjcd,jdf->sjcf", arrived_rows, w_gate_up, preferred_element_type=jnp.float32
    )
    hidden_rows = swiglu(gate_up_rows[..., :FFE], gate_up_rows[..., FFE:]).astype(jnp.bfloat16)
    result_rows = jnp.einsum(
        "sjcf,jfd->sjcd", hidden_rows, w_down, preferred_element_type=jnp.float32
    ).astype(jnp.bfloat16)
    returned = lax.all_to_all(
        result_rows, ("dp", "seq", "rep"), split_axis=0, concat_axis=0, tiled=True
    ).reshape(experts_total * capacity, model_width)
    safe_targets = jnp.minimum(targets, experts_total * capacity - 1)
    picked_rows = returned[safe_targets].astype(jnp.float32)
    weights_kept = jnp.where(kept_pairs, gate_values, 0.0)
    mixed = (middle + jnp.sum(weights_kept[..., None] * picked_rows, axis=1)).astype(jnp.bfloat16)
    grad_output = cotangent[0].astype(jnp.float32)
    grad_gates = jnp.where(kept_pairs, jnp.sum(picked_rows * grad_output[:, None, :], axis=-1), 0.0)
    grad_pairs = (
        (weights_kept[..., None] * grad_output[:, None, :])
        .astype(jnp.bfloat16)
        .reshape(pair_count, model_width)
    )
    grad_padded = jnp.concatenate([grad_pairs, jnp.zeros((1, model_width), jnp.bfloat16)], axis=0)
    grad_outgoing = grad_padded[sources].reshape(devices, local_experts, capacity, model_width)
    grad_arrived = lax.all_to_all(
        grad_outgoing, ("dp", "seq", "rep"), split_axis=0, concat_axis=0, tiled=True
    )
    hidden_f, hidden_pull = jax.vjp(swiglu, gate_up_rows[..., :FFE], gate_up_rows[..., FFE:])
    hidden = hidden_f.astype(jnp.bfloat16)
    grad_hidden = jnp.einsum(
        "sjcd,jfd->sjcf", grad_arrived, w_down, preferred_element_type=jnp.float32
    )
    grad_down = jnp.einsum(
        "sjcf,sjcd->jfd", hidden, grad_arrived, preferred_element_type=jnp.float32
    )
    grad_gate_in, grad_up_in = hidden_pull(grad_hidden)
    grad_act = jnp.concatenate([grad_gate_in, grad_up_in], axis=-1).astype(jnp.bfloat16)
    grad_gate_up = jnp.einsum(
        "sjcd,sjcf->jdf", arrived_rows, grad_act, preferred_element_type=jnp.float32
    )
    grad_sent = jnp.einsum(
        "sjcf,jdf->sjcd", grad_act, w_gate_up, preferred_element_type=jnp.float32
    ).astype(jnp.bfloat16)
    grad_back = lax.all_to_all(
        grad_sent, ("dp", "seq", "rep"), split_axis=0, concat_axis=0, tiled=True
    ).reshape(experts_total * capacity, model_width)
    grad_routed = jnp.sum(
        jnp.where(kept_pairs[..., None], grad_back[safe_targets].astype(jnp.float32), 0.0), axis=1
    )
    regathered = (
        lax.all_gather(w_query, ("dp", "seq", "rep"), axis=0, tiled=True),
        lax.all_gather(key_matrix, ("dp", "seq", "rep"), axis=0, tiled=True),
        lax.all_gather(value_matrix, ("dp", "seq", "rep"), axis=0, tiled=True),
        lax.all_gather(w_out, ("dp", "seq", "rep"), axis=0, tiled=True),
        lax.all_gather(w_router, ("dp", "seq", "rep"), axis=0, tiled=True),
    )
    query_weights, key_weights, value_weights, out_weights, router_weights = regathered
    grad_chosen = gate_values * (
        grad_gates - jnp.sum(gate_values * grad_gates, axis=-1, keepdims=True)
    )
    grad_logits = jnp.sum(jnp.where(pick_table, grad_chosen[..., None], 0.0), axis=1).astype(
        jnp.bfloat16
    )
    grad_router = jnp.einsum("td,te->de", routed, grad_logits, preferred_element_type=jnp.float32)
    grad_routed = grad_routed + jnp.einsum(
        "te,de->td", grad_logits, router_weights, preferred_element_type=jnp.float32
    )
    grad_middle_norm, grad_moe_gain = second_pull(grad_routed)
    grad_middle = grad_output + grad_middle_norm
    grad_branch = grad_middle.astype(jnp.bfloat16)
    grad_out = jnp.einsum("tf,td->fd", attended, grad_branch, preferred_element_type=jnp.float32)
    attended_gradient = jnp.einsum(
        "td,fd->tf", grad_branch, out_weights, preferred_element_type=jnp.float32
    ).astype(jnp.bfloat16)
    gathered_keys, gathered_values = (
        lax.all_gather(flattened_keys, ("seq", "rep"), axis=0, tiled=True),
        lax.all_gather(value_head_rows, ("seq", "rep"), axis=0, tiled=True),
    )
    blocks = key_blocks(gathered_keys, gathered_values, documents, sequence_length)
    grouped_gradient = attended_gradient.reshape(
        resident_rows, KEY_VALUE_HEADS, heads_per_group, HEAD_DIM
    ).transpose(1, 2, 0, 3)
    delta_rows = jnp.sum(grouped_gradient.astype(jnp.float32) * attended_f, axis=-1)
    grad_query_grouped, key_gradient_pieces, value_gradient_pieces = attention_grads(
        grouped_queries,
        grouped_gradient,
        blocks,
        query_doc,
        positions,
        log_total,
        delta_rows,
        first_block,
        end_block,
    )
    full_key_gradient = (key_gradient_pieces * attention_scale).reshape(
        sequence_length, KEY_VALUE_HEADS * HEAD_DIM
    )
    full_value_gradient = value_gradient_pieces.reshape(sequence_length, KEY_VALUE_HEADS * HEAD_DIM)
    local_key_gradient, grad_value_own = (
        lax.psum_scatter(
            full_key_gradient.astype(jnp.bfloat16), ("seq", "rep"), scatter_dimension=0, tiled=True
        ).astype(jnp.float32),
        lax.psum_scatter(
            full_value_gradient.astype(jnp.bfloat16),
            ("seq", "rep"),
            scatter_dimension=0,
            tiled=True,
        ).astype(jnp.float32),
    )
    rotated_query_gradient = (
        grad_query_grouped.transpose(2, 0, 1, 3).reshape(resident_rows, QUERY_HEADS, HEAD_DIM)
        * attention_scale
    )
    grad_query_proj, grad_key_proj, grad_query_gain, grad_key_gain = heads_pull(
        (
            rotated_query_gradient,
            local_key_gradient.reshape(resident_rows, KEY_VALUE_HEADS, HEAD_DIM),
        )
    )
    grad_query_low = grad_query_proj.astype(jnp.bfloat16)
    grad_key_low = grad_key_proj.astype(jnp.bfloat16)
    grad_value_low = grad_value_own.astype(jnp.bfloat16)
    grad_query = jnp.einsum("td,tf->df", normed, grad_query_low, preferred_element_type=jnp.float32)
    grad_key = jnp.einsum("td,tf->df", normed, grad_key_low, preferred_element_type=jnp.float32)
    grad_value = jnp.einsum("td,tf->df", normed, grad_value_low, preferred_element_type=jnp.float32)
    grad_normed = jnp.einsum(
        "tf,df->td", grad_query_low, query_weights, preferred_element_type=jnp.float32
    )
    grad_normed = grad_normed + jnp.einsum(
        "tf,df->td", grad_key_low, key_weights, preferred_element_type=jnp.float32
    )
    grad_normed = grad_normed + jnp.einsum(
        "tf,df->td", grad_value_low, value_weights, preferred_element_type=jnp.float32
    )
    grad_inputs_norm, grad_attn_gain = first_pull(grad_normed)
    input_grad = grad_middle + grad_inputs_norm
    owned = (
        lax.psum_scatter(grad_query, ("dp", "seq", "rep"), scatter_dimension=0, tiled=True),
        lax.psum_scatter(grad_key, ("dp", "seq", "rep"), scatter_dimension=0, tiled=True),
        lax.psum_scatter(grad_value, ("dp", "seq", "rep"), scatter_dimension=0, tiled=True),
        lax.psum_scatter(grad_out, ("dp", "seq", "rep"), scatter_dimension=0, tiled=True),
        lax.psum_scatter(grad_router, ("dp", "seq", "rep"), scatter_dimension=0, tiled=True),
        lax.psum_scatter(grad_attn_gain, ("dp", "seq", "rep"), scatter_dimension=0, tiled=True),
        lax.psum_scatter(grad_moe_gain, ("dp", "seq", "rep"), scatter_dimension=0, tiled=True),
        lax.psum_scatter(grad_query_gain, ("dp", "seq", "rep"), scatter_dimension=0, tiled=True),
        lax.psum_scatter(grad_key_gain, ("dp", "seq", "rep"), scatter_dimension=0, tiled=True),
    )
    return (
        mixed[None],
        input_grad[None],
        owned[0],
        owned[1],
        owned[2],
        owned[3],
        owned[4],
        owned[5],
        owned[6],
        owned[7],
        owned[8],
        grad_gate_up,
        grad_down,
    )


def solution(mesh):
    placed = (
        P("dp", ("seq", "rep"), None),
        P("dp", None),
        P("dp", ("seq", "rep"), None),
        P("dp", ("seq", "rep")),
        P(("dp", "seq", "rep"), None),
        P(("dp", "seq", "rep"), None),
        P(("dp", "seq", "rep"), None),
        P(("dp", "seq", "rep"), None),
        P(("dp", "seq", "rep"), None),
        P(("dp", "seq", "rep")),
        P(("dp", "seq", "rep")),
        P(("dp", "seq", "rep")),
        P(("dp", "seq", "rep")),
        P(("dp", "seq", "rep"), None, None),
        P(("dp", "seq", "rep"), None, None),
        P("dp", ("seq", "rep"), None),
    )
    return jax.shard_map(
        body,
        mesh=mesh,
        in_specs=placed,
        out_specs=(
            P("dp", ("seq", "rep"), None),
            P("dp", ("seq", "rep"), None),
            P(("dp", "seq", "rep"), None),
            P(("dp", "seq", "rep"), None),
            P(("dp", "seq", "rep"), None),
            P(("dp", "seq", "rep"), None),
            P(("dp", "seq", "rep"), None),
            P(("dp", "seq", "rep")),
            P(("dp", "seq", "rep")),
            P(("dp", "seq", "rep")),
            P(("dp", "seq", "rep")),
            P(("dp", "seq", "rep"), None, None),
            P(("dp", "seq", "rep"), None, None),
        ),
        check_vma=False,
    )
```

profile of v0, /device:TPU:0, one launch (start us, length us, event | category | flops | bytes accessed | tf_op | source)
XLA Modules:
  0.0 2928.9 jit_solution(5646648879672564200)
XLA Ops:
  12.1 42.2 %all-reduce.15 = (bf16[2048]{0:T(1024)(128)(2,1)S(1)}, bf16[128]{0:T(256)(128)(2,1)S(1)}, bf16[128]{0:T(256)(128)(2,1)S(1)}, bf16[2048]{0:T(1024)(128)(2,1)S(1)}) all-reduce(bf16[2048]{0:T(1024)(128)(2,1)S(1)} %dynamic-update-slice, bf16[128]{0:T(256)(128)(2,1)S(1)} %dynamic-update-slice.1, ...), channel_id=1, replica_groups=mesh['dp'=4,'seq'=4,'rep'=2] {'dp','seq','rep'}, use_global_device_ids=true, to_apply=%add.6 | all-reduce | flops 4352 | bytes 17408
  56.1 14.3 all-gather.8.cloned.1.call-done
  78.6 50.2 %all-gather.14.cloned.1.call-done = bf16[2048,512]{1,0:T(8,128)(2,1)} async-done(((bf16[64,512]{1,0:T(8,128)(2,1)}), bf16[2048,512]{1,0:T(8,128)(2,1)}) %all-gather.14.cloned.1.call-update) | async-done | bytes 2097168 | tf_op jit(solution)/shard_map/all_gather | solution.py:195
  137.4 68.3 %all-gather = bf16[32,64,32]{1,2,0:T(8,128)(2,1)S(1)} all-gather(bf16[1,64,32]{1,2,0:T(8,128)(2,1)S(1)} %bitcast.438), channel_id=1, replica_groups=mesh['dp'=4,'seq'=4,'rep'=2] {'dp','seq','rep'}, dimensions={0}, use_global_device_ids=true | all-gather | bytes 135168 | tf_op jit(solution)/shard_map/all_gather | solution.py:197
  217.4 112.1 %all-gather.12.cloned.1.call-done = bf16[2048,4096]{1,0:T(8,128)(2,1)} async-done(((bf16[64,4096]{1,0:T(8,128)(2,1)}), bf16[2048,4096]{1,0:T(8,128)(2,1)}) %all-gather.12.cloned.1.call-update) | async-done | bytes 16777232 | tf_op jit(solution)/shard_map/all_gather | solution.py:193
  329.5 22.7 copy.111
  388.3 57.2 %all-gather.18.cloned.1.call-done = bf16[4096,2048]{1,0:T(8,128)(2,1)} async-done(((bf16[128,2048]{1,0:T(8,128)(2,1)}), bf16[4096,2048]{1,0:T(8,128)(2,1)}) %all-gather.18.cloned.1.call-update) | async-done | bytes 16777232 | tf_op jit(solution)/shard_map/all_gather | solution.py:196
  494.7 77.7 %all-to-all-done = bf16[32,1,32,2048]{3,2,1,0:T(8,128)(2,1)} async-done(((bf16[32,1,32,2048]{3,2,1,0:T(8,128)(2,1)}), bf16[32,1,32,2048]{3,2,1,0:T(8,128)(2,1)}, u32[]{:S(2)}, u32[]{:S(2)}) %all-to-all-start) | async-done | bytes 4194336 | tf_op jit(solution)/shard_map/all_to_all | solution.py:291
  587.7 84.3 %all-to-all-done.2 = bf16[32,1,32,2048]{3,2,1,0:T(8,128)(2,1)} async-done(((bf16[32,1,32,2048]{3,2,1,0:T(8,128)(2,1)}), bf16[32,1,32,2048]{3,2,1,0:T(8,128)(2,1)}, u32[]{:S(2)}, u32[]{:S(2)}) %all-to-all-start.2) | async-done | bytes 4194336 | tf_op jit(solution)/shard_map/all_to_all | solution.py:317
  703.5 84.8 %all-to-all-done.1 = bf16[32,1,32,2048]{3,2,1,0:T(8,128)(2,1)} async-done(((bf16[32,1,32,2048]{3,2,1,0:T(8,128)(2,1)}), bf16[32,1,32,2048]{3,2,1,0:T(8,128)(2,1)}, u32[]{:S(2)}, u32[]{:S(2)}) %all-to-all-start.1) | async-done | bytes 4194336 | tf_op jit(solution)/shard_map/all_to_all | solution.py:301
  810.2 77.8 %all-to-all-done.3 = bf16[32,1,32,2048]{3,2,1,0:T(8,128)(2,1)} async-done(((bf16[32,1,32,2048]{3,2,1,0:T(8,128)(2,1)}), bf16[32,1,32,2048]{3,2,1,0:T(8,128)(2,1)}, u32[]{:S(2)}, u32[]{:S(2)}) %all-to-all-start.3) | async-done | bytes 4194336 | tf_op jit(solution)/shard_map/all_to_all | solution.py:336
  908.6 12.8 fusion.95
  926.8 12.5 while.42
  947.9 68.1 %reduce-scatter.10.cloned.1.call-done = bf16[128,512]{1,0:T(8,128)(2,1)} async-done(((bf16[1024,512]{1,0:T(8,128)(2,1)}), bf16[128,512]{1,0:T(8,128)(2,1)}) %reduce-scatter.10.cloned.1.call-update) | async-done | bytes 131088 | tf_op jit(solution)/shard_map/reduce_scatter | solution.py:392
  1021.4 61.5 %reduce-scatter.12.cloned.1.call-done = bf16[128,512]{1,0:T(8,128)(2,1)} async-done(((bf16[1024,512]{1,0:T(8,128)(2,1)}), bf16[128,512]{1,0:T(8,128)(2,1)}) %reduce-scatter.12.cloned.1.call-update) | async-done | bytes 131088 | tf_op jit(solution)/shard_map/reduce_scatter | solution.py:395
  1087.8 14.4 fusion.121
  1111.9 13.2 fusion.118
  1146.1 12.5 fusion.162
  1158.6 60.6 %reduce-scatter.22.cloned.1.call-done = f32[64,32]{1,0:T(8,128)} async-done(((f32[2048,32]{1,0:T(8,128)}), f32[64,32]{1,0:T(8,128)}) %reduce-scatter.22.cloned.1.call-update) | async-done | bytes 8208
  1227.2 38.8 %all-reduce.14 = (f32[2048]{0:T(1024)S(1)}, f32[2048]{0:T(1024)S(1)}, f32[128]{0:T(128)S(1)}, f32[128]{0:T(128)S(1)}) all-reduce(f32[2048]{0:T(1024)S(1)} %get-tuple-element.461, f32[2048]{0:T(1024)S(1)} %copy-done.41, f32[128]{0:T(128)S(1)} %get-tuple-element.455, ...), channel_id=9, replica_groups=mesh['dp'=4,'seq'=4,'rep'=2] {'dp','seq','rep'}, use_global_device_ids=true, to_apply=%region_37.38.clone | all-reduce | flops 4352 | bytes 34816
  1271.4 91.2 %reduce-scatter.16.cloned.1.call-done = f32[64,512]{1,0:T(8,128)} async-done(((f32[2048,512]{1,0:T(8,128)}), f32[64,512]{1,0:T(8,128)}) %reduce-scatter.16.cloned.1.call-update) | async-done | bytes 131088 | tf_op jit(solution)/shard_map/reduce_scatter | solution.py:431
  1362.6 144.9 %reduce-scatter.18.cloned.1.call-done = f32[64,512]{1,0:T(8,128)} async-done(((f32[2048,512]{1,0:T(8,128)}), f32[64,512]{1,0:T(8,128)}) %reduce-scatter.18.cloned.1.call-update) | async-done | bytes 131088 | tf_op jit(solution)/shard_map/reduce_scatter | solution.py:432
  1507.5 705.8 %reduce-scatter.20.cloned.1.call-done = f32[128,2048]{1,0:T(8,128)} async-done(((f32[4096,2048]{1,0:T(8,128)}), f32[128,2048]{1,0:T(8,128)}) %reduce-scatter.20.cloned.1.call-update) | async-done | bytes 1048592 | tf_op jit(solution)/shard_map/reduce_scatter | solution.py:433
  2213.3 708.9 %reduce-scatter.14.cloned.1.call-done = f32[64,4096]{1,0:T(8,128)} async-done(((f32[2048,4096]{1,0:T(8,128)}), f32[64,4096]{1,0:T(8,128)}) %reduce-scatter.14.cloned.1.call-update) | async-done | bytes 1048592 | tf_op jit(solution)/shard_map/reduce_scatter | solution.py:430
  (310 shorter events, 298.7 us)
Async XLA Ops:
  7.2 664.8 %copy-start = (bf16[1,768,2048]{2,1,0:T(8,128)(2,1)S(1)}, bf16[1,768,2048]{2,1,0:T(8,128)(2,1)}, u32[]{:S(2)}) copy-start(bf16[1,768,2048]{2,1,0:T(8,128)(2,1)} %param.36) | copy-start | bytes 9437188
  7.2 63.1 %all-gather.8.cloned.1.call-start = ((), (), s32[]{:S(2)}) async-start(), calls=%async_computation.11 | async-start | bytes 2162688 | tf_op jit(solution)/shard_map/all_gather | solution.py:194
  7.9 120.8 %all-gather.14.cloned.1.call-start = ((), (), s32[]{:S(2)}) async-start(), calls=%async_computation.14 | async-start | bytes 2162688 | tf_op jit(solution)/shard_map/all_gather | solution.py:195
  8.7 199.5 %all-gather.10.cloned.1.call-start = ((), (), s32[]{:S(2)}) async-start(), calls=%async_computation.12 | async-start | bytes 1179648 | tf_op jit(solution)/shard_map/all_gather | solution.py:242
  54.4 297.8 %copy-start.31 = (f32[2048]{0:T(1024)}, f32[2048]{0:T(1024)S(1)}, u32[]{:S(2)}) copy-start(f32[2048]{0:T(1024)S(1)} %convert_element_type.220) | copy-start | bytes 24580
  55.8 296.4 %copy-start.42 = (f32[128]{0:T(128)}, f32[128]{0:T(128)S(1)}, u32[]{:S(2)}) copy-start(f32[128]{0:T(128)S(1)} %fusion.148) | copy-start | bytes 1540
  56.0 306.2 %copy-start.25 = (f32[128,64]{0,1:T(8,128)}, f32[128,64]{0,1:T(8,128)S(1)}, u32[]{:S(2)}) copy-start(f32[128,64]{0,1:T(8,128)S(1)} %get-tuple-element.575) | copy-start | bytes 98308
  56.0 306.2 %copy-start.28 = (f32[128,64]{0,1:T(8,128)}, f32[128,64]{0,1:T(8,128)S(1)}, u32[]{:S(2)}) copy-start(f32[128,64]{0,1:T(8,128)S(1)} %get-tuple-element.576) | copy-start | bytes 98308
  78.5 134.3 %all-gather.16.cloned.1.call-start = ((), (), s32[]{:S(2)}) async-start(), calls=%async_computation.15 | async-start | bytes 1179648 | tf_op jit(solution)/shard_map/all_gather | solution.py:243
  131.7 197.8 %all-gather.12.cloned.1.call-start = ((), (), s32[]{:S(2)}) async-start(), calls=%async_computation.13 | async-start | bytes 17301504 | tf_op jit(solution)/shard_map/all_gather | solution.py:193
  132.3 313.2 %all-gather.18.cloned.1.call-start = ((), (), s32[]{:S(2)}) async-start(), calls=%async_computation.16 | async-start | bytes 17301504 | tf_op jit(solution)/shard_map/all_gather | solution.py:196
  137.3 223.3 %copy-start.49 = (f32[128]{0:T(128)}, f32[128]{0:T(128)S(1)}, u32[]{:S(2)}) copy-start(f32[128]{0:T(128)S(1)} %convert_element_type.226) | copy-start | bytes 1540
  472.8 99.7 %all-to-all-start = ((bf16[32,1,32,2048]{3,2,1,0:T(8,128)(2,1)}), bf16[32,1,32,2048]{3,2,1,0:T(8,128)(2,1)}, u32[]{:S(2)}, u32[]{:S(2)}) async-start(bf16[32,1,32,2048]{3,2,1,0:T(8,128)(2,1)} %bitcast.407), calls=%async_computation | async-start | bytes 8388608 | tf_op jit(solution)/shard_map/all_to_all | solution.py:291
  572.5 99.5 %all-to-all-start.2 = ((bf16[32,1,32,2048]{3,2,1,0:T(8,128)(2,1)}), bf16[32,1,32,2048]{3,2,1,0:T(8,128)(2,1)}, u32[]{:S(2)}, u32[]{:S(2)}) async-start(bf16[32,1,32,2048]{3,2,1,0:T(8,128)(2,1)} %bitcast.408), calls=%async_computation.2 | async-start | bytes 8388608 | tf_op jit(solution)/shard_map/all_to_all | solution.py:317
  688.2 100.2 %all-to-all-start.1 = ((bf16[32,1,32,2048]{3,2,1,0:T(8,128)(2,1)}), bf16[32,1,32,2048]{3,2,1,0:T(8,128)(2,1)}, u32[]{:S(2)}, u32[]{:S(2)}) async-start(bf16[32,1,32,2048]{3,2,1,0:T(8,128)(2,1)} %convert_bitcast_fusion.1), calls=%async_computation.1 | async-start | bytes 8388608 | tf_op jit(solution)/shard_map/all_to_all | solution.py:301
  788.4 99.5 %all-to-all-start.3 = ((bf16[32,1,32,2048]{3,2,1,0:T(8,128)(2,1)}), bf16[32,1,32,2048]{3,2,1,0:T(8,128)(2,1)}, u32[]{:S(2)}, u32[]{:S(2)}) async-start(bf16[32,1,32,2048]{3,2,1,0:T(8,128)(2,1)} %convert_bitcast_fusion), calls=%async_computation.3 | async-start | bytes 8388608 | tf_op jit(solution)/shard_map/all_to_all | solution.py:336
  792.0 224.1 %reduce-scatter.10.cloned.1.call-start = ((), (), s32[]{:S(2)}) async-start(), calls=%async_computation.17 | async-start | bytes 1179648 | tf_op jit(solution)/shard_map/reduce_scatter | solution.py:392
  943.1 139.8 %reduce-scatter.12.cloned.1.call-start = ((), (), s32[]{:S(2)}) async-start(), calls=%async_computation.18 | async-start | bytes 1179648 | tf_op jit(solution)/shard_map/reduce_scatter | solution.py:395
  946.4 272.8 %reduce-scatter.22.cloned.1.call-start = ((), (), s32[]{:S(2)}) async-start(), calls=%async_computation.23 | async-start | bytes 1081344
  947.9 414.7 %reduce-scatter.16.cloned.1.call-start = ((), (), s32[]{:S(2)}) async-start(), calls=%async_computation.20 | async-start | bytes 4325376 | tf_op jit(solution)/shard_map/reduce_scatter | solution.py:431
  1021.4 486.1 %reduce-scatter.18.cloned.1.call-start = ((), (), s32[]{:S(2)}) async-start(), calls=%async_computation.21 | async-start | bytes 4325376 | tf_op jit(solution)/shard_map/reduce_scatter | solution.py:432
  1086.6 1126.7 %reduce-scatter.20.cloned.1.call-start = ((), (), s32[]{:S(2)}) async-start(), calls=%async_computation.22 | async-start | bytes 34603008 | tf_op jit(solution)/shard_map/reduce_scatter | solution.py:433
  1102.2 1820.0 %reduce-scatter.14.cloned.1.call-start = ((), (), s32[]{:S(2)}) async-start(), calls=%async_computation.19 | async-start | bytes 34603008 | tf_op jit(solution)/shard_map/reduce_scatter | solution.py:430
  1220.7 1701.5 %copy-start.1 = (bf16[1,768,2048]{2,1,0:T(8,128)(2,1)S(1)}, bf16[1,768,2048]{2,1,0:T(8,128)(2,1)}, u32[]{:S(2)}) copy-start(bf16[1,768,2048]{2,1,0:T(8,128)(2,1)} %param.36) | copy-start | bytes 9437188
  (55 other events, 1488.3 us)
Sparse Core Ops, SparseCore 0:
  11.0 59.2 all-gather.7
  73.3 55.4 all-gather.13
  131.5 39.7 all-gather.9
  173.8 39.0 all-gather.15
  215.8 113.6 all-gather.11
  332.4 113.0 all-gather.17
  943.2 72.8 reduce-scatter.9
  1020.4 62.4 reduce-scatter.11
  1085.1 134.0 reduce-scatter.21
  1222.1 140.4 reduce-scatter.15
  1365.5 141.9 reduce-scatter.17
  1510.3 702.8 reduce-scatter.19
  2216.3 705.8 reduce-scatter.13
where the time goes:
time: 2940 us; the launch traced here: 2930 us
  waiting for transfers between devices  2400 us (82%)
  matrix products  170 us (6%)
  blocking collectives  149 us (5%)
  local copies, waits for them, and re-layouts  132 us (4%)
  other arithmetic  41.1 us (1%)
    reduce_scatter x1, waiting for transfers between devices, body(): lax.psum_scatter(grad_query, ('dp', 'seq', 'rep'), scatter_dimension=0, t...  709 us
    reduce_scatter x1, waiting for transfers between devices, body(): lax.psum_scatter(grad_out, ('dp', 'seq', 'rep'), scatter_dimension=0, til...  706 us
    reduce_scatter x1, waiting for transfers between devices, body(): lax.psum_scatter(grad_value, ('dp', 'seq', 'rep'), scatter_dimension=0, t...  145 us
    all_gather x1, waiting for transfers between devices, body(): lax.all_gather(w_query, ('dp', 'seq', 'rep'), axis=0, tiled=True)  112 us
    reduce_scatter x1, waiting for transfers between devices, body(): lax.psum_scatter(grad_key, ('dp', 'seq', 'rep'), scatter_dimension=0, til...  91.2 us
    all_to_all x1, waiting for transfers between devices, body(): lax.all_to_all(result_rows, ('dp', 'seq', 'rep'), split_axis=0, concat_ax...  84.8 us
    all_to_all x1, waiting for transfers between devices, body(): lax.all_to_all(grad_outgoing, ('dp', 'seq', 'rep'), split_axis=0, concat_...  84.3 us
    unnamed x2, blocking collectives  81 us
  transfers between devices with their start and end apart: 17, of which 16 were waited for; matrix products, arithmetic and copies ran while one was open for 8% of the time, Pallas kernels for 0%

commit v1 on v0

v1 whole, which is shorter than its diff:
```python
import functools

import jax
import jax.numpy as jnp
from jax import lax
from jax.experimental import pallas as pl
from jax.experimental.pallas import tpu as pltpu
from jax.sharding import PartitionSpec as P

QUERY_HEADS = 32
KEY_VALUE_HEADS = 4
HEAD_DIM = 128
FFE = 768
TOPK = 8

EPS = 1e-06
THETA = 1000000.0
BIG_NEG = -1e30
ALL = ("dp", "seq", "rep")
PLANE = ("dp", "rep")
F32 = jnp.float32
BF16 = jnp.bfloat16
LOG2E = 1.4426950408889634
VMEM_LIMIT = 52 * 1024 * 1024


def norm_rows(values, gain_vector):
    return values * lax.rsqrt(jnp.mean(values * values, axis=-1, keepdims=True) + EPS) * gain_vector


def swap(blocks, axes):
    return lax.all_to_all(blocks, axes, split_axis=0, concat_axis=0, tiled=True)


def gather(shard, axes, count):
    return swap(jnp.broadcast_to(shard[None], (count,) + shard.shape), axes)


def dot(a, b):
    return jnp.dot(a, b, preferred_element_type=F32)


def dot_nt(a, b):
    return lax.dot_general(a, b, (((1,), (1,)), ((), ())), preferred_element_type=F32)


def dot_tn(a, b):
    return lax.dot_general(a, b, (((0,), (0,)), ((), ())), preferred_element_type=F32)


def rotary_tables(positions):
    half_width = HEAD_DIM // 2
    frequency = THETA ** (-2.0 * jnp.arange(half_width, dtype=F32) / HEAD_DIM)
    angles = positions.astype(F32)[:, None] * frequency[None, :]
    cosine, sine = jnp.cos(angles), jnp.sin(angles)
    return (
        jnp.concatenate([cosine, cosine], axis=-1),
        jnp.concatenate([-sine, sine], axis=-1),
    )


def write_bias(bias, query_doc, query_pos, key_doc):
    key_pos = lax.broadcasted_iota(jnp.int32, bias.shape, 1)
    allowed = (query_doc == key_doc) & (key_pos <= query_pos)
    bias[...] = jnp.where(allowed, 0.0, BIG_NEG)


def rotated(projected, gain, cosine, sine):
    scale = lax.rsqrt(jnp.mean(projected * projected, axis=-1, keepdims=True) + EPS)
    unit = projected * scale
    gained = unit * gain
    return scale, unit, gained * cosine + pltpu.roll(gained, HEAD_DIM // 2, 1) * sine


def forward_kernel(
    q_ref, k_ref, v_ref, qdoc_ref, kdoc_ref, qpos_ref, cos_ref, sin_ref, gain_ref, out_ref, total_ref, bias
):
    @pl.when(pl.program_id(1) == 0)
    def _():
        write_bias(bias, qdoc_ref[0], qpos_ref[...], kdoc_ref[0])

    _, _, turned = rotated(q_ref[...], gain_ref[...], cos_ref[...], sin_ref[...])
    factor = HEAD_DIM ** (-0.5) * LOG2E
    scores = dot_nt(turned.astype(BF16), k_ref[0]) * factor + bias[...]
    highest = jnp.max(scores, axis=-1, keepdims=True)
    exponent = jnp.exp2(scores - highest)
    total = jnp.sum(exponent, axis=-1, keepdims=True)
    probs = (exponent * (1.0 / total)).astype(BF16)
    out_ref[...] = dot(probs, v_ref[0]).astype(BF16)
    total_ref[0, 0] = highest + jnp.log2(total)


def backward_kernel(
    q_ref,
    k_ref,
    v_ref,
    qdoc_ref,
    kdoc_ref,
    qpos_ref,
    cos_ref,
    sin_ref,
    gain_ref,
    total_ref,
    grad_ref,
    dq_ref,
    dkv_ref,
    dgain_ref,
    bias,
    dk_sum,
    dv_sum,
):
    seq, head = pl.program_id(0), pl.program_id(1)

    @pl.when(head == 0)
    def _():
        write_bias(bias, qdoc_ref[0], qpos_ref[...], kdoc_ref[0])
        dk_sum[...] = jnp.zeros_like(dk_sum)
        dv_sum[...] = jnp.zeros_like(dv_sum)

    @pl.when((head == 0) & (seq == 0))
    def _():
        dgain_ref[...] = jnp.zeros_like(dgain_ref)

    gain, cosine, sine = gain_ref[...], cos_ref[...], sin_ref[...]
    scale, unit, turned = rotated(q_ref[...], gain, cosine, sine)
    turned = turned.astype(BF16)
    attention_scale = HEAD_DIM ** (-0.5)
    scores = dot_nt(turned, k_ref[0]) * (attention_scale * LOG2E) + bias[...]
    probs = jnp.exp2(scores - total_ref[0, 0])
    grad = grad_ref[...]
    grad_probs = dot_nt(grad, v_ref[0])
    delta = jnp.sum(probs * grad_probs, axis=-1, keepdims=True)
    grad_scores = (probs * (grad_probs - delta)).astype(BF16)
    dv_sum[...] += dot_tn(probs.astype(BF16), grad)
    dk_sum[...] += dot_tn(grad_scores, turned)
    grad_turned = dot(grad_scores, k_ref[0]) * attention_scale
    grad_gained = grad_turned * cosine - pltpu.roll(grad_turned, HEAD_DIM // 2, 1) * sine
    dgain_ref[...] += jnp.sum(grad_gained * unit, axis=0, keepdims=True)
    weighted = grad_gained * gain
    dq_ref[...] = (
        scale * (weighted - unit * jnp.mean(weighted * unit, axis=-1, keepdims=True))
    ).astype(BF16)

    @pl.when(head == pl.num_programs(1) - 1)
    def _():
        shape = dkv_ref.shape[:1] + dkv_ref.shape[2:3] + (HEAD_DIM,)
        dkv_ref[:, 0, :, :HEAD_DIM] = (dk_sum[...] * attention_scale).astype(BF16).reshape(shape)
        dkv_ref[:, 0, :, HEAD_DIM:] = dv_sum[...].astype(BF16).reshape(shape)


def attention_specs(rows, length):
    return [
        pl.BlockSpec((rows, HEAD_DIM), lambda s, h: (s, h)),
        pl.BlockSpec((1, length, HEAD_DIM), lambda s, h: (s, 0, 0)),
        pl.BlockSpec((1, length, HEAD_DIM), lambda s, h: (s, 0, 1)),
        pl.BlockSpec((1, rows, 1), lambda s, h: (s, 0, 0)),
        pl.BlockSpec((1, 1, length), lambda s, h: (s, 0, 0)),
        pl.BlockSpec((rows, 1), lambda s, h: (0, 0)),
        pl.BlockSpec((rows, HEAD_DIM), lambda s, h: (0, 0)),
        pl.BlockSpec((rows, HEAD_DIM), lambda s, h: (0, 0)),
        pl.BlockSpec((1, HEAD_DIM), lambda s, h: (0, 0)),
    ]


def attention_forward(operands, sequences, heads, rows, length):
    pairs = sequences * heads * rows * length
    return pl.pallas_call(
        forward_kernel,
        grid=(sequences, heads),
        in_specs=attention_specs(rows, length),
        out_specs=[
            pl.BlockSpec((rows, HEAD_DIM), lambda s, h: (s, h)),
            pl.BlockSpec((1, 1, rows, 1), lambda s, h: (s, h, 0, 0)),
        ],
        out_shape=[
            jax.ShapeDtypeStruct((sequences * rows, heads * HEAD_DIM), BF16),
            jax.ShapeDtypeStruct((sequences, heads, rows, 1), F32),
        ],
        scratch_shapes=[pltpu.VMEM((rows, length), F32)],
        compiler_params=pltpu.CompilerParams(vmem_limit_bytes=VMEM_LIMIT),
        cost_estimate=pl.CostEstimate(
            flops=4 * pairs * HEAD_DIM, bytes_accessed=8 << 20, transcendentals=pairs
        ),
    )(*operands)


def attention_backward(operands, sequences, heads, rows, length):
    pairs = sequences * heads * rows * length
    parts = length // rows
    return pl.pallas_call(
        backward_kernel,
        grid=(sequences, heads),
        in_specs=attention_specs(rows, length)
        + [
            pl.BlockSpec((1, 1, rows, 1), lambda s, h: (s, h, 0, 0)),
            pl.BlockSpec((rows, HEAD_DIM), lambda s, h: (s, h)),
        ],
        out_specs=[
            pl.BlockSpec((rows, HEAD_DIM), lambda s, h: (s, h)),
            pl.BlockSpec((parts, 1, rows, 2 * HEAD_DIM), lambda s, h: (0, s, 0, 0)),
            pl.BlockSpec((1, HEAD_DIM), lambda s, h: (0, 0)),
        ],
        out_shape=[
            jax.ShapeDtypeStruct((sequences * rows, heads * HEAD_DIM), BF16),
            jax.ShapeDtypeStruct((parts, sequences, rows, 2 * HEAD_DIM), BF16),
            jax.ShapeDtypeStruct((1, HEAD_DIM), F32),
        ],
        scratch_shapes=[
            pltpu.VMEM((rows, length), F32),
            pltpu.VMEM((length, HEAD_DIM), F32),
            pltpu.VMEM((length, HEAD_DIM), F32),
        ],
        compiler_params=pltpu.CompilerParams(vmem_limit_bytes=VMEM_LIMIT),
        cost_estimate=pl.CostEstimate(
            flops=10 * pairs * HEAD_DIM, bytes_accessed=12 << 20, transcendentals=pairs
        ),
    )(*operands)


def body(
    tokens,
    segments,
    routes,
    priority,
    w_query,
    key_matrix,
    value_matrix,
    w_out,
    w_router,
    attn_gain,
    moe_gain,
    query_gain,
    key_norm_weight,
    w_gate_up,
    w_down,
    cotangent,
):
    own_rows, width = tokens.shape[1], tokens.shape[2]
    length = segments.shape[1]
    dp_size, seq_size, rep_size = (lax.axis_size(name) for name in ALL)
    devices = dp_size * seq_size * rep_size
    members = dp_size * rep_size
    seq_at, rep_at = lax.axis_index("seq"), lax.axis_index("rep")
    experts = devices * w_gate_up.shape[0]
    capacity = own_rows * TOPK // experts
    slots = experts * capacity
    depth = w_router.shape[0]
    heads = QUERY_HEADS // members
    head_width = heads * HEAD_DIM
    rows = rep_size * own_rows
    plane_rows = members * own_rows

    choice_ids = routes[0]
    expert_ids = jnp.arange(experts, dtype=jnp.int32)
    picked = jnp.any(choice_ids[:, :, None] == expert_ids[None, None, :], axis=1)
    earlier = (priority[0][None, :] < priority[0][:, None]).astype(BF16)
    slot_index = dot(earlier, picked.astype(BF16)).astype(jnp.int32)
    slot_ids = jnp.arange(capacity, dtype=jnp.int32)
    table = picked[:, :, None] & (slot_index[:, :, None] == slot_ids[None, None, :])
    placing = table.astype(BF16).reshape(own_rows, slots)

    packed = jnp.concatenate(
        [w_router.reshape(-1), attn_gain, moe_gain, query_gain, key_norm_weight]
    )
    unpacked = gather(packed, ALL, devices)
    bounds = [0]
    for part in (w_router.size, depth, depth, query_gain.size, key_norm_weight.size):
        bounds.append(bounds[-1] + part)
    small = [unpacked[:, a:b] for a, b in zip(bounds[:-1], bounds[1:])]
    router = small[0].reshape(width, experts)
    first_gain, second_gain, query_norm_gain, key_norm_gain = (
        piece.reshape(-1).astype(F32) for piece in small[1:]
    )

    plane_tokens = gather(tokens[0], PLANE, members).reshape(plane_rows, width).astype(F32)
    query_part = w_query.reshape(depth, dp_size, heads, rep_size, HEAD_DIM).transpose(1, 3, 0, 2, 4)
    query_part = query_part.reshape(members, depth, head_width)

    def spread(matrix):
        split = matrix.reshape(depth, dp_size, HEAD_DIM).transpose(1, 0, 2)[:, None]
        return jnp.broadcast_to(split, (dp_size, rep_size, depth, HEAD_DIM)).reshape(
            members, depth, HEAD_DIM
        )

    leaving = jnp.concatenate([query_part, spread(key_matrix), spread(value_matrix)], axis=-1)
    columns = leaving.shape[-1]
    weights = gather(swap(leaving, PLANE), "seq", seq_size)
    weights = (
        weights.reshape(seq_size, dp_size, rep_size * depth, columns)
        .transpose(1, 0, 2, 3)
        .reshape(width, columns)
    )
    whole_heads = w_out.shape[0] == HEAD_DIM
    if whole_heads:
        out_weights = gather(w_out, "seq", seq_size).reshape(head_width, width)
    else:
        group = lax.all_gather(w_out, ("seq", "rep"), axis=0, tiled=True)
        group = group.reshape(heads, rep_size, HEAD_DIM, width)
        out_weights = lax.dynamic_index_in_dim(group, rep_at, 1, keepdims=False).reshape(
            head_width, width
        )

    dy_and_picks = jnp.concatenate([cotangent[0], picked.astype(BF16)], axis=-1)
    dy_sent = dot_tn(placing, dy_and_picks).astype(BF16).reshape(experts, capacity, width + experts)
    dy_arrived = swap(dy_sent, ALL).reshape(slots, width + experts)
    dy_rows, pick_rows = dy_arrived[:, :width], dy_arrived[:, width:].astype(F32)

    scale_first = lax.rsqrt(jnp.mean(plane_tokens * plane_tokens, axis=-1, keepdims=True) + EPS)
    unit_first = plane_tokens * scale_first
    normed = (unit_first * first_gain).astype(BF16)
    projected = dot(normed, weights)
    query_proj = projected[:, :head_width]
    key_proj = projected[:, head_width : head_width + HEAD_DIM]
    value_rows = projected[:, head_width + HEAD_DIM :].astype(BF16)
    positions = seq_at * rows + jnp.arange(rows, dtype=jnp.int32)
    cosine, sine = rotary_tables(positions)

    def make_keys(key_in, gain_in):
        gained = norm_rows(key_in, gain_in).reshape(dp_size, rows, HEAD_DIM)
        rolled = jnp.roll(gained, HEAD_DIM // 2, axis=-1)
        return (gained * cosine[None] + rolled * sine[None]).reshape(plane_rows, HEAD_DIM)

    key_rows, key_pull = jax.vjp(make_keys, key_proj, key_norm_gain)
    key_value = jnp.concatenate([key_rows.astype(BF16), value_rows], axis=-1)
    key_value = gather(key_value.reshape(dp_size, rows, 2 * HEAD_DIM), "seq", seq_size)
    key_value = key_value.transpose(1, 0, 2, 3).reshape(dp_size, length, 2 * HEAD_DIM)

    documents = gather(segments[0], "dp", dp_size)
    query_doc = lax.dynamic_slice_in_dim(documents, seq_at * rows, rows, axis=1)
    operands = (
        query_proj,
        key_value,
        key_value,
        query_doc[:, :, None],
        documents[:, None, :],
        positions[:, None],
        cosine,
        sine,
        query_norm_gain[None],
    )
    attended, totals = attention_forward(operands, dp_size, heads, rows, length)
    out_parts = dot(attended, out_weights).astype(BF16).reshape(members, own_rows, width)
    middle = tokens[0].astype(F32) + jnp.sum(swap(out_parts, PLANE).astype(F32), axis=0)

    scale_second = lax.rsqrt(jnp.mean(middle * middle, axis=-1, keepdims=True) + EPS)
    unit_second = middle * scale_second
    routed = (unit_second * second_gain).astype(BF16)
    sent = dot_tn(placing, routed).astype(BF16).reshape(experts, capacity, width)
    routed_rows = swap(sent, ALL).reshape(slots, width)

    def gates_of(token_rows, choices):
        logits = jnp.where(choices, dot(token_rows, router), BIG_NEG)
        exponent = jnp.where(
            choices, jnp.exp(logits - jnp.max(logits, axis=-1, keepdims=True)), 0.0
        )
        return exponent / jnp.maximum(jnp.sum(exponent, axis=-1, keepdims=True), 1e-30)

    gates = gates_of(routed, picked)
    own_expert = lax.axis_index(ALL)
    gate_rows = lax.dynamic_slice_in_dim(
        gates_of(routed_rows, pick_rows > 0.5), own_expert, 1, axis=1
    )
    gate_up_weights, down_weights = w_gate_up[0], w_down[0]
    grad_hidden = dot_nt(dy_rows, down_weights)
    gate_up = dot(routed_rows, gate_up_weights)
    gate_in, up_in = gate_up[:, :FFE], gate_up[:, FFE:]
    sigmoid = jax.nn.sigmoid(gate_in)
    silu = gate_in * sigmoid
    hidden_f = silu * up_in
    hidden = hidden_f.astype(BF16)
    grad_gates_sent = jnp.sum(hidden_f * grad_hidden, axis=-1)
    scaled = grad_hidden * gate_rows
    grad_act = jnp.concatenate(
        [scaled * up_in * (sigmoid * (1.0 + gate_in * (1.0 - sigmoid))), scaled * silu], axis=-1
    ).astype(BF16)
    grad_pairs = dot_nt(grad_act, gate_up_weights).astype(BF16)
    grad_gates_back = swap(grad_gates_sent.reshape(devices, capacity), ALL)
    grad_back = swap(grad_pairs.reshape(devices, capacity, width), ALL).reshape(slots, width)
    results = (dot(hidden, down_weights) * gate_rows).astype(BF16)
    returned = swap(results.reshape(devices, capacity, width), ALL).reshape(slots, width)
    grad_gate_up = dot_tn(routed_rows, grad_act)
    grad_down = dot_tn((hidden_f * gate_rows).astype(BF16), dy_rows)

    mixed = (middle + dot(placing, returned)).astype(BF16)
    grad_gates = jnp.sum(jnp.where(table, grad_gates_back[None], 0.0), axis=-1)
    grad_logits = (
        gates * (grad_gates - jnp.sum(gates * grad_gates, axis=-1, keepdims=True))
    ).astype(BF16)
    grad_router = dot_tn(routed, grad_logits)
    grad_routed = dot(placing, grad_back) + dot_nt(grad_logits, router)
    grad_moe_gain = jnp.sum(grad_routed * unit_second, axis=0)
    weighted = grad_routed * second_gain
    grad_middle = cotangent[0].astype(F32) + scale_second * (
        weighted - unit_second * jnp.mean(weighted * unit_second, axis=-1, keepdims=True)
    )

    grad_branch = gather(grad_middle.astype(BF16), PLANE, members).reshape(plane_rows, width)
    grad_attended = dot_nt(grad_branch, out_weights).astype(BF16)
    grad_out = dot_tn(attended, grad_branch)
    if whole_heads:
        grad_out = grad_out.astype(BF16).reshape(seq_size, HEAD_DIM, width)
        grad_out = jnp.sum(swap(grad_out, "seq").astype(F32), axis=0)
    else:
        group = jnp.zeros((heads, rep_size, HEAD_DIM, width), BF16)
        group = lax.dynamic_update_index_in_dim(
            group, grad_out.astype(BF16).reshape(heads, HEAD_DIM, width), rep_at, 1
        )
        grad_out = lax.psum_scatter(
            group.reshape(heads * rep_size * HEAD_DIM, width).astype(F32),
            ("seq", "rep"),
            scatter_dimension=0,
            tiled=True,
        )
    grad_query_proj, grad_key_value, grad_query_gain = attention_backward(
        operands + (totals, grad_attended), dp_size, heads, rows, length
    )
    grad_key_value = jnp.sum(swap(grad_key_value, "seq").astype(F32), axis=0)
    grad_key_value = grad_key_value.reshape(plane_rows, 2 * HEAD_DIM)
    grad_key_proj, grad_key_gain = key_pull(grad_key_value[:, :HEAD_DIM])
    grad_projected = jnp.concatenate(
        [
            grad_query_proj,
            grad_key_proj.astype(BF16),
            grad_key_value[:, HEAD_DIM:].astype(BF16),
        ],
        axis=-1,
    )
    grad_normed = dot_nt(grad_projected, weights)
    grad_weights = dot_tn(normed, grad_projected).astype(BF16)
    grad_weights = grad_weights.reshape(dp_size, seq_size, rep_size * depth, columns)
    grad_weights = swap(grad_weights.transpose(1, 0, 2, 3), "seq")
    grad_weights = jnp.sum(grad_weights.astype(F32), axis=0).astype(BF16)
    grad_weights = swap(grad_weights.reshape(members, depth, columns), PLANE)
    grad_query = (
        grad_weights[:, :, :head_width]
        .reshape(dp_size, rep_size, depth, heads, HEAD_DIM)
        .transpose(2, 0, 3, 1, 4)
        .reshape(depth, QUERY_HEADS * HEAD_DIM)
        .astype(F32)
    )

    def joined(piece):
        summed = jnp.sum(
            piece.reshape(dp_size, rep_size, depth, HEAD_DIM).astype(F32), axis=1
        )
        return summed.transpose(1, 0, 2).reshape(depth, KEY_VALUE_HEADS * HEAD_DIM)

    grad_key = joined(grad_weights[:, :, head_width : head_width + HEAD_DIM])
    grad_value = joined(grad_weights[:, :, head_width + HEAD_DIM :])
    grad_attn_gain = jnp.sum(grad_normed * unit_first, axis=0)
    normed_parts = grad_normed.astype(BF16).reshape(members, own_rows, width)
    own_grad_normed = jnp.sum(swap(normed_parts, PLANE).astype(F32), axis=0)
    own_tokens = tokens[0].astype(F32)
    own_scale = lax.rsqrt(jnp.mean(own_tokens * own_tokens, axis=-1, keepdims=True) + EPS)
    own_unit = own_tokens * own_scale
    weighted = own_grad_normed * first_gain
    input_grad = grad_middle + own_scale * (
        weighted - own_unit * jnp.mean(weighted * own_unit, axis=-1, keepdims=True)
    )

    packed = jnp.concatenate(
        [
            piece.reshape(devices, -1)
            for piece in (grad_router, grad_attn_gain, grad_moe_gain, grad_query_gain, grad_key_gain)
        ],
        axis=-1,
    )
    owned = jnp.sum(swap(packed, ALL), axis=0)
    small = [owned[a:b] for a, b in zip(bounds[:-1], bounds[1:])]
    return (
        mixed[None],
        input_grad[None],
        grad_query,
        grad_key,
        grad_value,
        grad_out,
        small[0].reshape(depth, experts),
        small[1],
        small[2],
        small[3],
        small[4],
        grad_gate_up[None],
        grad_down[None],
    )


def solution(mesh):
    tokens_spec = P("dp", ("seq", "rep"), None)
    rows_spec = P(ALL, None)
    vector_spec = P(ALL)
    expert_spec = P(ALL, None, None)
    return jax.shard_map(
        body,
        mesh=mesh,
        in_specs=(
            tokens_spec,
            P("dp", None),
            tokens_spec,
            P("dp", ("seq", "rep")),
            rows_spec,
            rows_spec,
            rows_spec,
            rows_spec,
            rows_spec,
            vector_spec,
            vector_spec,
            vector_spec,
            vector_spec,
            expert_spec,
            expert_spec,
            tokens_spec,
        ),
        out_specs=(
            tokens_spec,
            tokens_spec,
            rows_spec,
            rows_spec,
            rows_spec,
            rows_spec,
            rows_spec,
            vector_spec,
            vector_spec,
            vector_spec,
            vector_spec,
            expert_spec,
            expert_spec,
        ),
        check_vma=False,
    )
```

time: 2940 us -> 1160 us (0.39)
  waiting for transfers between devices: 2400 us -> 635 us
  starting transfers between devices: 16.1 us -> 72.9 us
  matrix products: 170 us -> 120 us
  Pallas kernels: 0 us -> 48.2 us
  local copies, waits for them, and re-layouts: 132 us -> 83.9 us
    reduce_scatter x6 -> x0, waiting for transfers between devices: 1780 us -> none  [the longest x1 709 us: body(): lax.psum_scatter(grad_query, ('dp', 'seq', 'rep'), scatter_dimension=0, t...]
    all_to_all x4 -> x16, waiting for transfers between devices: 325 us -> 635 us  [swap(): return lax.all_to_all(blocks, axes, split_axis=0, concat_axis=0, tiled=True)]
    all_gather x6 -> x0, waiting for transfers between devices: 234 us -> none  [the longest x1 112 us: body(): lax.all_gather(w_query, ('dp', 'seq', 'rep'), axis=0, tiled=True)]
    all_to_all x0 -> x4, blocking collectives: none -> 133 us  [swap(): return lax.all_to_all(blocks, axes, split_axis=0, concat_axis=0, tiled=True)]
    unnamed x2 -> x0, blocking collectives: 81 us -> none
    all_gather x1 -> x0, blocking collectives: 68.3 us -> none  [body(): lax.all_gather(w_router, ('dp', 'seq', 'rep'), axis=0, tiled=True)]
    unnamed x14 -> x0, waiting for transfers between devices: 63.2 us -> none
    all_to_all x4 -> x16, starting transfers between devices: 15.2 us -> 72.9 us  [swap(): return lax.all_to_all(blocks, axes, split_axis=0, concat_axis=0, tiled=True)]
  transfers between devices with their start and end apart: 17 -> 16, of which waited for: 16 -> 13; matrix products, arithmetic and copies ran while one was open for 8% -> 15% of each run, Pallas kernels for 0% -> 4%
where the time goes in v1:
time: 1160 us; the launch traced here: 1140 us
  waiting for transfers between devices  635 us (55%)
  blocking collectives  133 us (11%)
  matrix products  120 us (10%)
  local copies, waits for them, and re-layouts  83.9 us (7%)
  starting transfers between devices  72.9 us (6%)
  other arithmetic  49.6 us (4%)
  Pallas kernels  48.2 us (4%)
    all_to_all x16, waiting for transfers between devices, swap(): return lax.all_to_all(blocks, axes, split_axis=0, concat_axis=0, tiled=True)  635 us
    all_to_all x4, blocking collectives, swap(): return lax.all_to_all(blocks, axes, split_axis=0, concat_axis=0, tiled=True)  133 us
    all_to_all x16, starting transfers between devices, swap(): return lax.all_to_all(blocks, axes, split_axis=0, concat_axis=0, tiled=True)  72.9 us
    dot_general x7, matrix products, dot_tn(): lax.dot_general(a, b, (((0,), (0,)), ((), ())), preferred_element_type=F32)  41.7 us
    dot_general x9, matrix products, dot(): return jnp.dot(a, b, preferred_element_type=F32)  39.5 us
    dot_general x5, matrix products, dot_nt(): lax.dot_general(a, b, (((1,), (1,)), ((), ())), preferred_element_type=F32)  38.7 us
    pallas_call x1, Pallas kernels, attention_backward(): pl.pallas_call(backward_kernel, grid=(sequences, heads), in_specs=attenti...  28.9 us
  transfers between devices with their start and end apart: 16, of which 13 were waited for; matrix products, arithmetic and copies ran while one was open for 15% of the time, Pallas kernels for 4%

profile of v1, /device:TPU:0, one launch (start us, length us, event | category | flops | bytes accessed | tf_op | source)
XLA Modules:
  0.0 1144.5 jit_solution(17973620354773699489)
XLA Ops:
  27.9 15.6 %all_to_all.113 = bf16[8,64,768]{2,1,0:T(8,128)(2,1)S(1)} all-to-all(bf16[8,64,768]{2,1,0:T(8,128)(2,1)} %pad_maximum_fusion.4), channel_id=1, replica_groups=mesh['dp'=4,'seq'=4,'rep'=2] {'dp','rep'}, dimensions={0} | all-to-all | bytes 1572864 | tf_op jit(solution)/shard_map/all_to_all | solution.py:32
  45.1 51.4 %all_to_all.114 = bf16[8,128,2048]{2,1,0:T(8,128)(2,1)} all-to-all(bf16[8,128,2048]{2,1,0:T(8,128)(2,1)S(1)} %broadcast_in_dim.56), channel_id=1, replica_groups=mesh['dp'=4,'seq'=4,'rep'=2] {'dp','rep'}, dimensions={0} | all-to-all | bytes 8388608 | tf_op jit(solution)/shard_map/all_to_all | solution.py:32
  116.8 58.0 %all-to-all-done.3 = bf16[4,8,64,768]{3,2,1,0:T(8,128)(2,1)} async-done(((bf16[4,8,64,768]{3,2,1,0:T(8,128)(2,1)}), bf16[4,8,64,768]{3,2,1,0:T(8,128)(2,1)}, u32[]{:S(2)}, u32[]{:S(2)}) %all-to-all-start.3) | async-done | bytes 3145760 | tf_op jit(solution)/shard_map/all_to_all | solution.py:32
  189.8 52.3 %all_to_all.115 = bf16[4,4,256,256]{3,2,1,0:T(8,128)(2,1)} all-to-all(bf16[4,4,256,256]{3,2,1,0:T(8,128)(2,1)S(1)} %broadcast_in_dim.66), channel_id=1, replica_groups=mesh['dp'=4,'seq'=4,'rep'=2] {'seq'}, dimensions={0} | all-to-all | bytes 4194304 | tf_op jit(solution)/shard_map/all_to_all | solution.py:32
  255.4 19.4 %shard_map.258 = (bf16[1024,512]{1,0:T(8,128)(2,1)S(1)}, f32[4,4,256,1]{3,2,1,0:T(8,128)}) custom-call(f32[1024,512]{1,0:T(8,128)} %slice.101.q_ref, bf16[4,1024,256]{2,1,0:T(8,128)(2,1)} %bitcast.197, bf16[4,1024,256]{2,1,0:T(8,128)(2,1)} %bitcast.198, s32[4,256,1]{2,1,0:T(8,128)S(1)} %copy-done.2, s32[4,1,1024]{2,1,0:T(1,128)S(1)} %all-to-all-done.5.kdoc_ref, ...), custom_call_target="tpu_custom_call" | custom-call | flops 2147483648 | bytes 8388608 | tf_op jit(solution)/shard_map/pallas_call | solution.py:167
  275.8 20.7 %all-to-all-done.6 = bf16[4,128,2048]{2,1,0:T(8,128)(2,1)} async-done(((bf16[4,128,2048]{2,1,0:T(8,128)(2,1)}), bf16[4,128,2048]{2,1,0:T(8,128)(2,1)}, u32[]{:S(2)}, u32[]{:S(2)}) %all-to-all-start.6) | async-done | bytes 2097184 | tf_op jit(solution)/shard_map/all_to_all | solution.py:32
  325.7 29.8 %all-to-all-done.7 = bf16[8,128,2048]{2,1,0:T(8,128)(2,1)} async-done(((bf16[8,128,2048]{2,1,0:T(8,128)(2,1)}), bf16[8,128,2048]{2,1,0:T(8,128)(2,1)}, u32[]{:S(2)}, u32[]{:S(2)}) %all-to-all-start.7) | async-done | bytes 4194336 | tf_op jit(solution)/shard_map/all_to_all | solution.py:32
  371.3 89.5 %all-to-all-done.9 = bf16[32,32,2080]{2,1,0:T(8,128)(2,1)} async-done(((bf16[32,32,2080]{2,1,0:T(8,128)(2,1)}), bf16[32,32,2080]{2,1,0:T(8,128)(2,1)}, u32[]{:S(2)}, u32[]{:S(2)}) %all-to-all-start.9) | async-done | bytes 4259872 | tf_op jit(solution)/shard_map/all_to_all | solution.py:32
  471.8 88.8 %all-to-all-done.8 = bf16[32,32,2048]{2,1,0:T(8,128)(2,1)} async-done(((bf16[32,32,2048]{2,1,0:T(8,128)(2,1)}), bf16[32,32,2048]{2,1,0:T(8,128)(2,1)}, u32[]{:S(2)}, u32[]{:S(2)}) %all-to-all-start.8) | async-done | bytes 4194336 | tf_op jit(solution)/shard_map/all_to_all | solution.py:32
  564.5 10.0 fusion.2
  574.6 10.0 multiply_convert_fusion.5
  589.2 11.1 fusion.4
  611.6 90.6 %all-to-all-done.11 = bf16[32,32,2048]{2,1,0:T(8,128)(2,1)} async-done(((bf16[32,32,2048]{2,1,0:T(8,128)(2,1)}), bf16[32,32,2048]{2,1,0:T(8,128)(2,1)}, u32[]{:S(2)}, u32[]{:S(2)}) %all-to-all-start.11) | async-done | bytes 4194336 | tf_op jit(solution)/shard_map/all_to_all | solution.py:32
  721.8 41.4 %all-to-all-done.13 = bf16[8,128,2048]{2,1,0:T(8,128)(2,1)} async-done(((bf16[8,128,2048]{2,1,0:T(8,128)(2,1)}), bf16[8,128,2048]{2,1,0:T(8,128)(2,1)}, u32[]{:S(2)}, u32[]{:S(2)}) %all-to-all-start.13) | async-done | bytes 4194336 | tf_op jit(solution)/shard_map/all_to_all | solution.py:32
  773.1 28.9 %shard_map.259 = (bf16[1024,512]{1,0:T(8,128)(2,1)S(1)}, bf16[4,4,256,256]{3,2,1,0:T(8,128)(2,1)}, f32[1,128]{1,0:T(1,128)S(1)}) custom-call(f32[1024,512]{1,0:T(8,128)} %slice.101.q_ref, bf16[4,1024,256]{2,1,0:T(8,128)(2,1)} %bitcast.199, bf16[4,1024,256]{2,1,0:T(8,128)(2,1)} %bitcast.200, s32[4,256,1]{2,1,0:T(8,128)S(1)} %copy-done.3, ...), custom_call_target="tpu_custom_call" | custom-call | flops 5368709120 | bytes 12582912 | tf_op jit(solution)/shard_map/pallas_call | solution.py:190
  801.9 60.8 %all-to-all-done.10 = bf16[32,32,2048]{2,1,0:T(8,128)(2,1)} async-done(((bf16[32,32,2048]{2,1,0:T(8,128)(2,1)}), bf16[32,32,2048]{2,1,0:T(8,128)(2,1)}, u32[]{:S(2)}, u32[]{:S(2)}) %all-to-all-start.10) | async-done | bytes 4194336 | tf_op jit(solution)/shard_map/all_to_all | solution.py:32
  873.1 42.7 %all-to-all-done.14 = bf16[4,4,256,256]{3,2,1,0:T(8,128)(2,1)} async-done(((bf16[4,4,256,256]{3,2,1,0:T(8,128)(2,1)}), bf16[4,4,256,256]{3,2,1,0:T(8,128)(2,1)}, u32[]{:S(2)}, u32[]{:S(2)}) %all-to-all-start.14) | async-done | bytes 2097184 | tf_op jit(solution)/shard_map/all_to_all | solution.py:32
  932.3 10.2 multiply_reduce_fusion
  943.0 25.4 %all-to-all-done.18 = bf16[4,128,2048]{2,1,0:T(8,128)(2,1)} async-done(((bf16[4,128,2048]{2,1,0:T(8,128)(2,1)}), bf16[4,128,2048]{2,1,0:T(8,128)(2,1)}, u32[]{:S(2)}, u32[]{:S(2)}) %all-to-all-start.18) | async-done | bytes 2097184 | tf_op jit(solution)/shard_map/all_to_all | solution.py:32
  968.4 13.5 %all_to_all.116 = f32[32,1,2184]{2,1,0:T(1,128)S(1)} all-to-all(f32[32,1,2184]{2,1,0:T(1,128)S(1)} %copy.152), channel_id=1, replica_groups=mesh['dp'=4,'seq'=4,'rep'=2] {'dp','seq','rep'}, dimensions={0} | all-to-all | bytes 559104 | tf_op jit(solution)/shard_map/all_to_all | solution.py:32
  994.3 40.5 %all-to-all-done.15 = bf16[8,128,2048]{2,1,0:T(8,128)(2,1)} async-done(((bf16[8,128,2048]{2,1,0:T(8,128)(2,1)}), bf16[8,128,2048]{2,1,0:T(8,128)(2,1)}, u32[]{:S(2)}, u32[]{:S(2)}) %all-to-all-start.15) | async-done | bytes 4194336 | tf_op jit(solution)/shard_map/all_to_all | solution.py:32
  1039.9 9.5 convolution_bitcast_fusion.1
  1049.5 11.6 %convolution_bitcast_fusion = f32[1,2048,1536]{2,1,0:T(8,128)} fusion(bf16[1024,2048]{1,0:T(8,128)(2,1)} %bitcast.27, bf16[1024,768]{1,0:T(8,128)(2,1)S(1)} %copy-done.56, bf16[1024,768]{1,0:T(8,128)(2,1)S(1)} %copy-done.55), kind=kOutput, calls=%fused_computation | convolution fusion | flops 6448742400 | bytes 19922944 | tf_op jit(solution)/shard_map/dot_general | solution.py:48
  1073.3 37.7 %all-to-all-done.16 = bf16[4,4,128,768]{3,2,1,0:T(8,128)(2,1)} async-done(((bf16[4,4,128,768]{3,2,1,0:T(8,128)(2,1)}), bf16[4,4,128,768]{3,2,1,0:T(8,128)(2,1)}, u32[]{:S(2)}, u32[]{:S(2)}) %all-to-all-start.16) | async-done | bytes 3145760 | tf_op jit(solution)/shard_map/all_to_all | solution.py:32
  (266 shorter events, 272.8 us)
Async XLA Ops:
  0.6 573.9 %copy-start = (bf16[1,768,2048]{2,1,0:T(8,128)(2,1)S(1)}, bf16[1,768,2048]{2,1,0:T(8,128)(2,1)}, u32[]{:S(2)}) copy-start(bf16[1,768,2048]{2,1,0:T(8,128)(2,1)} %param.30) | copy-start | bytes 9437188
  9.1 18.8 %all-to-all-start.1 = ((bf16[32,2,1092]{2,1,0:T(2,128)(2,1)}), bf16[32,2,1092]{2,1,0:T(2,128)(2,1)S(1)}, u32[]{:S(2)}, u32[]{:S(2)}) async-start(bf16[32,2,1092]{2,1,0:T(2,128)(2,1)} %reshape.450), calls=%async_computation.1 | async-start | bytes 294912 | tf_op jit(solution)/shard_map/all_to_all | solution.py:32
  98.5 76.2 %all-to-all-start.3 = ((bf16[4,8,64,768]{3,2,1,0:T(8,128)(2,1)}), bf16[4,8,64,768]{3,2,1,0:T(8,128)(2,1)}, u32[]{:S(2)}, u32[]{:S(2)}) async-start(bf16[4,8,64,768]{3,2,1,0:T(8,128)(2,1)} %broadcast_in_dim.64), calls=%async_computation.3 | async-start | bytes 6291456 | tf_op jit(solution)/shard_map/all_to_all | solution.py:32
  176.0 12.4 %all-to-all-start.5 = ((s32[4,1,1024]{2,1,0:T(1,128)}), s32[4,1,1024]{2,1,0:T(1,128)S(1)}, u32[]{:S(2)}, u32[]{:S(2)}) async-start(s32[4,1,1024]{2,1,0:T(1,128)} %broadcast_in_dim.67), calls=%async_computation.5 | async-start | bytes 32768 | tf_op jit(solution)/shard_map/all_to_all | solution.py:32
  188.5 53.6 %copy-start.26 = (bf16[128,2048]{1,0:T(8,128)(2,1)S(1)}, bf16[128,2048]{1,0:T(8,128)(2,1)}, u32[]{:S(2)}) copy-start(bf16[128,2048]{1,0:T(8,128)(2,1)} %param.23) | copy-start | bytes 1572868
  243.7 52.7 %all-to-all-start.6 = ((bf16[4,128,2048]{2,1,0:T(8,128)(2,1)}), bf16[4,128,2048]{2,1,0:T(8,128)(2,1)}, u32[]{:S(2)}, u32[]{:S(2)}) async-start(bf16[4,128,2048]{2,1,0:T(8,128)(2,1)} %broadcast_in_dim.69), calls=%async_computation.6 | async-start | bytes 4194304 | tf_op jit(solution)/shard_map/all_to_all | solution.py:32
  302.6 52.9 %all-to-all-start.7 = ((bf16[8,128,2048]{2,1,0:T(8,128)(2,1)}), bf16[8,128,2048]{2,1,0:T(8,128)(2,1)}, u32[]{:S(2)}, u32[]{:S(2)}) async-start(bf16[8,128,2048]{2,1,0:T(8,128)(2,1)} %bitcast.187), calls=%async_computation.7 | async-start | bytes 8388608 | tf_op jit(solution)/shard_map/all_to_all | solution.py:32
  355.5 105.3 %all-to-all-start.9 = ((bf16[32,32,2080]{2,1,0:T(8,128)(2,1)}), bf16[32,32,2080]{2,1,0:T(8,128)(2,1)}, u32[]{:S(2)}, u32[]{:S(2)}) async-start(bf16[32,32,2080]{2,1,0:T(8,128)(2,1)} %bitcast.176), calls=%async_computation.9 | async-start | bytes 8912896 | tf_op jit(solution)/shard_map/all_to_all | solution.py:32
  460.8 99.9 %all-to-all-start.8 = ((bf16[32,32,2048]{2,1,0:T(8,128)(2,1)}), bf16[32,32,2048]{2,1,0:T(8,128)(2,1)}, u32[]{:S(2)}, u32[]{:S(2)}) async-start(bf16[32,32,2048]{2,1,0:T(8,128)(2,1)} %bitcast.175), calls=%async_computation.8 | async-start | bytes 8388608 | tf_op jit(solution)/shard_map/all_to_all | solution.py:32
  586.0 14.3 %all-to-all-start.12 = ((f32[32,1,32]{2,1,0:T(1,128)}), f32[32,1,32]{2,1,0:T(1,128)}, u32[]{:S(2)}, u32[]{:S(2)}) async-start(f32[32,1,32]{2,1,0:T(1,128)} %all_to_all.83), calls=%async_computation.12 | async-start | bytes 32768 | tf_op jit(solution)/shard_map/all_to_all | solution.py:32
  600.3 101.9 %all-to-all-start.11 = ((bf16[32,32,2048]{2,1,0:T(8,128)(2,1)}), bf16[32,32,2048]{2,1,0:T(8,128)(2,1)}, u32[]{:S(2)}, u32[]{:S(2)}) async-start(bf16[32,32,2048]{2,1,0:T(8,128)(2,1)} %bitcast.185), calls=%async_computation.11 | async-start | bytes 8388608 | tf_op jit(solution)/shard_map/all_to_all | solution.py:32
  710.4 52.8 %all-to-all-start.13 = ((bf16[8,128,2048]{2,1,0:T(8,128)(2,1)}), bf16[8,128,2048]{2,1,0:T(8,128)(2,1)}, u32[]{:S(2)}, u32[]{:S(2)}) async-start(bf16[8,128,2048]{2,1,0:T(8,128)(2,1)} %broadcast_in_dim.78), calls=%async_computation.13 | async-start | bytes 8388608 | tf_op jit(solution)/shard_map/all_to_all | solution.py:32
  763.2 99.6 %all-to-all-start.10 = ((bf16[32,32,2048]{2,1,0:T(8,128)(2,1)}), bf16[32,32,2048]{2,1,0:T(8,128)(2,1)}, u32[]{:S(2)}, u32[]{:S(2)}) async-start(bf16[32,32,2048]{2,1,0:T(8,128)(2,1)} %bitcast.186), calls=%async_computation.10 | async-start | bytes 8388608 | tf_op jit(solution)/shard_map/all_to_all | solution.py:32
  801.9 65.3 %copy-start.7 = (bf16[1024,512]{1,0:T(8,128)(2,1)S(1)}, bf16[1024,512]{1,0:T(8,128)(2,1)}, u32[]{:S(2)}) copy-start(bf16[1024,512]{1,0:T(8,128)(2,1)} %copy-done.6) | copy-start | bytes 3145732
  862.8 53.0 %all-to-all-start.14 = ((bf16[4,4,256,256]{3,2,1,0:T(8,128)(2,1)}), bf16[4,4,256,256]{3,2,1,0:T(8,128)(2,1)}, u32[]{:S(2)}, u32[]{:S(2)}) async-start(bf16[4,4,256,256]{3,2,1,0:T(8,128)(2,1)} %get-tuple-element.21), calls=%async_computation.14 | async-start | bytes 4194304 | tf_op jit(solution)/shard_map/all_to_all | solution.py:32
  873.1 47.5 %copy-start.9 = (f32[128,2048]{1,0:T(8,128)S(1)}, f32[128,2048]{1,0:T(8,128)}, u32[]{:S(2)}) copy-start(f32[128,2048]{1,0:T(8,128)} %get-tuple-element.112) | copy-start | bytes 3145732
  873.1 47.5 %copy-start.33 = (f32[2048]{0:T(1024)S(1)}, f32[2048]{0:T(1024)}, u32[]{:S(2)}) copy-start(f32[2048]{0:T(1024)} %reshape.432) | copy-start | bytes 24580
  873.1 47.5 %copy-start.42 = (bf16[128,32]{0,1:T(8,128)(2,1)S(1)}, bf16[128,32]{0,1:T(8,128)(2,1)}, u32[]{:S(2)}) copy-start(bf16[128,32]{0,1:T(8,128)(2,1)} %multiply_convert_fusion.9) | copy-start | bytes 24580
  873.1 47.5 %copy-start.50 = (f32[128]{0:T(128)S(1)}, f32[128]{0:T(128)}, u32[]{:S(2)}) copy-start(f32[128]{0:T(128)} %copy-done.48) | copy-start | bytes 1540
  915.8 52.6 %all-to-all-start.18 = ((bf16[4,128,2048]{2,1,0:T(8,128)(2,1)}), bf16[4,128,2048]{2,1,0:T(8,128)(2,1)}, u32[]{:S(2)}, u32[]{:S(2)}) async-start(bf16[4,128,2048]{2,1,0:T(8,128)(2,1)} %bitcast.201), calls=%async_computation.18 | async-start | bytes 4194304 | tf_op jit(solution)/shard_map/all_to_all | solution.py:32
  981.9 53.0 %all-to-all-start.15 = ((bf16[8,128,2048]{2,1,0:T(8,128)(2,1)}), bf16[8,128,2048]{2,1,0:T(8,128)(2,1)}, u32[]{:S(2)}, u32[]{:S(2)}) async-start(bf16[8,128,2048]{2,1,0:T(8,128)(2,1)} %bitcast.184), calls=%async_computation.15 | async-start | bytes 8388608 | tf_op jit(solution)/shard_map/all_to_all | solution.py:32
  1034.8 76.2 %all-to-all-start.16 = ((bf16[4,4,128,768]{3,2,1,0:T(8,128)(2,1)}), bf16[4,4,128,768]{3,2,1,0:T(8,128)(2,1)}, u32[]{:S(2)}, u32[]{:S(2)}) async-start(bf16[4,4,128,768]{3,2,1,0:T(8,128)(2,1)} %bitcast.178), calls=%async_computation.16 | async-start | bytes 6291456 | tf_op jit(solution)/shard_map/all_to_all | solution.py:32
  1073.3 45.7 %copy-start.53 = (f32[128]{0:T(128)S(1)}, f32[128]{0:T(128)}, u32[]{:S(2)}) copy-start(f32[128]{0:T(128)} %copy-done.52) | copy-start | bytes 1540
  1114.5 16.3 %all-to-all-start.17 = ((bf16[8,64,768]{2,1,0:T(8,128)(2,1)}), bf16[8,64,768]{2,1,0:T(8,128)(2,1)}, u32[]{:S(2)}, u32[]{:S(2)}) async-start(bf16[8,64,768]{2,1,0:T(8,128)(2,1)} %bitcast.195), calls=%async_computation.17 | async-start | bytes 1572864 | tf_op jit(solution)/shard_map/all_to_all | solution.py:32
  (49 other events, 249.0 us)

commit v2 on v1

v2 whole, which is shorter than its diff:
```python
import functools

import jax
import jax.numpy as jnp
from jax import lax
from jax.experimental import pallas as pl
from jax.experimental.pallas import tpu as pltpu
from jax.sharding import PartitionSpec as P

QUERY_HEADS = 32
KEY_VALUE_HEADS = 4
HEAD_DIM = 128
FFE = 768
TOPK = 8

EPS = 1e-06
THETA = 1000000.0
BIG_NEG = -1e30
LOG2E = 1.4426950408889634
ALL = ("dp", "seq", "rep")
PLANE = ("dp", "rep")
F32 = jnp.float32
BF16 = jnp.bfloat16
VMEM_LIMIT = 56 * 1024 * 1024
SCALE = HEAD_DIM ** (-0.5)
SIDE, CORE, CROSS = 1, 2, 4
FLIPS = (CROSS | SIDE, CROSS, SIDE, 0)
LANES = 128
PRIORITY_ROW, DOCUMENT_ROW, MOE_GAIN_ROW, QUERY_GAIN_ROW, KEY_GAIN_ROW, ATTN_GAIN_ROW, PACKET_ROWS = 8, 9, 10, 11, 12, 13, 16


def dot(a, b):
    return jnp.dot(a, b, preferred_element_type=F32)


def dot_nt(a, b):
    return lax.dot_general(a, b, (((1,), (1,)), ((), ())), preferred_element_type=F32)


def dot_tn(a, b):
    return lax.dot_general(a, b, (((0,), (0,)), ((), ())), preferred_element_type=F32)


def after(value, *earlier):
    return lax.optimization_barrier((value,) + earlier)[0]


def swap(blocks, axes):
    return lax.all_to_all(blocks, axes, split_axis=0, concat_axis=0, tiled=True)


def spread(shard, axes, count):
    return swap(jnp.broadcast_to(shard[None], (count,) + shard.shape), axes)


def shape_of(shape, dtype):
    return jax.ShapeDtypeStruct(shape, dtype)


def run(kernel, outs, *operands, scratch=(), flops=0, transcendentals=0):
    in_specs = [pl.BlockSpec(memory_space=pltpu.SMEM)]
    in_specs += [pl.BlockSpec(memory_space=pltpu.VMEM)] * (len(operands) - 1)
    touched = sum(o.size * o.dtype.itemsize for o in operands[1:])
    touched += sum(o.size * o.dtype.itemsize for o in outs)
    return pl.pallas_call(
        kernel,
        in_specs=in_specs,
        out_specs=[pl.BlockSpec(memory_space=pltpu.VMEM)] * len(outs),
        out_shape=outs,
        scratch_shapes=scratch,
        compiler_params=pltpu.CompilerParams(vmem_limit_bytes=VMEM_LIMIT),
        cost_estimate=pl.CostEstimate(
            flops=int(flops), bytes_accessed=int(touched), transcendentals=int(transcendentals)
        ),
    )(*operands)


def plane_move(block, bits):
    return lax.ppermute(block, PLANE, [(index, index ^ bits) for index in range(8)])


def plane_gather(block):
    half = block.shape[0] // 2
    across, aside, core = (plane_move(block, bits) for bits in (CROSS, SIDE, CORE))
    far = [plane_move(across[:half], SIDE), plane_move(aside[half:], CROSS)]
    across_core, aside_core = plane_move(across, CORE), plane_move(aside, CORE)
    far_core = [plane_move(piece, CORE) for piece in far]
    return [block, aside, core, aside_core, across] + far + [across_core] + far_core


def place_plane(refs, member, write):
    rows = refs[0].shape[0]
    offsets = [(0, 0), (1, 0), (2, 0), (3, 0), (4, 0), (5, 0), (5, rows // 2), (6, 0), (7, 0), (7, rows // 2)]
    for ref, (bits, start) in zip(refs, offsets):
        write(pl.multiple_of((member ^ bits) * rows + start, rows // 2), ref)


def first_sums(_, arrived, kept, far_low, far_high, across, aside, own):
    half = far_low.shape[0]
    sums = [arrived[i].astype(F32) + kept[i].astype(F32) for i in range(4)]
    far_low[...] = sums[0][:half].astype(BF16)
    far_high[...] = sums[0][half:].astype(BF16)
    across[...] = sums[1].astype(BF16)
    aside[...] = sums[2].astype(BF16)
    own[...] = sums[3]


def second_sums(_, across, aside, from_across, from_aside, across_out, aside_out):
    half = from_across.shape[0]
    across_out[:half] = across[:half]
    across_out[half:] = (across[half:].astype(F32) + from_aside[...].astype(F32)).astype(BF16)
    aside_out[:half] = (aside[:half].astype(F32) + from_across[...].astype(F32)).astype(BF16)
    aside_out[half:] = aside[half:]


def plane_reduce(info, sent, kept):
    _, rows, width = sent.shape
    piece, whole = shape_of((rows // 2, width), BF16), shape_of((rows, width), BF16)
    arrived = plane_move(sent, CORE)
    far_low, far_high, across, aside, own = run(
        first_sums, [piece, piece, whole, whole, shape_of((rows, width), F32)], info, arrived, kept
    )
    from_across, from_aside = plane_move(far_low, CROSS), plane_move(far_high, SIDE)
    across, aside = run(
        second_sums, [whole, whole], info, across, aside, from_across, from_aside
    )
    return own, plane_move(across, CROSS), plane_move(aside, SIDE)


UP, DOWN = ((0, 1), (1, 2), (2, 3)), ((3, 2), (2, 1), (1, 0))
ORDER = ((0, 1, 2, 3), (1, 2, 0, 3), (2, 1, 3, 0), (3, 2, 1, 0))
OFFSETS = (0, -1, 1, -2, 2, -3, 3)


def line_move(block, pairs):
    return lax.ppermute(block, "seq", list(pairs))


def line_gather(block, count):
    if count != 4:
        return [spread(block, "seq", count)]
    up1, down1 = line_move(block, UP), line_move(block, DOWN)
    up2, down2 = line_move(up1, UP[1:]), line_move(down1, DOWN[1:])
    up3, down3 = line_move(up2, UP[2:]), line_move(down2, DOWN[2:])
    return [block, up1, down1, up2, down2, up3, down3]


def place_line(refs, place, count, write):
    if len(refs) == 1:
        for index in range(count):
            write(index, refs[0].at[index])
        return
    for offset, ref in zip(OFFSETS, refs):
        index = place + offset

        @pl.when((index >= 0) & (index < count))
        def _(index=index, ref=ref):
            write(index, ref)


def needed_offsets(steps):
    return [o for o in OFFSETS if any(ORDER[z][step] - z == o for z in range(4) for step in steps)]


def needed(sources, steps):
    if len(sources) == 1:
        return sources
    return [dict(zip(OFFSETS, sources))[o] for o in needed_offsets(steps)]


def block_of_step(refs, info, steps, step):
    if len(refs) == 1:
        return refs[0][info[4 + step]]
    by_offset = dict(zip(needed_offsets(steps), refs))
    offsets = [ORDER[z][step] - z for z in range(4)]
    block = by_offset[offsets[3]][...]
    for z in range(3):
        if offsets[z] != offsets[3]:
            block = jnp.where(info[0] == z, by_offset[offsets[z]][...], block)
    return block


def line_steps(blocks, place):
    if len(blocks) == 1:
        return [blocks[0][step] for step in range(blocks[0].shape[0])]
    block, up1, down1, up2, down2, up3, down3 = blocks
    low = place < 2
    return [
        block,
        jnp.where(low, down1, up1),
        jnp.where(low, jnp.where(place == 0, down2, up1), jnp.where(place == 3, up2, down1)),
        jnp.where(low, jnp.where(place == 0, down3, down2), jnp.where(place == 3, up3, up2)),
    ]


def line_reduce(parts, place, count):
    if count != 4:
        total = jnp.sum(swap(jnp.stack(parts).astype(BF16), "seq").astype(F32), axis=0)
        return total, None, None
    own, first, second, third = parts
    edge = (place == 0) | (place == 3)
    inward = line_move(third.astype(BF16), [(0, 1), (3, 2)])
    middle = jnp.where(edge, second, third + inward).astype(BF16)
    up, down = line_move(middle, UP[:2]), line_move(middle, DOWN[:2])
    up = (jnp.where(place == 2, second, first) + up).astype(BF16)
    down = (jnp.where(place == 1, second, first) + down).astype(BF16)
    return own, line_move(up, UP), line_move(down, DOWN)


def total_of(terms):
    return sum(term.astype(F32) for term in terms if term is not None)


def pick(blocks, index, axis=0):
    return lax.dynamic_index_in_dim(blocks, index, axis, keepdims=False)


def pack_weights_kernel(*refs):
    *query_refs, key_ref, value_ref, query_out, key_value_out = refs
    for j, ref in enumerate(query_refs):
        query_out[0, :, j * HEAD_DIM : (j + 1) * HEAD_DIM] = ref[...]
    takes_keys = lax.rem(pl.program_id(0), 2) == 0
    key_value_out[0] = jnp.where(takes_keys, key_ref[...], value_ref[...])


def pack_weights(w_query, key_matrix, value_matrix, members, rep_size, heads):
    depth = w_query.shape[0]
    group = heads * rep_size

    def head_spec(j):
        return pl.BlockSpec(
            (depth, HEAD_DIM), lambda m: (0, (m // rep_size) * group + j * rep_size + m % rep_size)
        )

    group_spec = pl.BlockSpec((depth, HEAD_DIM), lambda m: (0, m // rep_size))
    return pl.pallas_call(
        pack_weights_kernel,
        grid=(members,),
        in_specs=[head_spec(j) for j in range(heads)]
        + [group_spec, group_spec],
        out_specs=[
            pl.BlockSpec((1, depth, heads * HEAD_DIM), lambda m: (m, 0, 0)),
            pl.BlockSpec((1, depth, HEAD_DIM), lambda m: (m, 0, 0)),
        ],
        out_shape=[
            shape_of((members, depth, heads * HEAD_DIM), BF16),
            shape_of((members, depth, HEAD_DIM), BF16),
        ],
        cost_estimate=pl.CostEstimate(flops=1 << 20, bytes_accessed=2 << 20, transcendentals=0),
    )(*([w_query] * heads), key_matrix, value_matrix)


def packet_kernel(info, routes, priority, documents, moe_gain, query_gain, key_gain, attn_gain, out):
    own = info[2]
    eye = lax.broadcasted_iota(jnp.int32, (LANES, LANES), 0) == lax.broadcasted_iota(
        jnp.int32, (LANES, LANES), 1
    )
    rows = [dot_tn(routes[...].astype(BF16), eye.astype(BF16)), priority[...].astype(F32)]
    rows.append(documents[...].astype(F32))
    for ref, at in ((moe_gain, 0), (query_gain, own), (key_gain, own), (attn_gain, 0)):
        size = ref.shape[1]
        lane = lax.broadcasted_iota(jnp.int32, (size, LANES), 1)
        value = lax.broadcasted_iota(jnp.int32, (size, LANES), 0)
        rows.append(dot(ref[...], (lane == at * size + value).astype(BF16)))
    packet = jnp.concatenate(rows + [jnp.zeros((PACKET_ROWS - 14, LANES), F32)], axis=0).astype(BF16)
    for index in range(out.shape[0]):
        out[index] = packet


def normalize_kernel(info, gain, *refs):
    out = refs[-1]

    def write(row, ref):
        values = ref[...].astype(F32)
        scale = lax.rsqrt(jnp.mean(values * values, axis=-1, keepdims=True) + EPS)
        out[pl.ds(row, ref.shape[0]), :] = (values * scale * gain[...]).astype(BF16)

    place_plane(refs[:-1], info[1], write)


def place_weights(refs, info, count, out, groups):
    rows = out.shape[0] // (groups * count)

    def write(index, ref):
        for group in range(groups):
            start = pl.multiple_of((group * count + index) * rows, rows)
            out[pl.ds(start, rows), :] = ref[pl.ds(group * rows, rows), :]

    place_line(refs, info[0], count, write)


def turn(values, cosine, sine):
    return values * cosine + pltpu.roll(values, HEAD_DIM // 2, 1) * sine


def key_value_kernel(count, groups, info, units, cosine, sine, gain, *refs):
    *sources, weights, key_proj, out = refs
    place_weights(sources, info, count, weights, groups)
    projected = dot(units[...], weights[...])
    key_proj[...] = projected
    scale = lax.rsqrt(jnp.mean(projected * projected, axis=-1, keepdims=True) + EPS)
    keys = projected * scale * gain[...]
    rows = out.shape[1]
    for group in range(groups):
        part = slice(group * rows, (group + 1) * rows)
        turned = turn(keys[part], cosine[...], sine[...])
        out[group] = jnp.where(info[3] == 0, turned, projected[part]).astype(BF16)


def query_kernel(count, groups, info, units, *refs):
    *sources, weights, out = refs
    place_weights(sources, info, count, weights, groups)
    out[...] = dot(units[...], weights[...])


def attention_setup(info, sources, qdoc_ref, kdoc_ref, qpos_ref, bias, keys, values):
    key_pos = lax.broadcasted_iota(jnp.int32, bias.shape, 1)
    allowed = (qdoc_ref[0] == kdoc_ref[0]) & (key_pos <= qpos_ref[...])
    bias[...] = jnp.where(allowed, 0.0, BIG_NEG)
    rows, count = bias.shape[0], len(sources) // 2
    for step in range(count):
        part = pl.ds(pl.multiple_of(info[4 + step] * rows, rows), rows)
        mine, other = sources[step][0], sources[count + step][0]
        keys[part, :] = jnp.where(info[3] == 0, mine, other)
        values[part, :] = jnp.where(info[3] == 0, other, mine)


def rotated(projected, gain, cosine, sine):
    scale = lax.rsqrt(jnp.mean(projected * projected, axis=-1, keepdims=True) + EPS)
    unit = projected * scale
    return scale, unit, turn(unit * gain, cosine, sine)


def forward_kernel(info, q_ref, qdoc_ref, kdoc_ref, qpos_ref, cos_ref, sin_ref, gain_ref, *refs):
    *sources, out_ref, total_ref, bias, keys, values = refs

    @pl.when(pl.program_id(1) == 0)
    def _():
        attention_setup(info, sources, qdoc_ref, kdoc_ref, qpos_ref, bias, keys, values)

    _, _, turned = rotated(q_ref[...], gain_ref[...], cos_ref[...], sin_ref[...])
    scores = dot_nt(turned.astype(BF16), keys[...]) * (SCALE * LOG2E) + bias[...]
    highest = jnp.max(scores, axis=-1, keepdims=True)
    exponent = jnp.exp2(scores - highest)
    total = jnp.sum(exponent, axis=-1, keepdims=True)
    probs = (exponent * (1.0 / total)).astype(BF16)
    out_ref[...] = dot(probs, values[...]).astype(BF16)
    total_ref[0, 0] = highest + jnp.log2(total)


def backward_kernel(info, q_ref, qdoc_ref, kdoc_ref, qpos_ref, cos_ref, sin_ref, gain_ref, *refs):
    *sources, total_ref, grad_ref, dq_ref, kept_ref, sent_ref, dgain_ref, bias, key_rows, value_rows, dk_sum, dv_sum = refs
    seq, head = pl.program_id(0), pl.program_id(1)

    @pl.when(head == 0)
    def _():
        attention_setup(info, sources, qdoc_ref, kdoc_ref, qpos_ref, bias, key_rows, value_rows)
        dk_sum[...] = jnp.zeros_like(dk_sum)
        dv_sum[...] = jnp.zeros_like(dv_sum)

    @pl.when((head == 0) & (seq == 0))
    def _():
        dgain_ref[...] = jnp.zeros_like(dgain_ref)

    gain, cosine, sine = gain_ref[...], cos_ref[...], sin_ref[...]
    scale, unit, turned = rotated(q_ref[...], gain, cosine, sine)
    turned = turned.astype(BF16)
    keys, values = key_rows[...], value_rows[...]
    scores = dot_nt(turned, keys) * (SCALE * LOG2E) + bias[...]
    probs = jnp.exp2(scores - total_ref[0, 0])
    grad = grad_ref[...]
    grad_probs = dot_nt(grad, values)
    delta = jnp.sum(probs * grad_probs, axis=-1, keepdims=True)
    grad_scores = (probs * (grad_probs - delta)).astype(BF16)
    dv_sum[...] += dot_tn(probs.astype(BF16), grad)
    dk_sum[...] += dot_tn(grad_scores, turned)
    grad_turned = dot(grad_scores, keys) * SCALE
    grad_gained = turn(grad_turned, cosine, -sine)
    dgain_ref[...] += jnp.sum(grad_gained * unit, axis=0, keepdims=True)
    weighted = grad_gained * gain
    dq_ref[...] = (
        scale * (weighted - unit * jnp.mean(weighted * unit, axis=-1, keepdims=True))
    ).astype(BF16)

    @pl.when(head == pl.num_programs(1) - 1)
    def _():
        shape = kept_ref.shape[:1] + kept_ref.shape[2:]
        dk, dv = dk_sum[...] * SCALE, dv_sum[...]
        kept_ref[:, 0] = jnp.where(info[3] == 0, dk, dv).astype(BF16).reshape(shape)
        sent_ref[:, 0] = jnp.where(info[3] == 0, dv, dk).astype(BF16).reshape(shape)


def attention_specs(rows, length, sources, first=0):
    specs = [
        pl.BlockSpec(memory_space=pltpu.SMEM),
        pl.BlockSpec((rows, HEAD_DIM), lambda s, h: (first + s, h)),
        pl.BlockSpec((1, rows, 1), lambda s, h: (first + s, 0, 0)),
        pl.BlockSpec((1, 1, length), lambda s, h: (first + s, 0, 0)),
        pl.BlockSpec((rows, 1), lambda s, h: (0, 0)),
        pl.BlockSpec((rows, HEAD_DIM), lambda s, h: (0, 0)),
        pl.BlockSpec((rows, HEAD_DIM), lambda s, h: (0, 0)),
        pl.BlockSpec((1, HEAD_DIM), lambda s, h: (0, 0)),
    ]
    return specs + [
        pl.BlockSpec((1, rows, HEAD_DIM), lambda s, h: (first + s, 0, 0)) for _ in sources
    ]


def attention_forward(operands, sources, sequences, heads, rows, length):
    pairs = sequences * heads * rows * length
    return pl.pallas_call(
        forward_kernel,
        grid=(sequences, heads),
        in_specs=attention_specs(rows, length, sources),
        out_specs=[
            pl.BlockSpec((rows, HEAD_DIM), lambda s, h: (s, h)),
            pl.BlockSpec((1, 1, rows, 1), lambda s, h: (s, h, 0, 0)),
        ],
        out_shape=[
            shape_of((sequences * rows, heads * HEAD_DIM), BF16),
            shape_of((sequences, heads, rows, 1), F32),
        ],
        scratch_shapes=[
            pltpu.VMEM((rows, length), F32),
            pltpu.VMEM((length, HEAD_DIM), BF16),
            pltpu.VMEM((length, HEAD_DIM), BF16),
        ],
        compiler_params=pltpu.CompilerParams(vmem_limit_bytes=VMEM_LIMIT),
        cost_estimate=pl.CostEstimate(
            flops=4 * pairs * HEAD_DIM, bytes_accessed=8 << 20, transcendentals=pairs
        ),
    )(*operands, *sources)


def attention_backward(operands, sources, totals, grads, first, sequences, heads, rows, length):
    pairs = sequences * heads * rows * length
    parts = length // rows
    key_value_spec = pl.BlockSpec((parts, 1, rows, HEAD_DIM), lambda s, h: (0, s, 0, 0))
    key_value_shape = shape_of((parts, sequences, rows, HEAD_DIM), BF16)
    return pl.pallas_call(
        backward_kernel,
        grid=(sequences, heads),
        in_specs=attention_specs(rows, length, sources, first)
        + [
            pl.BlockSpec((1, 1, rows, 1), lambda s, h: (first + s, h, 0, 0)),
            pl.BlockSpec((rows, HEAD_DIM), lambda s, h: (first + s, h)),
        ],
        out_specs=[
            pl.BlockSpec((rows, HEAD_DIM), lambda s, h: (s, h)),
            key_value_spec,
            key_value_spec,
            pl.BlockSpec((1, HEAD_DIM), lambda s, h: (0, 0)),
        ],
        out_shape=[
            shape_of((sequences * rows, heads * HEAD_DIM), BF16),
            key_value_shape,
            key_value_shape,
            shape_of((1, HEAD_DIM), F32),
        ],
        scratch_shapes=[
            pltpu.VMEM((rows, length), F32),
            pltpu.VMEM((length, HEAD_DIM), BF16),
            pltpu.VMEM((length, HEAD_DIM), BF16),
            pltpu.VMEM((length, HEAD_DIM), F32),
            pltpu.VMEM((length, HEAD_DIM), F32),
        ],
        compiler_params=pltpu.CompilerParams(vmem_limit_bytes=VMEM_LIMIT),
        cost_estimate=pl.CostEstimate(
            flops=10 * pairs * HEAD_DIM, bytes_accessed=8 << 20, transcendentals=pairs
        ),
    )(*operands, *sources, totals, grads)


def key_value_back_kernel(groups, info, own, up, down, key_proj, cosine, sine, gain, out, dgain):
    rows = own.shape[1]
    total = jnp.zeros_like(dgain)
    for group in range(groups):
        grad = own[group].astype(F32) + up[group].astype(F32) + down[group].astype(F32)
        part = slice(group * rows, (group + 1) * rows)
        values_grad = grad
        grad = turn(grad, cosine[...], -sine[...])
        keys = key_proj[part]
        scale = lax.rsqrt(jnp.mean(keys * keys, axis=-1, keepdims=True) + EPS)
        unit = keys * scale
        total = total + jnp.sum(grad * unit, axis=0, keepdims=True)
        weighted = grad * gain[...]
        keys_grad = scale * (weighted - unit * jnp.mean(weighted * unit, axis=-1, keepdims=True))
        out[part, :] = jnp.where(info[3] == 0, keys_grad, values_grad).astype(BF16)
    dgain[...] = jnp.where(info[3] == 0, total, 0.0)


def out_sent_kernel(count, info, attended, *refs):
    *sources, sent, weights = refs

    def write(index, ref):
        start = pl.multiple_of(index * HEAD_DIM, HEAD_DIM)
        weights[pl.ds(start, HEAD_DIM), :] = ref[...]

    place_line(sources, info[0], count, write)
    out_parts(info, CORE, attended, weights, sent)


def out_kept_kernel(info, attended, weights, kept):
    out_parts(info, 0, attended, weights, kept)


def rows_for(info, flip, ref, rows):
    return [
        ref[pl.ds(pl.multiple_of((info[1] ^ (bits | flip)) * rows, rows), rows), :] for bits in FLIPS
    ]


def out_parts(info, flip, attended, weights, out):
    rows, width = out.shape[1:]
    left = jnp.concatenate(rows_for(info, flip, attended, rows), axis=0)
    for start in range(0, width, 512):
        part = slice(start, start + 512)
        out[:, :, part] = dot(left, weights[:, part]).astype(BF16).reshape(4, rows, 512)


def normed_grad_kernel(flip, info, query_grad, key_value_grad, query_weights, key_value_weights, units, out, sums):
    rows, width = out.shape[1:]
    left = jnp.concatenate(rows_for(info, flip, query_grad, rows), axis=0)
    other = jnp.concatenate(rows_for(info, flip, key_value_grad, rows), axis=0)
    unit = jnp.concatenate(rows_for(info, flip, units, rows), axis=0)
    for start in range(0, width, 512):
        part = slice(start, start + 512)
        grad = dot_nt(left, query_weights[part]) + dot_nt(other, key_value_weights[part])
        out[:, :, part] = grad.astype(BF16).reshape(4, rows, 512)
        sums[:, part] = jnp.sum(grad * unit[:, part].astype(F32), axis=0, keepdims=True)


def middle_kernel(info, own, across, aside, tokens, gain, middle, routed, scale_out):
    values = own[...] + across[...].astype(F32) + aside[...].astype(F32) + tokens[...].astype(F32)
    scale = lax.rsqrt(jnp.mean(values * values, axis=-1, keepdims=True) + EPS)
    middle[...] = values
    routed[...] = (values * scale * gain[...]).astype(BF16)
    scale_out[...] = scale


def gradient_spread_kernel(info, weights, *refs):
    *blocks, gathered, attended_grad = refs

    def write(row, ref):
        gathered[pl.ds(row, ref.shape[0]), :] = ref[...]

    place_plane(blocks, info[1], write)
    attended_grad[...] = dot_nt(gathered[...], weights[...]).astype(BF16)


def gates_of(token_rows, router, choices):
    logits = jnp.where(choices, dot(token_rows, router), BIG_NEG)
    exponent = jnp.where(choices, jnp.exp(logits - jnp.max(logits, axis=-1, keepdims=True)), 0.0)
    return exponent / jnp.maximum(jnp.sum(exponent, axis=-1, keepdims=True), 1e-30)


def gates_kernel(info, routed, router, picked, gates):
    gates[...] = gates_of(routed[...], router[...], picked[...][:, : gates.shape[1]] > 0.5)


def dispatch_kernel(steps, info, table, *refs):
    *blocks, out = refs
    members = out.shape[0]
    slots = table.shape[2] // members
    for at, step in enumerate(steps):
        block = block_of_step(blocks, info, steps, step)
        rows = dot_tn(table[info[4 + step]], block).astype(BF16)
        out[:, at * slots : (at + 1) * slots, :] = rows.reshape(members, slots, out.shape[2])


def dispatch_with_choices_kernel(steps, info, table, picked, *refs):
    *blocks, out = refs
    members, _, width = out.shape
    slots = table.shape[2] // members
    for at, step in enumerate(steps):
        place = table[info[4 + step]]
        part = slice(at * slots, (at + 1) * slots)
        rows = dot_tn(place, block_of_step(blocks, info, steps, step)).astype(BF16)
        choices = dot_tn(place, picked[info[4 + step]]).astype(BF16)
        model = rows.shape[1]
        out[:, part, :model] = rows.reshape(members, slots, model)
        out[:, part, model:] = choices.reshape(members, slots, width - model)


def combine_kernel(steps, info, table, arrived, *outs):
    members, _, width = arrived.shape
    slots = table.shape[2] // members
    for at, (step, out) in enumerate(zip(steps, outs)):
        rows = arrived[:, at * slots : (at + 1) * slots, :].reshape(members * slots, width)
        out[...] = dot(table[info[4 + step]], rows).astype(out.dtype)


def combine_all_kernel(info, table, arrived, out):
    members, _, width = arrived.shape
    slots = table.shape[2] // members
    for step in range(out.shape[0]):
        rows = arrived[:, step * slots : (step + 1) * slots, :].reshape(members * slots, width)
        place = info[4 + step]
        out[place] = dot(table[place], rows).astype(BF16)


def expert_prepare_kernel(info, arrived, down, grad_hidden):
    members, slots, _ = arrived.shape
    model = down.shape[2]
    rows = arrived[:, :, :model].reshape(members * slots, model)
    for start in range(0, FFE, 256):
        grad = dot_nt(rows, down[0, start : start + 256, :])
        grad_hidden[:, :, start : start + 256] = grad.reshape(members, slots, 256)


def expert_kernel(first, experts, info, arrived, grad_hidden, dy_rows, router, weights, act, hidden_out, back):
    members, slots, width = arrived.shape
    rows = members * slots
    inputs = arrived[...].reshape(rows, width)
    part = slice(first, first + slots)
    chosen = dy_rows[:, part, width:].reshape(rows, -1)[:, :experts] > 0.5
    own = lax.broadcasted_iota(jnp.int32, (rows, experts), 1) == info[2]
    gate = jnp.sum(
        jnp.where(own, gates_of(inputs, router[...], chosen), 0.0), axis=-1, keepdims=True
    )
    grad_gate = jnp.zeros((rows, 1), F32)
    for start in range(0, FFE, 256):
        piece = slice(start, start + 256)
        lower = slice(FFE + start, FFE + start + 256)
        gate_in = dot(inputs, weights[0, :, piece])
        up_in = dot(inputs, weights[0, :, lower])
        grad_in = grad_hidden[:, part, piece].reshape(rows, 256)
        sigmoid = 1.0 / (1.0 + jnp.exp(-gate_in))
        silu = gate_in * sigmoid
        hidden = silu * up_in
        grad_gate = grad_gate + jnp.sum(hidden * grad_in, axis=-1, keepdims=True)
        scaled = grad_in * gate
        act[:, piece] = (scaled * up_in * (sigmoid + silu * (1.0 - sigmoid))).astype(BF16)
        act[:, lower] = (scaled * silu).astype(BF16)
        hidden_out[:, piece] = (hidden * gate).astype(BF16)
    for start in range(0, width, 512):
        piece = slice(start, start + 512)
        grad = dot_nt(act[...], weights[0, piece, :]).astype(BF16)
        back[:, :, piece] = grad.reshape(members, slots, 512)
    extra = back.shape[2] - width
    high = grad_gate.astype(BF16).astype(F32)
    lane = lax.broadcasted_iota(jnp.int32, (rows, extra), 1)
    columns = jnp.where(lane == info[2], high, 0.0)
    columns = columns + jnp.where(lane == info[2] + experts, grad_gate - high, 0.0)
    back[:, :, width:] = columns.astype(BF16).reshape(members, slots, extra)


def results_kernel(info, down, *refs):
    *hiddens, out = refs
    members, _, width = out.shape
    slots = out.shape[1] // len(hiddens)
    for at, hidden in enumerate(hiddens):
        for start in range(0, width, 512):
            piece = slice(start, start + 512)
            rows = dot(hidden[...], down[0, :, piece]).astype(BF16)
            out[:, at * slots : (at + 1) * slots, piece] = rows.reshape(members, slots, 512)


def gate_up_grad(rows, acts):
    count, groups = rows[0].shape[0], len(rows)
    width, columns = rows[0].shape[1], acts[0].shape[1]
    tile = 512

    def kernel(*refs):
        out = refs[-1]
        total = dot_tn(refs[0][...], refs[groups][...])
        for group in range(1, groups):
            total = total + dot_tn(refs[group][...], refs[groups + group][...])
        out[0] = total

    return pl.pallas_call(
        kernel,
        grid=(width // tile,),
        in_specs=[pl.BlockSpec((count, tile), lambda i: (0, i))] * groups
        + [pl.BlockSpec((count, columns), lambda i: (0, 0))] * groups,
        out_specs=pl.BlockSpec((1, tile, columns), lambda i: (0, i, 0)),
        out_shape=shape_of((1, width, columns), F32),
        compiler_params=pltpu.CompilerParams(vmem_limit_bytes=VMEM_LIMIT),
        cost_estimate=pl.CostEstimate(
            flops=2 * groups * count * width * columns, bytes_accessed=24 << 20, transcendentals=0
        ),
    )(*rows, *acts)


def down_grad(hiddens, arrived, model):
    groups, tile = len(hiddens), 256
    count = hiddens[0].shape[0]
    slots = arrived.shape[1] // groups

    def kernel(*refs):
        *lefts, right, out = refs
        total = 0.0
        for group, left in enumerate(lefts):
            rows = right[:, group * slots : (group + 1) * slots, :model].reshape(count, model)
            total = total + dot_tn(left[...], rows)
        out[0] = total

    return pl.pallas_call(
        kernel,
        grid=(FFE // tile,),
        in_specs=[pl.BlockSpec((count, tile), lambda i: (0, i))] * groups
        + [pl.BlockSpec(arrived.shape, lambda i: (0, 0, 0))],
        out_specs=pl.BlockSpec((1, tile, model), lambda i: (0, i, 0)),
        out_shape=shape_of((1, FFE, model), F32),
        compiler_params=pltpu.CompilerParams(vmem_limit_bytes=VMEM_LIMIT),
        cost_estimate=pl.CostEstimate(
            flops=2 * groups * count * FFE * model, bytes_accessed=16 << 20, transcendentals=0
        ),
    )(*hiddens, arrived)


def token_back_kernel(info, own, up, down, gates, router, middle, scale, gain, cotangent, routed, grad_middle, grad_branch, grad_gain, grad_router):
    width = middle.shape[1]
    experts = gates.shape[1]
    total = own[...].astype(F32) + up[...].astype(F32) + down[...].astype(F32)
    extra = total[:, width:]
    grad_gates = extra[:, :experts] + extra[:, experts : 2 * experts]
    values = gates[...]
    grad_logits = values * (grad_gates - jnp.sum(values * grad_gates, axis=-1, keepdims=True))
    grad_logits = grad_logits.astype(BF16)
    grad_routed = total[:, :width] + dot_nt(grad_logits, router[...])
    unit = middle[...] * scale[...]
    grad_gain[...] = jnp.sum(grad_routed * unit, axis=0, keepdims=True)
    weighted = grad_routed * gain[...]
    grad = cotangent[...].astype(F32) + scale[...] * (
        weighted - unit * jnp.mean(weighted * unit, axis=-1, keepdims=True)
    )
    grad_middle[...] = grad
    grad_branch[...] = grad.astype(BF16)
    grad_router[...] = dot_tn(routed[...], grad_logits)


def input_grad_kernel(info, own, across, aside, tokens, gain, grad_middle, out):
    weighted = (own[...] + across[...].astype(F32) + aside[...].astype(F32)) * gain[...]
    values = tokens[...].astype(F32)
    scale = lax.rsqrt(jnp.mean(values * values, axis=-1, keepdims=True) + EPS)
    unit = values * scale
    out[...] = grad_middle[...] + scale * (
        weighted - unit * jnp.mean(weighted * unit, axis=-1, keepdims=True)
    )


def unpack_query_kernel(rep_size, info, arrived, out):
    members, _, columns = arrived.shape
    heads = columns // HEAD_DIM
    for member in range(members):
        for j in range(heads):
            head = (member // rep_size) * heads * rep_size + j * rep_size + member % rep_size
            out[:, head * HEAD_DIM : (head + 1) * HEAD_DIM] = (
                arrived[member, :, j * HEAD_DIM : (j + 1) * HEAD_DIM].astype(F32)
            )


def unpack_key_value_kernel(rep_size, info, arrived, keys, values):
    for group in range(arrived.shape[0] // rep_size):
        part = slice(group * HEAD_DIM, (group + 1) * HEAD_DIM)
        keys[:, part] = arrived[group * rep_size].astype(F32)
        values[:, part] = arrived[group * rep_size + 1].astype(F32)


def body(
    tokens,
    segments,
    routes,
    priority,
    w_query,
    key_matrix,
    value_matrix,
    w_out,
    w_router,
    attn_gain,
    moe_gain,
    query_gain,
    key_norm_weight,
    w_gate_up,
    w_down,
    cotangent,
):
    own_rows, width = tokens.shape[1], tokens.shape[2]
    length = segments.shape[1]
    dp_size, seq_size, rep_size = (lax.axis_size(name) for name in ALL)
    devices = dp_size * seq_size * rep_size
    members = dp_size * rep_size
    dp_at, seq_at, rep_at = (lax.axis_index(name) for name in ALL)
    experts = devices * w_gate_up.shape[0]
    capacity = own_rows * TOPK // experts
    plane_slots = members * capacity
    depth = w_router.shape[0]
    heads = QUERY_HEADS // members
    head_width = heads * HEAD_DIM
    rows = rep_size * own_rows
    plane_rows = members * own_rows
    chunk = members * depth
    extra = -(-2 * experts // LANES) * LANES
    if seq_size == 4:
        order = [jnp.array(ORDER, jnp.int32)[seq_at, step] for step in range(4)]
    else:
        order = [jnp.int32(step) for step in range(seq_size)]
    info = jnp.stack([seq_at, lax.axis_index(PLANE), lax.axis_index(ALL), rep_at] + order)
    own_tokens, own_cotangent = tokens[0], cotangent[0]

    token_blocks = plane_gather(own_tokens)
    query_part, key_value_part = pack_weights(
        w_query, key_matrix, value_matrix, members, rep_size, heads
    )
    key_value_part = swap(key_value_part, PLANE)
    own_documents = lax.dynamic_slice_in_dim(segments, (seq_at * rep_size + rep_at) * own_rows, own_rows, 1)
    packet = run(
        packet_kernel,
        [shape_of((devices, PACKET_ROWS, LANES), BF16)],
        info,
        routes[0],
        priority,
        own_documents,
        moe_gain[None],
        query_gain[None],
        key_norm_weight[None],
        attn_gain[None],
    )[0]
    packet = swap(after(packet, key_value_part), ALL)
    query_part = swap(after(query_part, packet), PLANE)
    key_value_sources = line_gather(key_value_part.reshape(chunk, HEAD_DIM), seq_size)
    query_sources = line_gather(query_part.reshape(chunk, head_width), seq_size)
    router = spread(after(w_router, query_part), ALL, devices).reshape(width, experts)

    packet = packet.astype(F32)
    documents = packet[:, DOCUMENT_ROW].reshape(dp_size, length).astype(jnp.int32)
    first_gain = packet[:, ATTN_GAIN_ROW, :depth].reshape(1, width)
    second_gain = packet[:, MOE_GAIN_ROW, :depth].reshape(1, width)
    query_norm_gain = jnp.sum(packet[:, QUERY_GAIN_ROW], axis=0, keepdims=True)
    key_norm_gain = jnp.sum(packet[:, KEY_GAIN_ROW], axis=0, keepdims=True)
    meta = packet.reshape(dp_size, seq_size, rep_size, PACKET_ROWS, LANES)
    meta = pick(pick(meta, dp_at), rep_at, 1).astype(jnp.int32)
    choice_ids, priority_rank = meta[:, :TOPK], meta[:, PRIORITY_ROW]
    expert_lanes = -(-experts // LANES) * LANES
    expert_ids = jnp.arange(expert_lanes, dtype=jnp.int32)
    picked = jnp.any(choice_ids[:, :, :, None] == expert_ids, axis=1)
    earlier = (priority_rank[:, None, :] < priority_rank[:, :, None]).astype(BF16)
    plane_picked = pick(
        picked[:, :, :experts].reshape(seq_size, own_rows, dp_size, seq_size, rep_size), seq_at, 3
    ).reshape(seq_size, own_rows, members)
    slot_index = jnp.einsum(
        "bts,bse->bte", earlier, plane_picked.astype(BF16), preferred_element_type=F32
    ).astype(jnp.int32)
    slot_ids = jnp.arange(capacity, dtype=jnp.int32)
    table = plane_picked[..., None] & (slot_index[..., None] == slot_ids)
    table = table.reshape(seq_size, own_rows, plane_slots).astype(BF16)
    picked = picked.astype(BF16)

    units = run(
        normalize_kernel, [shape_of((plane_rows, width), BF16)], info, first_gain, *token_blocks
    )[0]
    positions = seq_at * rows + jnp.arange(rows, dtype=jnp.int32)
    frequency = THETA ** (-2.0 * jnp.arange(HEAD_DIM // 2, dtype=F32) / HEAD_DIM)
    angles = positions.astype(F32)[:, None] * jnp.concatenate([frequency, frequency])[None, :]
    sign = jnp.where(jnp.arange(HEAD_DIM) < HEAD_DIM // 2, -1.0, 1.0)
    cosine, sine = jnp.cos(angles), jnp.sin(angles) * sign[None, :]
    key_value_weights, key_proj, key_value_rows = run(
        functools.partial(key_value_kernel, seq_size, dp_size),
        [
            shape_of((width, HEAD_DIM), BF16),
            shape_of((plane_rows, HEAD_DIM), F32),
            shape_of((dp_size, rows, HEAD_DIM), BF16),
        ],
        info,
        units,
        cosine,
        sine,
        key_norm_gain,
        *key_value_sources,
        flops=2 * plane_rows * width * HEAD_DIM,
    )
    mine = line_steps(line_gather(key_value_rows, seq_size), seq_at)
    key_values = mine + [plane_move(block, SIDE) for block in mine]
    query_weights, query_proj = run(
        functools.partial(query_kernel, seq_size, dp_size),
        [shape_of((width, head_width), BF16), shape_of((plane_rows, head_width), F32)],
        info,
        units,
        *query_sources,
        flops=2 * plane_rows * width * head_width,
    )

    steps = list(range(seq_size))
    groups = [steps[: seq_size // 2], steps[seq_size // 2 :]]
    group_slots = len(groups[0]) * capacity
    group_rows = members * group_slots
    cotangent_sources = [lax.all_gather(after(own_cotangent, key_values[0]), "seq")]

    whole_heads = w_out.shape[0] == HEAD_DIM
    if whole_heads:
        out_sources = [lax.all_gather(w_out, "seq")]
    else:
        group = lax.all_gather(w_out, ("seq", "rep"), axis=0, tiled=True)
        group = group.reshape(heads, rep_size, HEAD_DIM, width)
        out_sources = [pick(group, rep_at, 1)]

    query_proj = after(query_proj, router)
    query_doc = lax.dynamic_slice_in_dim(documents, seq_at * rows, rows, axis=1)
    operands = (
        info,
        query_proj,
        query_doc[:, :, None],
        documents[:, None, :],
        positions[:, None],
        cosine,
        sine,
        query_norm_gain,
    )
    attended, totals = attention_forward(operands, key_values, dp_size, heads, rows, length)
    parts_shape = shape_of((4, own_rows, width), BF16)
    part_flops = 8 * own_rows * head_width * width
    sent, out_weights = run(
        functools.partial(out_sent_kernel, heads),
        [parts_shape, shape_of((head_width, width), BF16)],
        info,
        attended,
        *out_sources,
        flops=part_flops,
    )
    kept = run(out_kept_kernel, [parts_shape], info, attended, out_weights, flops=part_flops)[0]
    row_f32, row_bf16 = shape_of((own_rows, width), F32), shape_of((own_rows, width), BF16)
    middle, routed, scale_second = run(
        middle_kernel,
        [row_f32, row_bf16, shape_of((own_rows, 1), F32)],
        info,
        *plane_reduce(info, sent, kept),
        own_tokens,
        second_gain,
    )

    routed_sources = line_gather(routed, seq_size)
    own_picked = pick(picked, seq_at)
    gates = run(
        gates_kernel, [shape_of((own_rows, experts), F32)], info, routed, router, own_picked
    )[0]
    dy_rows = run(
        functools.partial(dispatch_with_choices_kernel, steps),
        [shape_of((members, seq_size * capacity, width + expert_lanes), BF16)],
        info,
        table,
        picked,
        *cotangent_sources,
        flops=2 * own_rows * seq_size * plane_slots * width,
    )[0]
    dy_rows = swap(after(dy_rows, routed), PLANE)
    grad_hidden = run(
        expert_prepare_kernel,
        [shape_of((members, seq_size * capacity, FFE), F32)],
        info,
        dy_rows,
        w_down,
        flops=2 * seq_size * plane_slots * width * FFE,
    )[0]
    arrived, acts, hiddens, backs = [], [], [], []
    token = dy_rows
    for group in groups:
        outgoing = run(
            functools.partial(dispatch_kernel, group),
            [shape_of((members, group_slots, width), BF16)],
            info,
            table,
            *needed(routed_sources, group),
            flops=2 * own_rows * len(group) * plane_slots * width,
        )[0]
        arrived.append(swap(after(outgoing, token), PLANE))
        token = arrived[-1]
    for at in range(2):
        act, hidden, back = run(
            functools.partial(expert_kernel, at * group_slots, experts),
            [
                shape_of((group_rows, 2 * FFE), BF16),
                shape_of((group_rows, FFE), BF16),
                shape_of((members, group_slots, width + extra), BF16),
            ],
            info,
            arrived[at],
            grad_hidden,
            dy_rows,
            router,
            w_gate_up,
            flops=8 * group_rows * width * FFE,
        )
        acts.append(act)
        hiddens.append(hidden)
        backs.append(back)
    pair_parts = [None] * seq_size
    token = arrived[-1]
    for at in (1, 0):
        returned = swap(after(backs[at], token), PLANE)
        token = returned
        kinds = [F32 if step == 0 else BF16 for step in groups[at]]
        combined = run(
            functools.partial(combine_kernel, groups[at]),
            [shape_of((own_rows, width + extra), kind) for kind in kinds],
            info,
            table,
            returned,
            flops=2 * own_rows * len(groups[at]) * plane_slots * (width + extra),
        )
        for step, part in zip(groups[at], combined):
            pair_parts[step] = part
    results = run(
        results_kernel,
        [shape_of((members, seq_size * capacity, width), BF16)],
        info,
        w_down,
        *hiddens,
        flops=4 * group_rows * width * FFE,
    )[0]
    results = swap(after(results, token), PLANE)
    pair_terms = line_reduce(pair_parts, seq_at, seq_size)
    pair_terms = [jnp.zeros(pair_parts[0].shape, BF16) if t is None else t for t in pair_terms]
    grad_gate_up = gate_up_grad([rows_.reshape(group_rows, width) for rows_ in arrived], acts)
    grad_down = down_grad(hiddens, dy_rows, width)
    pair_terms[2] = after(pair_terms[2], grad_gate_up, grad_down)
    grad_middle, grad_branch, grad_moe_gain, grad_router = run(
        token_back_kernel,
        [row_f32, row_bf16, shape_of((1, width), F32), shape_of((width, experts), F32)],
        info,
        *pair_terms,
        gates,
        router,
        middle,
        scale_second,
        second_gain,
        own_cotangent,
        routed,
    )
    result_parts = run(
        combine_all_kernel,
        [shape_of((seq_size, own_rows, width), BF16)],
        info,
        table,
        results,
        flops=2 * own_rows * seq_size * plane_slots * width,
    )[0]
    result_sum = lax.psum_scatter(result_parts, "seq", scatter_dimension=0, tiled=False)
    mixed = (middle + result_sum.astype(F32)).astype(BF16)

    branch_blocks = plane_gather(grad_branch)
    grad_branch, grad_attended = run(
        gradient_spread_kernel,
        [shape_of((plane_rows, width), BF16), shape_of((plane_rows, head_width), BF16)],
        info,
        out_weights,
        *branch_blocks,
        flops=2 * plane_rows * head_width * width,
    )
    grad_out = dot_tn(attended, grad_branch).astype(BF16)
    grad_attended = after(grad_attended, grad_out)
    if whole_heads:
        grad_out = grad_out.reshape(heads, HEAD_DIM, width)
        grad_out = lax.psum_scatter(grad_out, "seq", scatter_dimension=0, tiled=False).astype(F32)
    else:
        group = jnp.zeros((heads, rep_size, HEAD_DIM, width), F32)
        group = lax.dynamic_update_index_in_dim(
            group, grad_out.reshape(heads, HEAD_DIM, width).astype(F32), rep_at, 1
        )
        grad_out = lax.psum_scatter(
            group.reshape(heads * rep_size * HEAD_DIM, width),
            ("seq", "rep"),
            scatter_dimension=0,
            tiled=True,
        )
    half = dp_size // 2
    query_grads, kept_grads, sent_grads, gain_grads = zip(
        *(
            attention_backward(
                operands, key_values, totals, grad_attended, first, half, heads, rows, length
            )
            for first in (0, half)
        )
    )
    grad_query_proj = jnp.concatenate(query_grads)
    grad_query_gain = gain_grads[0] + gain_grads[1]
    kept_grads = [
        kept.astype(F32) + plane_move(sent, SIDE).astype(F32)
        for kept, sent in zip(kept_grads, sent_grads)
    ]
    grad_key_value = jnp.concatenate(kept_grads, axis=1).astype(BF16)
    key_value_terms = line_reduce(
        [pick(grad_key_value, index) for index in order], seq_at, seq_size
    )
    key_value_terms = [
        jnp.zeros((dp_size, rows, HEAD_DIM), BF16) if t is None else t for t in key_value_terms
    ]
    grad_key_value, grad_key_gain = run(
        functools.partial(key_value_back_kernel, dp_size),
        [shape_of((plane_rows, HEAD_DIM), BF16), shape_of((1, HEAD_DIM), F32)],
        info,
        *key_value_terms,
        key_proj,
        cosine,
        sine,
        key_norm_gain,
    )

    def weight_grad(grad, token):
        parts = dot_tn(units, grad).astype(BF16)
        parts = parts.reshape(dp_size, seq_size, rep_size * depth, grad.shape[1])
        parts = [pick(parts, index, 1) for index in order]
        total = total_of(line_reduce(parts, seq_at, seq_size)).astype(BF16)
        return swap(after(total.reshape(members, depth, grad.shape[1]), token), PLANE)

    query_arrived = weight_grad(grad_query_proj, results)
    grad_query = run(
        functools.partial(unpack_query_kernel, rep_size),
        [shape_of(w_query.shape, F32)],
        info,
        query_arrived,
    )[0]
    key_value_arrived = weight_grad(grad_key_value, query_arrived)
    grad_key, grad_value = run(
        functools.partial(unpack_key_value_kernel, rep_size),
        [shape_of(key_matrix.shape, F32)] * 2,
        info,
        key_value_arrived,
    )

    sums = []
    parts = []
    for flip in (CORE, 0):
        part, column_sums = run(
            functools.partial(normed_grad_kernel, flip),
            [parts_shape, shape_of((1, width), F32)],
            info,
            grad_query_proj,
            grad_key_value,
            query_weights,
            key_value_weights,
            units,
            flops=8 * own_rows * (head_width + HEAD_DIM) * width,
        )
        parts.append(part)
        sums.append(column_sums)
    input_grad = run(
        input_grad_kernel,
        [row_f32],
        info,
        *plane_reduce(info, *parts),
        own_tokens,
        first_gain,
        grad_middle,
    )[0]

    pieces = (grad_router, sums[0] + sums[1], grad_moe_gain, grad_query_gain, grad_key_gain)
    small = jnp.concatenate([piece.reshape(devices, -1) for piece in pieces], axis=-1)
    small = jnp.sum(swap(after(small, key_value_arrived), ALL), axis=0)
    bounds = [0]
    for piece in pieces:
        bounds.append(bounds[-1] + piece.size // devices)
    small = [small[a:b] for a, b in zip(bounds[:-1], bounds[1:])]
    return (
        mixed[None],
        input_grad[None],
        grad_query,
        grad_key,
        grad_value,
        grad_out,
        small[0].reshape(depth, experts),
        small[1] / attn_gain.astype(F32),
        small[2],
        small[3],
        small[4],
        grad_gate_up,
        grad_down,
    )


def solution(mesh):
    tokens_spec = P("dp", ("seq", "rep"), None)
    rows_spec = P(ALL, None)
    vector_spec = P(ALL)
    expert_spec = P(ALL, None, None)
    return jax.shard_map(
        body,
        mesh=mesh,
        in_specs=(
            (tokens_spec, P("dp", None), tokens_spec, P("dp", ("seq", "rep")))
            + (rows_spec,) * 5
            + (vector_spec,) * 4
            + (expert_spec, expert_spec, tokens_spec)
        ),
        out_specs=(
            (tokens_spec, tokens_spec)
            + (rows_spec,) * 5
            + (vector_spec,) * 4
            + (expert_spec, expert_spec)
        ),
        check_vma=False,
    )
```

time: 1160 us -> 778 us (0.67)
  waiting for transfers between devices: 635 us -> 253 us
  Pallas kernels: 48.2 us -> 232 us
  blocking collectives: 133 us -> 0 us
  starting transfers between devices: 72.9 us -> 185 us
  matrix products: 120 us -> 9.97 us
  local copies, waits for them, and re-layouts: 83.9 us -> 36.9 us
  other arithmetic: 49.6 us -> 27.5 us
  between operations: 2.05 us -> 22.9 us
    all_to_all x16 -> x13, waiting for transfers between devices: 635 us -> 64.3 us  [swap(): return lax.all_to_all(blocks, axes, split_axis=0, concat_axis=0, tiled=True)]
    ppermute x0 -> x78, waiting for transfers between devices: none -> 188 us  [the longest x44 118 us: line_move(): return lax.ppermute(block, 'seq', list(pairs))]
    pallas_call x0 -> x33, Pallas kernels: none -> 179 us  [the longest x30 155 us: run(): pl.pallas_call(kernel, in_specs=in_specs, out_specs=[pl.BlockSpec(memory_...]
    all_to_all x4 -> x0, blocking collectives: 133 us -> none  [swap(): return lax.all_to_all(blocks, axes, split_axis=0, concat_axis=0, tiled=True)]
    ppermute x0 -> x78, starting transfers between devices: none -> 126 us  [the longest x44 96.1 us: line_move(): return lax.ppermute(block, 'seq', list(pairs))]
    dot_general x14 -> x1, matrix products: 78.2 us -> 0.25 us  [body(): jnp.einsum('bts,bse->bte', earlier, plane_picked.astype(BF16), preferred_...]
    dot_general x7 -> x3, matrix products: 41.7 us -> 9.71 us  [dot_tn(): lax.dot_general(a, b, (((0,), (0,)), ((), ())), preferred_element_type=F32)]
    reduce_sum x16 -> x2, other arithmetic: 25.1 us -> 1.35 us  [the longest x1 1.17 us: body(): key_norm_gain = jnp.sum(packet[:, KEY_GAIN_ROW], axis=0, keepdims=True)]
  transfers between devices with their start and end apart: 16 -> 95, of which waited for: 13 -> 37; matrix products, arithmetic and copies ran while one was open for 15% -> 6% of each run, Pallas kernels for 4% -> 26%
where the time goes in v2:
time: 778 us; the launch traced here: 767 us
  waiting for transfers between devices  253 us (33%)
  Pallas kernels  232 us (30%)
  starting transfers between devices  185 us (24%)
  local copies, waits for them, and re-layouts  36.9 us (5%)
  other arithmetic  27.5 us (4%)
  between operations  22.9 us (3%)
  matrix products  9.97 us (1%)
    pallas_call x30, Pallas kernels, run(): pl.pallas_call(kernel, in_specs=in_specs, out_specs=[pl.BlockSpec(memory_...  155 us
    ppermute x44, waiting for transfers between devices, line_move(): return lax.ppermute(block, 'seq', list(pairs))  118 us
    ppermute x44, starting transfers between devices, line_move(): return lax.ppermute(block, 'seq', list(pairs))  96.1 us
    ppermute x34, waiting for transfers between devices, plane_move(): lax.ppermute(block, PLANE, [(index, index ^ bits) for index in range(8)])  70 us
    all_to_all x13, waiting for transfers between devices, swap(): return lax.all_to_all(blocks, axes, split_axis=0, concat_axis=0, tiled=True)  64.3 us
    all_to_all x13, starting transfers between devices, swap(): return lax.all_to_all(blocks, axes, split_axis=0, concat_axis=0, tiled=True)  58 us
    pallas_call x2, Pallas kernels, attention_backward(): pl.pallas_call(backward_kernel, grid=(sequences, heads), in_specs=attenti...  32.4 us
    ppermute x34, starting transfers between devices, plane_move(): lax.ppermute(block, PLANE, [(index, index ^ bits) for index in range(8)])  30.3 us
  transfers between devices with their start and end apart: 95, of which 37 were waited for; matrix products, arithmetic and copies ran while one was open for 6% of the time, Pallas kernels for 26%

profile of v2, /device:TPU:0, one launch (start us, length us, event | category | flops | bytes accessed | tf_op | source)
XLA Modules:
  0.0 767.0 jit_solution(9136694397998680142)
XLA Ops:
  58.3 8.1 %collective-permute-done.18.refs_4_ = bf16[512,128]{1,0:T(8,128)(2,1)} collective-permute-done((bf16[512,128]{1,0:T(8,128)(2,1)S(1)}, bf16[512,128]{1,0:T(8,128)(2,1)}, u32[]{:S(2)}, u32[]{:S(2)}) %collective-permute-start.18) | collective-permute-done | bytes 131104 | tf_op jit(solution)/shard_map/ppermute | solution.py:136
  67.5 10.0 %collective-permute-start.9 = (bf16[512,512]{1,0:T(8,128)(2,1)}, bf16[512,512]{1,0:T(8,128)(2,1)}, u32[]{:S(2)}, u32[]{:S(2)}) collective-permute-start(bf16[512,512]{1,0:T(8,128)(2,1)} %bitcast.14.refs_0_), channel_id=1, source_target_pairs={{0,2},{2,4},{4,6},{1,3},{3,5},{5,7},{8,10},{10,12},{12,14},{9,11},... | collective-permute-start | bytes 1572872 | tf_op jit(solution)/shard_map/ppermute | solution.py:136
  117.6 13.3 %collective-permute-done.23 = bf16[4,256,128]{2,1,0:T(8,128)(2,1)S(1)} collective-permute-done((bf16[4,256,128]{2,1,0:T(8,128)(2,1)S(1)}, bf16[4,256,128]{2,1,0:T(8,128)(2,1)S(1)}, u32[]{:S(2)}, u32[]{:S(2)}) %collective-permute-start.23) | collective-permute-done | bytes 262176 | tf_op jit(solution)/shard_map/ppermute | solution.py:136
  146.0 8.0 %all-to-all-done.3 = bf16[32,2,1024]{2,1,0:T(2,128)(2,1)S(1)} async-done(((bf16[32,2,1024]{2,1,0:T(2,128)(2,1)}), bf16[32,2,1024]{2,1,0:T(2,128)(2,1)S(1)}, u32[]{:S(2)}, u32[]{:S(2)}) %all-to-all-start.3) | async-done | bytes 131104 | tf_op jit(solution)/shard_map/all_to_all | solution.py:49
  155.2 7.9 %shard_map.294 = (bf16[2048,512]{1,0:T(8,128)(2,1)}, f32[1024,512]{1,0:T(8,128)}) custom-call(s32[8]{0:T(128)} %stack.19.info._, bf16[1024,2048]{1,0:T(8,128)(2,1)} %shard_map.293.units, bf16[512,512]{1,0:T(8,128)(2,1)} %bitcast.14.refs_0_, bf16[512,512]{1,0:T(8,128)(2,1)} %collective-permute-done.9.refs_1_, ...), custom_call_target="tpu_custom_call" | custom-call | flops 2147483648 | bytes 12058624 | tf_op jit(solution)/shard_map/pallas_call | solution.py:65
  168.3 20.5 %shard_map.296 = (bf16[1024,512]{1,0:T(8,128)(2,1)}, f32[4,4,256,1]{3,2,1,0:T(8,128)}) custom-call(s32[8]{0:T(128)} %stack.19.info._, f32[1024,512]{1,0:T(8,128)} %get-tuple-element.95.q_ref, s32[4,256,1]{2,1,0:T(8,128)} %copy.69.qdoc_ref, s32[4,1,1024]{2,1,0:T(1,128)} %bitcast.156, s32[256,1]{1,0:T(8,128)} %iota_add_fusion.qpos_ref, ...), custom_call_target="tpu_custom_call" | custom-call | flops 2147483648 | bytes 8388608 | tf_op jit(solution)/shard_map/pallas_call | solution.py:411
  243.9 10.3 %collective-permute-done.36.refs_1_.refs_0_ = bf16[128,2048]{1,0:T(8,128)(2,1)S(1)} collective-permute-done((bf16[128,2048]{1,0:T(8,128)(2,1)S(1)}, bf16[128,2048]{1,0:T(8,128)(2,1)S(1)}, u32[]{:S(2)}, u32[]{:S(2)}) %collective-permute-start.36) | collective-permute-done | bytes 524320 | tf_op jit(solution)/shard_map/ppermute | solution.py:136
  262.7 27.6 %all-to-all-done.4.arrived.dy_rows.refs_2_ = bf16[8,128,2176]{2,1,0:T(8,128)(2,1)} async-done(((bf16[8,128,2176]{2,1,0:T(8,128)(2,1)}), bf16[8,128,2176]{2,1,0:T(8,128)(2,1)}, u32[]{:S(2)}, u32[]{:S(2)}) %all-to-all-start.4) | async-done | bytes 4456480 | tf_op jit(solution)/shard_map/all_to_all | solution.py:49
  296.7 16.1 %collective-permute-done.39.refs_3_ = bf16[128,2048]{1,0:T(8,128)(2,1)S(1)} collective-permute-done((bf16[128,2048]{1,0:T(8,128)(2,1)S(1)}, bf16[128,2048]{1,0:T(8,128)(2,1)S(1)}, u32[]{:S(2)}, u32[]{:S(2)}) %collective-permute-start.39) | collective-permute-done | bytes 524320 | tf_op jit(solution)/shard_map/ppermute | solution.py:136
  314.1 14.0 %collective-permute-done.41.refs_5_ = bf16[128,2048]{1,0:T(8,128)(2,1)S(1)} collective-permute-done((bf16[128,2048]{1,0:T(8,128)(2,1)S(1)}, bf16[128,2048]{1,0:T(8,128)(2,1)S(1)}, u32[]{:S(2)}, u32[]{:S(2)}) %collective-permute-start.41) | collective-permute-done | bytes 524320 | tf_op jit(solution)/shard_map/ppermute | solution.py:136
  338.9 8.4 %shard_map.304.grad_hidden = f32[8,128,768]{2,1,0:T(8,128)} custom-call(s32[8]{0:T(128)} %stack.19.info._, bf16[8,128,2176]{2,1,0:T(8,128)(2,1)} %all-to-all-done.4.arrived.dy_rows.refs_2_, bf16[1,768,2048]{2,1,0:T(8,128)(2,1)} %down.3), custom_call_target="tpu_custom_call" | custom-call | flops 3221225472 | bytes 10747904 | tf_op jit(solution)/shard_map/pallas_call | solution.py:65
  347.2 17.4 %all-to-all-done.6.arrived = bf16[8,64,2048]{2,1,0:T(8,128)(2,1)} async-done(((bf16[8,64,2048]{2,1,0:T(8,128)(2,1)}), bf16[8,64,2048]{2,1,0:T(8,128)(2,1)}, u32[]{:S(2)}, u32[]{:S(2)}) %all-to-all-start.6) | async-done | bytes 2097184 | tf_op jit(solution)/shard_map/all_to_all | solution.py:49
  364.6 15.9 %shard_map.307 = (bf16[512,1536]{1,0:T(8,128)(2,1)}, bf16[512,768]{1,0:T(8,128)(2,1)}, bf16[8,64,2176]{2,1,0:T(8,128)(2,1)}) custom-call(s32[8]{0:T(128)} %stack.19.info._, bf16[8,64,2048]{2,1,0:T(8,128)(2,1)} %all-to-all-done.6.arrived, f32[8,128,768]{2,1,0:T(8,128)} %shard_map.304.grad_hidden, ...), custom_call_target="tpu_custom_call" | custom-call | flops 6442450944 | bytes 20709376 | tf_op jit(solution)/shard_map/pallas_call | solution.py:65
  384.4 15.8 %shard_map.305 = (bf16[512,1536]{1,0:T(8,128)(2,1)}, bf16[512,768]{1,0:T(8,128)(2,1)}, bf16[8,64,2176]{2,1,0:T(8,128)(2,1)}) custom-call(s32[8]{0:T(128)} %stack.19.info._, bf16[8,64,2048]{2,1,0:T(8,128)(2,1)} %copy-done.11, f32[8,128,768]{2,1,0:T(8,128)} %shard_map.304.grad_hidden, bf16[8,128,2176]{2,1,0:T(8,128)(2,1)} %all-to-all-done.4.arrived.dy_rows.refs_2_, ...), custom_call_target="tpu_custom_call" | custom-call | flops 6442450944 | bytes 20709376 | tf_op jit(solution)/shard_map/pallas_call | solution.py:65
  400.2 11.3 %all-to-all-done.7.arrived = bf16[8,64,2176]{2,1,0:T(8,128)(2,1)S(1)} async-done(((bf16[8,64,2176]{2,1,0:T(8,128)(2,1)}), bf16[8,64,2176]{2,1,0:T(8,128)(2,1)S(1)}, u32[]{:S(2)}, u32[]{:S(2)}) %all-to-all-start.7) | async-done | bytes 2228256 | tf_op jit(solution)/shard_map/all_to_all | solution.py:49
  421.1 12.8 %collective-permute-done.42 = bf16[128,2176]{1,0:T(8,128)(2,1)S(1)} collective-permute-done((bf16[128,2176]{1,0:T(8,128)(2,1)}, bf16[128,2176]{1,0:T(8,128)(2,1)S(1)}, u32[]{:S(2)}, u32[]{:S(2)}) %collective-permute-start.42) | collective-permute-done | bytes 557088 | tf_op jit(solution)/shard_map/ppermute | solution.py:136
  465.2 11.5 %shard_map.312 = f32[1,2048,1536]{2,1,0:T(8,128)} custom-call(bf16[512,2048]{1,0:T(8,128)(2,1)} %bitcast.137, bf16[512,2048]{1,0:T(8,128)(2,1)} %bitcast.34.refs_1_, bf16[512,1536]{1,0:T(8,128)(2,1)} %get-tuple-element.125.refs_2_, bf16[512,1536]{1,0:T(8,128)(2,1)} %get-tuple-element.126.refs_3_), custom_call_target="tpu_custom_call" | custom-call | flops 6442450944 | bytes 25165824 | tf_op jit(solution)/shard_map/pallas_call | solution.py:671
  487.6 9.0 %collective-permute-done.50.refs_4_ = bf16[128,2048]{1,0:T(8,128)(2,1)S(1)} collective-permute-done((bf16[128,2048]{1,0:T(8,128)(2,1)}, bf16[128,2048]{1,0:T(8,128)(2,1)S(1)}, u32[]{:S(2)}, u32[]{:S(2)}) %collective-permute-start.50) | collective-permute-done | bytes 524320 | tf_op jit(solution)/shard_map/ppermute | solution.py:79
  522.2 7.8 %shard_map.308 = bf16[8,128,2048]{2,1,0:T(8,128)(2,1)} custom-call(s32[8]{0:T(128)} %stack.19.info._, bf16[1,768,2048]{2,1,0:T(8,128)(2,1)} %down.3, bf16[512,768]{1,0:T(8,128)(2,1)} %get-tuple-element.112.refs_0_, bf16[512,768]{1,0:T(8,128)(2,1)} %get-tuple-element.114.refs_1_), custom_call_target="tpu_custom_call" | custom-call | flops 3221225472 | bytes 8912896 | tf_op jit(solution)/shard_map/pallas_call | solution.py:65
  539.0 16.1 %shard_map.317 = (bf16[512,512]{1,0:T(8,128)(2,1)}, bf16[4,2,256,128]{3,2,1,0:T(8,128)(2,1)}, bf16[4,2,256,128]{3,2,1,0:T(8,128)(2,1)}, f32[1,128]{1,0:T(1,128)}) custom-call(s32[8]{0:T(128)} %stack.19.info._, f32[1024,512]{1,0:T(8,128)} %get-tuple-element.95.q_ref, s32[4,256,1]{2,1,0:T(8,128)} %copy.69.qdoc_ref, s32[4,1,1024]{2,1,0:T(1,128)} %bitcast.157, ...), custom_call_target="tpu_custom_call" | custom-call | flops 2684354560 | bytes 8388608 | tf_op jit(solution)/shard_map/pallas_call | solution.py:440
  557.1 16.3 %shard_map.318 = (bf16[512,512]{1,0:T(8,128)(2,1)}, bf16[4,2,256,128]{3,2,1,0:T(8,128)(2,1)}, bf16[4,2,256,128]{3,2,1,0:T(8,128)(2,1)}, f32[1,128]{1,0:T(1,128)}) custom-call(s32[8]{0:T(128)} %stack.19.info._, f32[1024,512]{1,0:T(8,128)} %get-tuple-element.95.q_ref, s32[4,256,1]{2,1,0:T(8,128)} %copy.69.qdoc_ref, s32[4,1,1024]{2,1,0:T(1,128)} %bitcast.158, ...), custom_call_target="tpu_custom_call" | custom-call | flops 2684354560 | bytes 8388608 | tf_op jit(solution)/shard_map/pallas_call | solution.py:440
  581.7 12.7 %collective-permute-done.56 = bf16[4,2,256,128]{3,2,1,0:T(8,128)(2,1)S(1)} collective-permute-done((bf16[4,2,256,128]{3,2,1,0:T(8,128)(2,1)}, bf16[4,2,256,128]{3,2,1,0:T(8,128)(2,1)S(1)}, u32[]{:S(2)}, u32[]{:S(2)}) %collective-permute-start.56) | collective-permute-done | bytes 524320 | tf_op jit(solution)/shard_map/ppermute | solution.py:79
  594.5 10.6 %collective-permute-done.57 = bf16[4,2,256,128]{3,2,1,0:T(8,128)(2,1)S(1)} collective-permute-done((bf16[4,2,256,128]{3,2,1,0:T(8,128)(2,1)}, bf16[4,2,256,128]{3,2,1,0:T(8,128)(2,1)S(1)}, u32[]{:S(2)}, u32[]{:S(2)}) %collective-permute-start.57) | collective-permute-done | bytes 524320 | tf_op jit(solution)/shard_map/ppermute | solution.py:79
  650.5 7.8 %collective-permute-done.62.down = bf16[4,256,128]{2,1,0:T(8,128)(2,1)S(1)} collective-permute-done((bf16[4,256,128]{2,1,0:T(8,128)(2,1)S(1)}, bf16[4,256,128]{2,1,0:T(8,128)(2,1)S(1)}, u32[]{:S(2)}, u32[]{:S(2)}) %collective-permute-start.62) | collective-permute-done | bytes 262176 | tf_op jit(solution)/shard_map/ppermute | solution.py:136
  (446 shorter events, 434.7 us)
Async XLA Ops:
  7.2 181.6 %all-gather.5.cloned.1.call-start = ((), (), s32[]{:S(2)}) async-start(), calls=%async_computation.17 | async-start | bytes 2621440 | tf_op jit(solution)/shard_map/all_gather | solution.py:892
  8.0 45.3 %collective-permute-start.3 = (bf16[128,2048]{1,0:T(8,128)(2,1)}, bf16[128,2048]{1,0:T(8,128)(2,1)S(1)}, u32[]{:S(2)}, u32[]{:S(2)}) collective-permute-start(bf16[128,2048]{1,0:T(8,128)(2,1)} %bitcast.119), channel_id=1, source_target_pairs={{0,16},{1,17},{8,24},{9,25},{16,0},{17,1},{24,8},{25,9},{2,18},{3,... | collective-permute-start | bytes 1572872 | tf_op jit(solution)/shard_map/ppermute | solution.py:79
  11.0 44.5 %collective-permute-start = (bf16[128,2048]{1,0:T(8,128)(2,1)}, bf16[128,2048]{1,0:T(8,128)(2,1)S(1)}, u32[]{:S(2)}, u32[]{:S(2)}) collective-permute-start(bf16[128,2048]{1,0:T(8,128)(2,1)} %bitcast.120), channel_id=1, source_target_pairs={{0,1},{1,0},{8,9},{9,8},{16,17},{17,16},{24,25},{25,24},{2,3},{3,2... | collective-permute-start | bytes 1572872 | tf_op jit(solution)/shard_map/ppermute | solution.py:79
  38.0 29.6 %collective-permute-start.1 = (bf16[128,2048]{1,0:T(8,128)(2,1)S(1)}, bf16[128,2048]{1,0:T(8,128)(2,1)S(1)}, u32[]{:S(2)}, u32[]{:S(2)}) collective-permute-start(bf16[128,2048]{1,0:T(8,128)(2,1)S(1)} %bitcast.124), channel_id=1, source_target_pairs={{0,8},{1,9},{8,0},{9,1},{16,24},{17,25},{24,16},{25,17},{2,10},{3,... | collective-permute-start | bytes 1572872 | tf_op jit(solution)/shard_map/ppermute | solution.py:79
  67.5 38.3 %collective-permute-start.9 = (bf16[512,512]{1,0:T(8,128)(2,1)}, bf16[512,512]{1,0:T(8,128)(2,1)}, u32[]{:S(2)}, u32[]{:S(2)}) collective-permute-start(bf16[512,512]{1,0:T(8,128)(2,1)} %bitcast.14.refs_0_), channel_id=1, source_target_pairs={{0,2},{2,4},{4,6},{1,3},{3,5},{5,7},{8,10},{10,12},{12,14},{9,11},... | collective-permute-start | bytes 1572872 | tf_op jit(solution)/shard_map/ppermute | solution.py:136
  77.6 29.8 %collective-permute-start.10 = (bf16[512,512]{1,0:T(8,128)(2,1)}, bf16[512,512]{1,0:T(8,128)(2,1)}, u32[]{:S(2)}, u32[]{:S(2)}) collective-permute-start(bf16[512,512]{1,0:T(8,128)(2,1)} %bitcast.14.refs_0_), channel_id=1, source_target_pairs={{6,4},{4,2},{2,0},{7,5},{5,3},{3,1},{14,12},{12,10},{10,8},{15,13}... | collective-permute-start | bytes 1572872 | tf_op jit(solution)/shard_map/ppermute | solution.py:136
  105.9 26.3 %collective-permute-start.11 = (bf16[512,512]{1,0:T(8,128)(2,1)}, bf16[512,512]{1,0:T(8,128)(2,1)}, u32[]{:S(2)}, u32[]{:S(2)}) collective-permute-start(bf16[512,512]{1,0:T(8,128)(2,1)} %collective-permute-done.9.refs_1_), channel_id=1, source_target_pairs={{2,4},{4,6},{3,5},{5,7},{10,12},{12,14},{11,13},{13,15},{18,20},{2... | collective-permute-start | bytes 1572872 | tf_op jit(solution)/shard_map/ppermute | solution.py:136
  107.4 26.4 %collective-permute-start.12 = (bf16[512,512]{1,0:T(8,128)(2,1)}, bf16[512,512]{1,0:T(8,128)(2,1)}, u32[]{:S(2)}, u32[]{:S(2)}) collective-permute-start(bf16[512,512]{1,0:T(8,128)(2,1)} %collective-permute-done.10.refs_2_), channel_id=1, source_target_pairs={{4,2},{2,0},{5,3},{3,1},{12,10},{10,8},{13,11},{11,9},{20,18},{18,... | collective-permute-start | bytes 1572872 | tf_op jit(solution)/shard_map/ppermute | solution.py:136
  140.6 81.1 %all-gather.7.cloned.1.call-start = ((), (), s32[]{:S(2)}) async-start(), calls=%async_computation.18 | async-start | bytes 2621440 | tf_op jit(solution)/shard_map/all_gather | solution.py:888
  234.6 55.8 %all-to-all-start.4 = ((bf16[8,128,2176]{2,1,0:T(8,128)(2,1)}), bf16[8,128,2176]{2,1,0:T(8,128)(2,1)}, u32[]{:S(2)}, u32[]{:S(2)}) async-start(bf16[8,128,2176]{2,1,0:T(8,128)(2,1)} %shard_map.303), calls=%async_computation.4 | async-start | bytes 8912896 | tf_op jit(solution)/shard_map/all_to_all | solution.py:49
  290.3 42.7 %all-to-all-start.5 = ((bf16[8,64,2048]{2,1,0:T(8,128)(2,1)}), bf16[8,64,2048]{2,1,0:T(8,128)(2,1)S(1)}, u32[]{:S(2)}, u32[]{:S(2)}) async-start(bf16[8,64,2048]{2,1,0:T(8,128)(2,1)} %shard_map.302), calls=%async_computation.5 | async-start | bytes 4194304 | tf_op jit(solution)/shard_map/all_to_all | solution.py:49
  334.3 30.3 %all-to-all-start.6 = ((bf16[8,64,2048]{2,1,0:T(8,128)(2,1)}), bf16[8,64,2048]{2,1,0:T(8,128)(2,1)}, u32[]{:S(2)}, u32[]{:S(2)}) async-start(bf16[8,64,2048]{2,1,0:T(8,128)(2,1)} %shard_map.306), calls=%async_computation.6 | async-start | bytes 4194304 | tf_op jit(solution)/shard_map/all_to_all | solution.py:49
  380.6 30.9 %all-to-all-start.7 = ((bf16[8,64,2176]{2,1,0:T(8,128)(2,1)}), bf16[8,64,2176]{2,1,0:T(8,128)(2,1)S(1)}, u32[]{:S(2)}, u32[]{:S(2)}) async-start(bf16[8,64,2176]{2,1,0:T(8,128)(2,1)} %get-tuple-element.117), calls=%async_computation.7 | async-start | bytes 4456448 | tf_op jit(solution)/shard_map/all_to_all | solution.py:49
  412.9 40.9 %all-to-all-start.8 = ((bf16[8,64,2176]{2,1,0:T(8,128)(2,1)}), bf16[8,64,2176]{2,1,0:T(8,128)(2,1)S(1)}, u32[]{:S(2)}, u32[]{:S(2)}) async-start(bf16[8,64,2176]{2,1,0:T(8,128)(2,1)} %get-tuple-element.118), calls=%async_computation.8 | async-start | bytes 4456448 | tf_op jit(solution)/shard_map/all_to_all | solution.py:49
  416.5 339.7 %reduce-scatter.5.cloned.1.call-start = ((), (), s32[]{:S(2)}) async-start(), calls=%async_computation.16 | async-start | bytes 2621440 | tf_op jit(solution)/shard_map/reduce_scatter | solution.py:1054
  530.0 92.4 %all-to-all-start.9 = ((bf16[8,128,2048]{2,1,0:T(8,128)(2,1)}), bf16[8,128,2048]{2,1,0:T(8,128)(2,1)}, u32[]{:S(2)}, u32[]{:S(2)}) async-start(bf16[8,128,2048]{2,1,0:T(8,128)(2,1)} %shard_map.308), calls=%async_computation.9 | async-start | bytes 8388608 | tf_op jit(solution)/shard_map/all_to_all | solution.py:49
  534.6 223.7 %reduce-scatter.3.cloned.1.call-start = ((), (), s32[]{:S(2)}) async-start(), calls=%async_computation.15 | async-start | bytes 2621440 | tf_op jit(solution)/shard_map/reduce_scatter | solution.py:1038
  555.1 39.2 %collective-permute-start.56 = (bf16[4,2,256,128]{3,2,1,0:T(8,128)(2,1)}, bf16[4,2,256,128]{3,2,1,0:T(8,128)(2,1)S(1)}, u32[]{:S(2)}, u32[]{:S(2)}) collective-permute-start(bf16[4,2,256,128]{3,2,1,0:T(8,128)(2,1)} %get-tuple-element.136), channel_id=1, source_target_pairs={{0,1},{1,0},{8,9},{9,8},{16,17},{17,16},{24,25},{25,24},{2,3},{3,2... | collective-permute-start | bytes 1572872 | tf_op jit(solution)/shard_map/ppermute | solution.py:79
  573.5 31.7 %collective-permute-start.57 = (bf16[4,2,256,128]{3,2,1,0:T(8,128)(2,1)}, bf16[4,2,256,128]{3,2,1,0:T(8,128)(2,1)S(1)}, u32[]{:S(2)}, u32[]{:S(2)}) collective-permute-start(bf16[4,2,256,128]{3,2,1,0:T(8,128)(2,1)} %get-tuple-element.138), channel_id=1, source_target_pairs={{0,1},{1,0},{8,9},{9,8},{16,17},{17,16},{24,25},{25,24},{2,3},{3,2... | collective-permute-start | bytes 1572872 | tf_op jit(solution)/shard_map/ppermute | solution.py:79
  578.1 33.3 %collective-permute-start.68 = (bf16[4,128,512]{2,1,0:T(8,128)(2,1)}, bf16[4,128,512]{2,1,0:T(8,128)(2,1)}, u32[]{:S(2)}, u32[]{:S(2)}) collective-permute-start(bf16[4,128,512]{2,1,0:T(8,128)(2,1)} %dynamic-slice_bitcast_fusion), channel_id=1, source_target_pairs={{0,2},{6,4},{1,3},{7,5},{8,10},{14,12},{9,11},{15,13},{16,18},{22,... | collective-permute-start | bytes 1572872 | tf_op jit(solution)/shard_map/ppermute | solution.py:136
  642.0 41.9 %collective-permute-start.72 = (bf16[4,128,512]{2,1,0:T(8,128)(2,1)}, bf16[4,128,512]{2,1,0:T(8,128)(2,1)S(1)}, u32[]{:S(2)}, u32[]{:S(2)}) collective-permute-start(bf16[4,128,512]{2,1,0:T(8,128)(2,1)} %get-tuple-element.211), channel_id=1, source_target_pairs={{6,4},{4,2},{2,0},{7,5},{5,3},{3,1},{14,12},{12,10},{10,8},{15,13}... | collective-permute-start | bytes 1572872 | tf_op jit(solution)/shard_map/ppermute | solution.py:136
  643.2 40.6 %collective-permute-start.70 = (bf16[4,128,512]{2,1,0:T(8,128)(2,1)}, bf16[4,128,512]{2,1,0:T(8,128)(2,1)S(1)}, u32[]{:S(2)}, u32[]{:S(2)}) collective-permute-start(bf16[4,128,512]{2,1,0:T(8,128)(2,1)} %get-tuple-element.210), channel_id=1, source_target_pairs={{0,2},{2,4},{4,6},{1,3},{3,5},{5,7},{8,10},{10,12},{12,14},{9,11},... | collective-permute-start | bytes 1572872 | tf_op jit(solution)/shard_map/ppermute | solution.py:136
  668.5 51.5 %collective-permute-start.63 = (bf16[4,128,2048]{2,1,0:T(8,128)(2,1)}, bf16[4,128,2048]{2,1,0:T(8,128)(2,1)}, u32[]{:S(2)}, u32[]{:S(2)}) collective-permute-start(bf16[4,128,2048]{2,1,0:T(8,128)(2,1)} %get-tuple-element.143), channel_id=1, source_target_pairs={{0,8},{1,9},{8,0},{9,1},{16,24},{17,25},{24,16},{25,17},{2,10},{3,... | collective-permute-start | bytes 6291464 | tf_op jit(solution)/shard_map/ppermute | solution.py:79
  712.3 31.1 %all-to-all-start.12 = ((f32[32,1,2184]{2,1,0:T(1,128)}), f32[32,1,2184]{2,1,0:T(1,128)S(1)}, u32[]{:S(2)}, u32[]{:S(2)}) async-start(f32[32,1,2184]{2,1,0:T(1,128)} %copy.79), calls=%async_computation.14 | async-start | bytes 589824 | tf_op jit(solution)/shard_map/all_to_all | solution.py:49
  (149 other events, 1913.4 us)
Sparse Core Ops, SparseCore 0:
  9.6 54.1 all-gather.4
  146.1 49.5 all-gather.6
  522.4 41.6 reduce-scatter.4
  627.0 63.9 reduce-scatter.2

commit v3 on v2

--- a/solution.py
+++ b/solution.py
@@ -42,7 +42,14 @@
 
 
 def after(value, *earlier):
-    return lax.optimization_barrier((value,) + earlier)[0]
+    return pl.pallas_call(
+        lambda *refs: None,
+        in_specs=[pl.BlockSpec(memory_space=pl.ANY)] * (1 + len(earlier)),
+        out_specs=pl.BlockSpec(memory_space=pl.ANY),
+        out_shape=jax.ShapeDtypeStruct(value.shape, value.dtype),
+        input_output_aliases={0: 0},
+        cost_estimate=pl.CostEstimate(flops=1000, bytes_accessed=1000, transcendentals=0),
+    )(value, *earlier)
 
 
 def swap(blocks, axes):
@@ -57,22 +64,28 @@
     return jax.ShapeDtypeStruct(shape, dtype)
 
 
-def run(kernel, outs, *operands, scratch=(), flops=0, transcendentals=0):
+def run(kernel, outs, *operands, tokens=(), flops=0, filler=False):
     in_specs = [pl.BlockSpec(memory_space=pltpu.SMEM)]
     in_specs += [pl.BlockSpec(memory_space=pltpu.VMEM)] * (len(operands) - 1)
+    in_specs += [pl.BlockSpec(memory_space=pl.ANY)] * len(tokens)
     touched = sum(o.size * o.dtype.itemsize for o in operands[1:])
     touched += sum(o.size * o.dtype.itemsize for o in outs)
+    if filler:
+        flops, touched = 1000, 1000
+
+    def body(*refs):
+        kernel(*refs[: len(operands)], *refs[len(operands) + len(tokens) :])
+
     return pl.pallas_call(
-        kernel,
+        body,
         in_specs=in_specs,
         out_specs=[pl.BlockSpec(memory_space=pltpu.VMEM)] * len(outs),
         out_shape=outs,
-        scratch_shapes=scratch,
         compiler_params=pltpu.CompilerParams(vmem_limit_bytes=VMEM_LIMIT),
         cost_estimate=pl.CostEstimate(
-            flops=int(flops), bytes_accessed=int(touched), transcendentals=int(transcendentals)
+            flops=int(flops), bytes_accessed=int(touched), transcendentals=0
         ),
-    )(*operands)
+    )(*operands, *tokens)
 
 
 def plane_move(block, bits):
@@ -124,91 +137,63 @@
     across, aside = run(
         second_sums, [whole, whole], info, across, aside, from_across, from_aside
     )
-    return own, plane_move(across, CROSS), plane_move(aside, SIDE)
-
-
-UP, DOWN = ((0, 1), (1, 2), (2, 3)), ((3, 2), (2, 1), (1, 0))
-ORDER = ((0, 1, 2, 3), (1, 2, 0, 3), (2, 1, 3, 0), (3, 2, 1, 0))
-OFFSETS = (0, -1, 1, -2, 2, -3, 3)
-
-
-def line_move(block, pairs):
-    return lax.ppermute(block, "seq", list(pairs))
+    return own, plane_move(across, CROSS), plane_move(aside, SIDE), across
+
+
+def line_move(block, bits):
+    return lax.ppermute(block, "seq", [(place, place ^ bits) for place in range(4)])
 
 
 def line_gather(block, count):
     if count != 4:
         return [spread(block, "seq", count)]
-    up1, down1 = line_move(block, UP), line_move(block, DOWN)
-    up2, down2 = line_move(up1, UP[1:]), line_move(down1, DOWN[1:])
-    up3, down3 = line_move(up2, UP[2:]), line_move(down2, DOWN[2:])
-    return [block, up1, down1, up2, down2, up3, down3]
+    near, second = line_move(block, 1), line_move(block, 2)
+    return [block, near, second, line_move(after(second, near), 1)]
+
+
+def line_gather_near(block, count):
+    return [block, line_move(block, 1)] if count == 4 else [block]
 
 
 def place_line(refs, place, count, write):
-    if len(refs) == 1:
-        for index in range(count):
-            write(index, refs[0].at[index])
-        return
-    for offset, ref in zip(OFFSETS, refs):
-        index = place + offset
-
-        @pl.when((index >= 0) & (index < count))
-        def _(index=index, ref=ref):
-            write(index, ref)
-
-
-def needed_offsets(steps):
-    return [o for o in OFFSETS if any(ORDER[z][step] - z == o for z in range(4) for step in steps)]
+    for at in range(count):
+        if len(refs) == 1:
+            write(at, refs[0].at[at])
+        else:
+            write(place ^ at, refs[at])
 
 
 def needed(sources, steps):
-    if len(sources) == 1:
-        return sources
-    return [dict(zip(OFFSETS, sources))[o] for o in needed_offsets(steps)]
+    return sources if len(sources) == 1 else [sources[step] for step in steps]
 
 
 def block_of_step(refs, info, steps, step):
     if len(refs) == 1:
         return refs[0][info[4 + step]]
-    by_offset = dict(zip(needed_offsets(steps), refs))
-    offsets = [ORDER[z][step] - z for z in range(4)]
-    block = by_offset[offsets[3]][...]
-    for z in range(3):
-        if offsets[z] != offsets[3]:
-            block = jnp.where(info[0] == z, by_offset[offsets[z]][...], block)
-    return block
-
-
-def line_steps(blocks, place):
+    pieces = len(refs) // len(steps)
+    at = steps.index(step) * pieces
+    return jnp.concatenate([ref[...] for ref in refs[at : at + pieces]], axis=0)
+
+
+def line_steps(blocks):
     if len(blocks) == 1:
         return [blocks[0][step] for step in range(blocks[0].shape[0])]
-    block, up1, down1, up2, down2, up3, down3 = blocks
-    low = place < 2
-    return [
-        block,
-        jnp.where(low, down1, up1),
-        jnp.where(low, jnp.where(place == 0, down2, up1), jnp.where(place == 3, up2, down1)),
-        jnp.where(low, jnp.where(place == 0, down3, down2), jnp.where(place == 3, up3, up2)),
-    ]
+    return blocks
+
+
+def line_forward(part, crossing):
+    return (part.astype(F32) + line_move(crossing, 1).astype(F32)).astype(BF16)
 
 
 def line_reduce(parts, place, count):
     if count != 4:
-        total = jnp.sum(swap(jnp.stack(parts).astype(BF16), "seq").astype(F32), axis=0)
-        return total, None, None
-    own, first, second, third = parts
-    edge = (place == 0) | (place == 3)
-    inward = line_move(third.astype(BF16), [(0, 1), (3, 2)])
-    middle = jnp.where(edge, second, third + inward).astype(BF16)
-    up, down = line_move(middle, UP[:2]), line_move(middle, DOWN[:2])
-    up = (jnp.where(place == 2, second, first) + up).astype(BF16)
-    down = (jnp.where(place == 1, second, first) + down).astype(BF16)
-    return own, line_move(up, UP), line_move(down, DOWN)
+        return [jnp.sum(swap(parts, "seq").astype(F32), axis=0)]
+    own, near, second, crossing = (pick(parts, place ^ bits) for bits in range(4))
+    return [own, line_move(line_forward(second, crossing), 2), line_move(near, 1)]
 
 
 def total_of(terms):
-    return sum(term.astype(F32) for term in terms if term is not None)
+    return sum(term.astype(F32) for term in terms)
 
 
 def pick(blocks, index, axis=0):
@@ -250,7 +235,7 @@
     )(*([w_query] * heads), key_matrix, value_matrix)
 
 
-def packet_kernel(info, routes, priority, documents, moe_gain, query_gain, key_gain, attn_gain, out):
+def packet_kernel(rep_size, info, weights, router, routes, priority, documents, moe_gain, query_gain, key_gain, attn_gain, out):
     own = info[2]
     eye = lax.broadcasted_iota(jnp.int32, (LANES, LANES), 0) == lax.broadcasted_iota(
         jnp.int32, (LANES, LANES), 1
@@ -263,19 +248,31 @@
         value = lax.broadcasted_iota(jnp.int32, (size, LANES), 0)
         rows.append(dot(ref[...], (lane == at * size + value).astype(BF16)))
     packet = jnp.concatenate(rows + [jnp.zeros((PACKET_ROWS - 14, LANES), F32)], axis=0).astype(BF16)
-    for index in range(out.shape[0]):
-        out[index] = packet
-
-
-def normalize_kernel(info, gain, *refs):
-    out = refs[-1]
+    depth, count = weights.shape[1], out.shape[0]
+    line = count // weights.shape[0]
+    for index in range(count):
+        member = index // (line * rep_size) * rep_size + index % rep_size
+        out[index, :depth] = weights[member]
+        out[index, depth : depth + PACKET_ROWS] = packet
+        out[index, depth + PACKET_ROWS :] = router[...]
+
+
+def gain_row(packet, depth, out):
+    for index in range(packet.shape[0]):
+        row = packet[index, depth + ATTN_GAIN_ROW : depth + ATTN_GAIN_ROW + 1, :depth]
+        out[:, index * depth : (index + 1) * depth] = row.astype(F32)
+
+
+def normalize_kernel(depth, info, packet, *refs):
+    *refs, out, gain = refs
+    gain_row(packet, depth, gain)
 
     def write(row, ref):
         values = ref[...].astype(F32)
         scale = lax.rsqrt(jnp.mean(values * values, axis=-1, keepdims=True) + EPS)
         out[pl.ds(row, ref.shape[0]), :] = (values * scale * gain[...]).astype(BF16)
 
-    place_plane(refs[:-1], info[1], write)
+    place_plane(refs, info[1], write)
 
 
 def place_weights(refs, info, count, out, groups):
@@ -293,14 +290,19 @@
     return values * cosine + pltpu.roll(values, HEAD_DIM // 2, 1) * sine
 
 
-def key_value_kernel(count, groups, info, units, cosine, sine, gain, *refs):
-    *sources, weights, key_proj, out = refs
-    place_weights(sources, info, count, weights, groups)
+def key_value_kernel(info, units, packet, cosine, sine, key_proj, out, weights, gain):
+    depth = units.shape[1] // packet.shape[0]
+    total = jnp.zeros(gain.shape, F32)
+    for index in range(packet.shape[0]):
+        weights[index * depth : (index + 1) * depth] = packet[index, :depth]
+        row = depth + KEY_GAIN_ROW
+        total = total + packet[index, row : row + 1, :].astype(F32)
+    gain[...] = total
     projected = dot(units[...], weights[...])
     key_proj[...] = projected
     scale = lax.rsqrt(jnp.mean(projected * projected, axis=-1, keepdims=True) + EPS)
-    keys = projected * scale * gain[...]
-    rows = out.shape[1]
+    keys = projected * scale * total
+    groups, rows, _ = out.shape
     for group in range(groups):
         part = slice(group * rows, (group + 1) * rows)
         turned = turn(keys[part], cosine[...], sine[...])
@@ -427,24 +429,32 @@
         ],
         compiler_params=pltpu.CompilerParams(vmem_limit_bytes=VMEM_LIMIT),
         cost_estimate=pl.CostEstimate(
-            flops=4 * pairs * HEAD_DIM, bytes_accessed=8 << 20, transcendentals=pairs
+            flops=1000, bytes_accessed=1000, transcendentals=0
         ),
     )(*operands, *sources)
 
 
-def attention_backward(operands, sources, totals, grads, first, sequences, heads, rows, length):
+def attention_backward(
+    operands, sources, totals, grads, first, sequences, heads, rows, length, tokens=()
+):
     pairs = sequences * heads * rows * length
     parts = length // rows
     key_value_spec = pl.BlockSpec((parts, 1, rows, HEAD_DIM), lambda s, h: (0, s, 0, 0))
     key_value_shape = shape_of((parts, sequences, rows, HEAD_DIM), BF16)
+    count = len(operands) + len(sources) + 2
+
+    def kernel(*refs):
+        backward_kernel(*refs[:count], *refs[count + len(tokens) :])
+
     return pl.pallas_call(
-        backward_kernel,
+        kernel,
         grid=(sequences, heads),
         in_specs=attention_specs(rows, length, sources, first)
         + [
             pl.BlockSpec((1, 1, rows, 1), lambda s, h: (first + s, h, 0, 0)),
             pl.BlockSpec((rows, HEAD_DIM), lambda s, h: (first + s, h)),
-        ],
+        ]
+        + [pl.BlockSpec(memory_space=pl.ANY)] * len(tokens),
         out_specs=[
             pl.BlockSpec((rows, HEAD_DIM), lambda s, h: (s, h)),
             key_value_spec,
@@ -466,16 +476,17 @@
         ],
         compiler_params=pltpu.CompilerParams(vmem_limit_bytes=VMEM_LIMIT),
         cost_estimate=pl.CostEstimate(
-            flops=10 * pairs * HEAD_DIM, bytes_accessed=8 << 20, transcendentals=pairs
+            flops=1000, bytes_accessed=1000, transcendentals=0
         ),
-    )(*operands, *sources, totals, grads)
-
-
-def key_value_back_kernel(groups, info, own, up, down, key_proj, cosine, sine, gain, out, dgain):
-    rows = own.shape[1]
+    )(*operands, *sources, totals, grads, *tokens)
+
+
+def key_value_back_kernel(groups, info, key_proj, cosine, sine, gain, *refs):
+    *terms, out, dgain = refs
+    rows = terms[0].shape[1]
     total = jnp.zeros_like(dgain)
     for group in range(groups):
-        grad = own[group].astype(F32) + up[group].astype(F32) + down[group].astype(F32)
+        grad = total_of([term[group] for term in terms])
         part = slice(group * rows, (group + 1) * rows)
         values_grad = grad
         grad = turn(grad, cosine[...], -sine[...])
@@ -582,38 +593,51 @@
         out[:, part, model:] = choices.reshape(members, slots, width - model)
 
 
-def combine_kernel(steps, info, table, arrived, *outs):
+def combined(table, place, arrived, at):
     members, _, width = arrived.shape
     slots = table.shape[2] // members
-    for at, (step, out) in enumerate(zip(steps, outs)):
-        rows = arrived[:, at * slots : (at + 1) * slots, :].reshape(members * slots, width)
-        out[...] = dot(table[info[4 + step]], rows).astype(out.dtype)
-
-
-def combine_all_kernel(info, table, arrived, out):
-    members, _, width = arrived.shape
-    slots = table.shape[2] // members
+    rows = arrived[:, at * slots : (at + 1) * slots, :].reshape(members * slots, width)
+    return dot(table[place], rows)
+
+
+def combine_kernel(first, info, table, arrived, *outs):
+    for at, out in enumerate(outs):
+        out[...] = combined(table, info[4 + first + at], arrived, at).astype(out.dtype)
+
+
+def forward_kernel_of_parts(info, part, arrived, out):
+    out[...] = (part[...].astype(F32) + arrived[...].astype(F32)).astype(BF16)
+
+
+def combine_stacked_kernel(first, info, table, arrived, out):
+    slots = table.shape[2] // arrived.shape[0]
+    steps = arrived.shape[1] // slots
     for step in range(out.shape[0]):
-        rows = arrived[:, step * slots : (step + 1) * slots, :].reshape(members * slots, width)
         place = info[4 + step]
-        out[place] = dot(table[place], rows).astype(BF16)
+        if first <= step < first + steps:
+            out[place] = combined(table, place, arrived, step - first).astype(BF16)
+        else:
+            out[place] = jnp.zeros(out.shape[1:], BF16)
+
+
+def copy_kernel(info, value, out):
+    out[...] = value[...]
 
 
 def expert_prepare_kernel(info, arrived, down, grad_hidden):
-    members, slots, _ = arrived.shape
-    model = down.shape[2]
+    members, model = arrived.shape[0], down.shape[2]
+    slots = grad_hidden.shape[0] // members
     rows = arrived[:, :, :model].reshape(members * slots, model)
     for start in range(0, FFE, 256):
         grad = dot_nt(rows, down[0, start : start + 256, :])
-        grad_hidden[:, :, start : start + 256] = grad.reshape(members, slots, 256)
-
-
-def expert_kernel(first, experts, info, arrived, grad_hidden, dy_rows, router, weights, act, hidden_out, back):
+        grad_hidden[:, start : start + 256] = grad
+
+
+def expert_kernel(experts, info, arrived, grad_hidden, dy_rows, router, weights, act, hidden_out, back):
     members, slots, width = arrived.shape
     rows = members * slots
     inputs = arrived[...].reshape(rows, width)
-    part = slice(first, first + slots)
-    chosen = dy_rows[:, part, width:].reshape(rows, -1)[:, :experts] > 0.5
+    chosen = dy_rows[:, :, width:].reshape(rows, -1)[:, :experts] > 0.5
     own = lax.broadcasted_iota(jnp.int32, (rows, experts), 1) == info[2]
     gate = jnp.sum(
         jnp.where(own, gates_of(inputs, router[...], chosen), 0.0), axis=-1, keepdims=True
@@ -624,7 +648,7 @@
         lower = slice(FFE + start, FFE + start + 256)
         gate_in = dot(inputs, weights[0, :, piece])
         up_in = dot(inputs, weights[0, :, lower])
-        grad_in = grad_hidden[:, part, piece].reshape(rows, 256)
+        grad_in = grad_hidden[:, piece]
         sigmoid = 1.0 / (1.0 + jnp.exp(-gate_in))
         silu = gate_in * sigmoid
         hidden = silu * up_in
@@ -645,18 +669,15 @@
     back[:, :, width:] = columns.astype(BF16).reshape(members, slots, extra)
 
 
-def results_kernel(info, down, *refs):
-    *hiddens, out = refs
-    members, _, width = out.shape
-    slots = out.shape[1] // len(hiddens)
-    for at, hidden in enumerate(hiddens):
-        for start in range(0, width, 512):
-            piece = slice(start, start + 512)
-            rows = dot(hidden[...], down[0, :, piece]).astype(BF16)
-            out[:, at * slots : (at + 1) * slots, piece] = rows.reshape(members, slots, 512)
-
-
-def gate_up_grad(rows, acts):
+def results_kernel(info, down, hidden, out):
+    members, slots, width = out.shape
+    for start in range(0, width, 512):
+        piece = slice(start, start + 512)
+        rows = dot(hidden[...], down[0, :, piece]).astype(BF16)
+        out[:, :, piece] = rows.reshape(members, slots, 512)
+
+
+def gate_up_grad(rows, acts, tokens):
     count, groups = rows[0].shape[0], len(rows)
     width, columns = rows[0].shape[1], acts[0].shape[1]
     tile = 512
@@ -672,47 +693,45 @@
         kernel,
         grid=(width // tile,),
         in_specs=[pl.BlockSpec((count, tile), lambda i: (0, i))] * groups
-        + [pl.BlockSpec((count, columns), lambda i: (0, 0))] * groups,
+        + [pl.BlockSpec((count, columns), lambda i: (0, 0))] * groups
+        + [pl.BlockSpec(memory_space=pl.ANY)] * len(tokens),
         out_specs=pl.BlockSpec((1, tile, columns), lambda i: (0, i, 0)),
         out_shape=shape_of((1, width, columns), F32),
         compiler_params=pltpu.CompilerParams(vmem_limit_bytes=VMEM_LIMIT),
         cost_estimate=pl.CostEstimate(
-            flops=2 * groups * count * width * columns, bytes_accessed=24 << 20, transcendentals=0
+            flops=1000, bytes_accessed=1000, transcendentals=0
         ),
-    )(*rows, *acts)
-
-
-def down_grad(hiddens, arrived, model):
+    )(*rows, *acts, *tokens)
+
+
+def down_grad(hiddens, arrived, model, tokens):
     groups, tile = len(hiddens), 256
     count = hiddens[0].shape[0]
-    slots = arrived.shape[1] // groups
 
     def kernel(*refs):
-        *lefts, right, out = refs
         total = 0.0
-        for group, left in enumerate(lefts):
-            rows = right[:, group * slots : (group + 1) * slots, :model].reshape(count, model)
-            total = total + dot_tn(left[...], rows)
-        out[0] = total
+        for left, right in zip(refs[:groups], refs[groups : 2 * groups]):
+            total = total + dot_tn(left[...], right[:, :, :model].reshape(count, model))
+        refs[-1][0] = total
 
     return pl.pallas_call(
         kernel,
         grid=(FFE // tile,),
         in_specs=[pl.BlockSpec((count, tile), lambda i: (0, i))] * groups
-        + [pl.BlockSpec(arrived.shape, lambda i: (0, 0, 0))],
+        + [pl.BlockSpec(arrived[0].shape, lambda i: (0, 0, 0))] * groups
+        + [pl.BlockSpec(memory_space=pl.ANY)] * len(tokens),
         out_specs=pl.BlockSpec((1, tile, model), lambda i: (0, i, 0)),
         out_shape=shape_of((1, FFE, model), F32),
         compiler_params=pltpu.CompilerParams(vmem_limit_bytes=VMEM_LIMIT),
-        cost_estimate=pl.CostEstimate(
-            flops=2 * groups * count * FFE * model, bytes_accessed=16 << 20, transcendentals=0
-        ),
-    )(*hiddens, arrived)
-
-
-def token_back_kernel(info, own, up, down, gates, router, middle, scale, gain, cotangent, routed, grad_middle, grad_branch, grad_gain, grad_router):
+        cost_estimate=pl.CostEstimate(flops=1000, bytes_accessed=1000, transcendentals=0),
+    )(*hiddens, *arrived, *tokens)
+
+
+def token_back_kernel(info, gates, router, middle, scale, gain, cotangent, routed, *refs):
+    *terms, grad_middle, grad_branch, grad_gain, grad_router = refs
     width = middle.shape[1]
     experts = gates.shape[1]
-    total = own[...].astype(F32) + up[...].astype(F32) + down[...].astype(F32)
+    total = total_of([term[...] for term in terms])
     extra = total[:, width:]
     grad_gates = extra[:, :experts] + extra[:, experts : 2 * experts]
     values = gates[...]
@@ -740,22 +759,25 @@
     )
 
 
-def unpack_query_kernel(rep_size, info, arrived, out):
+def mixed_kernel(info, middle, *refs):
+    *terms, out = refs
+    out[...] = (middle[...] + total_of([term[...] for term in terms])).astype(BF16)
+
+
+def unpack_weights_kernel(rep_size, info, arrived, queries, keys, values):
     members, _, columns = arrived.shape
-    heads = columns // HEAD_DIM
+    heads = columns // HEAD_DIM - 1
     for member in range(members):
+        group, rep = member // rep_size, member % rep_size
         for j in range(heads):
-            head = (member // rep_size) * heads * rep_size + j * rep_size + member % rep_size
-            out[:, head * HEAD_DIM : (head + 1) * HEAD_DIM] = (
-                arrived[member, :, j * HEAD_DIM : (j + 1) * HEAD_DIM].astype(F32)
-            )
-
-
-def unpack_key_value_kernel(rep_size, info, arrived, keys, values):
-    for group in range(arrived.shape[0] // rep_size):
-        part = slice(group * HEAD_DIM, (group + 1) * HEAD_DIM)
-        keys[:, part] = arrived[group * rep_size].astype(F32)
-        values[:, part] = arrived[group * rep_size + 1].astype(F32)
+            head = group * heads * rep_size + j * rep_size + rep
+            queries[:, head * HEAD_DIM : (head + 1) * HEAD_DIM] = arrived[
+                member, :, j * HEAD_DIM : (j + 1) * HEAD_DIM
+            ].astype(F32)
+        out = values if rep else keys
+        out[:, group * HEAD_DIM : (group + 1) * HEAD_DIM] = arrived[
+            member, :, heads * HEAD_DIM :
+        ].astype(F32)
 
 
 def body(
@@ -792,23 +814,27 @@
     plane_rows = members * own_rows
     chunk = members * depth
     extra = -(-2 * experts // LANES) * LANES
-    if seq_size == 4:
-        order = [jnp.array(ORDER, jnp.int32)[seq_at, step] for step in range(4)]
-    else:
-        order = [jnp.int32(step) for step in range(seq_size)]
-    info = jnp.stack([seq_at, lax.axis_index(PLANE), lax.axis_index(ALL), rep_at] + order)
+    entry = jnp.arange(4 + seq_size, dtype=jnp.int32)
+    info = (entry - 4) ^ seq_at if seq_size == 4 else entry - 4
+    places = (seq_at, lax.axis_index(PLANE), lax.axis_index(ALL), rep_at)
+    for index, place in enumerate(places):
+        info = jnp.where(entry == index, place, info)
     own_tokens, own_cotangent = tokens[0], cotangent[0]
 
     token_blocks = plane_gather(own_tokens)
     query_part, key_value_part = pack_weights(
         w_query, key_matrix, value_matrix, members, rep_size, heads
     )
-    key_value_part = swap(key_value_part, PLANE)
+    cotangent_sources = [lax.all_gather(own_cotangent, "seq")]
+    query_part = swap(after(query_part, token_blocks[1], token_blocks[4]), PLANE)
+    router_rows = w_router.size // LANES
     own_documents = lax.dynamic_slice_in_dim(segments, (seq_at * rep_size + rep_at) * own_rows, own_rows, 1)
     packet = run(
-        packet_kernel,
-        [shape_of((devices, PACKET_ROWS, LANES), BF16)],
+        functools.partial(packet_kernel, rep_size),
+        [shape_of((devices, depth + PACKET_ROWS + router_rows, LANES), BF16)],
         info,
+        key_value_part,
+        w_router.reshape(router_rows, LANES),
         routes[0],
         priority,
         own_documents,
@@ -816,19 +842,20 @@
         query_gain[None],
         key_norm_weight[None],
         attn_gain[None],
+        tokens=(query_part, *token_blocks[5:7]),
     )[0]
-    packet = swap(after(packet, key_value_part), ALL)
-    query_part = swap(after(query_part, packet), PLANE)
-    key_value_sources = line_gather(key_value_part.reshape(chunk, HEAD_DIM), seq_size)
-    query_sources = line_gather(query_part.reshape(chunk, head_width), seq_size)
-    router = spread(after(w_router, query_part), ALL, devices).reshape(width, experts)
+    packet = swap(packet, ALL)
+    arrival = packet
+    router = packet[:, depth + PACKET_ROWS :].reshape(devices, depth, experts)
+    router = router.reshape(width, experts)
+    packet = packet[:, depth : depth + PACKET_ROWS]
+    query_part = after(query_part.reshape(chunk, head_width), arrival, cotangent_sources[0])
+    query_sources = [lax.all_gather(query_part, "seq")]
 
     packet = packet.astype(F32)
     documents = packet[:, DOCUMENT_ROW].reshape(dp_size, length).astype(jnp.int32)
-    first_gain = packet[:, ATTN_GAIN_ROW, :depth].reshape(1, width)
     second_gain = packet[:, MOE_GAIN_ROW, :depth].reshape(1, width)
     query_norm_gain = jnp.sum(packet[:, QUERY_GAIN_ROW], axis=0, keepdims=True)
-    key_norm_gain = jnp.sum(packet[:, KEY_GAIN_ROW], axis=0, keepdims=True)
     meta = packet.reshape(dp_size, seq_size, rep_size, PACKET_ROWS, LANES)
     meta = pick(pick(meta, dp_at), rep_at, 1).astype(jnp.int32)
     choice_ids, priority_rank = meta[:, :TOPK], meta[:, PRIORITY_ROW]
@@ -847,31 +874,35 @@
     table = table.reshape(seq_size, own_rows, plane_slots).astype(BF16)
     picked = picked.astype(BF16)
 
-    units = run(
-        normalize_kernel, [shape_of((plane_rows, width), BF16)], info, first_gain, *token_blocks
-    )[0]
+    units, first_gain = run(
+        functools.partial(normalize_kernel, depth),
+        [shape_of((plane_rows, width), BF16), shape_of((1, width), F32)],
+        info,
+        arrival,
+        *token_blocks,
+    )
     positions = seq_at * rows + jnp.arange(rows, dtype=jnp.int32)
     frequency = THETA ** (-2.0 * jnp.arange(HEAD_DIM // 2, dtype=F32) / HEAD_DIM)
     angles = positions.astype(F32)[:, None] * jnp.concatenate([frequency, frequency])[None, :]
     sign = jnp.where(jnp.arange(HEAD_DIM) < HEAD_DIM // 2, -1.0, 1.0)
     cosine, sine = jnp.cos(angles), jnp.sin(angles) * sign[None, :]
-    key_value_weights, key_proj, key_value_rows = run(
-        functools.partial(key_value_kernel, seq_size, dp_size),
+    key_proj, key_value_rows, key_value_weights, key_norm_gain = run(
+        key_value_kernel,
         [
-            shape_of((width, HEAD_DIM), BF16),
             shape_of((plane_rows, HEAD_DIM), F32),
             shape_of((dp_size, rows, HEAD_DIM), BF16),
+            shape_of((width, HEAD_DIM), BF16),
+            shape_of((1, HEAD_DIM), F32),
         ],
         info,
         units,
+        arrival,
         cosine,
         sine,
-        key_norm_gain,
-        *key_value_sources,
         flops=2 * plane_rows * width * HEAD_DIM,
     )
-    mine = line_steps(line_gather(key_value_rows, seq_size), seq_at)
-    key_values = mine + [plane_move(block, SIDE) for block in mine]
+    mine = line_steps(line_gather(key_value_rows, seq_size))
+    other = [plane_move(block, SIDE) for block in mine[:-1]]
     query_weights, query_proj = run(
         functools.partial(query_kernel, seq_size, dp_size),
         [shape_of((width, head_width), BF16), shape_of((plane_rows, head_width), F32)],
@@ -880,22 +911,53 @@
         *query_sources,
         flops=2 * plane_rows * width * head_width,
     )
+    key_values = mine + other + [plane_move(mine[-1], SIDE)]
+
+    whole_heads = w_out.shape[0] == HEAD_DIM
+    if whole_heads:
+        held_w_out = run(
+            copy_kernel, [shape_of(w_out.shape, BF16)], info, w_out, tokens=mine[-1:]
+        )[0]
+        out_sources = [lax.all_gather(held_w_out, "seq")]
+    else:
+        group = lax.all_gather(w_out, ("seq", "rep"), axis=0, tiled=True)
+        group = group.reshape(heads, rep_size, HEAD_DIM, width)
+        out_sources = [pick(group, rep_at, 1)]
 
     steps = list(range(seq_size))
     groups = [steps[: seq_size // 2], steps[seq_size // 2 :]]
     group_slots = len(groups[0]) * capacity
     group_rows = members * group_slots
-    cotangent_sources = [lax.all_gather(after(own_cotangent, key_values[0]), "seq")]
-
-    whole_heads = w_out.shape[0] == HEAD_DIM
-    if whole_heads:
-        out_sources = [lax.all_gather(w_out, "seq")]
-    else:
-        group = lax.all_gather(w_out, ("seq", "rep"), axis=0, tiled=True)
-        group = group.reshape(heads, rep_size, HEAD_DIM, width)
-        out_sources = [pick(group, rep_at, 1)]
-
-    query_proj = after(query_proj, router)
+    group_rows = members * group_slots
+    def send_cotangent(group, held, *late):
+        outgoing = run(
+            functools.partial(dispatch_with_choices_kernel, group),
+            [shape_of((members, group_slots, width + expert_lanes), BF16)],
+            info,
+            table,
+            picked,
+            *cotangent_sources,
+            tokens=held,
+            flops=2 * own_rows * len(group) * plane_slots * width,
+        )[0]
+        return swap(after(outgoing, *late) if late else outgoing, PLANE)
+
+    dy_rows = [send_cotangent(groups[0], (key_value_rows,))]
+    dy_rows.append(
+        send_cotangent(groups[1], mine[2:3], dy_rows[0], query_proj, *key_values[seq_size:])
+    )
+    grad_hidden = [
+        run(
+            expert_prepare_kernel,
+            [shape_of((group_rows, FFE), F32)],
+            info,
+            rows_,
+            w_down,
+            filler=True,
+        )[0]
+        for rows_ in dy_rows
+    ]
+
     query_doc = lax.dynamic_slice_in_dim(documents, seq_at * rows, rows, axis=1)
     operands = (
         info,
@@ -916,58 +978,51 @@
         info,
         attended,
         *out_sources,
+        tokens=(dy_rows[1],),
         flops=part_flops,
     )
     kept = run(out_kept_kernel, [parts_shape], info, attended, out_weights, flops=part_flops)[0]
     row_f32, row_bf16 = shape_of((own_rows, width), F32), shape_of((own_rows, width), BF16)
+    *plane_terms, _ = plane_reduce(info, sent, kept)
     middle, routed, scale_second = run(
         middle_kernel,
         [row_f32, row_bf16, shape_of((own_rows, 1), F32)],
         info,
-        *plane_reduce(info, sent, kept),
+        *plane_terms,
         own_tokens,
         second_gain,
     )
 
-    routed_sources = line_gather(routed, seq_size)
+    if seq_size == 4:
+        half_rows = own_rows // 2
+        second = [line_move(routed[:half_rows], 2), line_move(routed[half_rows:], 2)]
+        routed_far = second + [line_move(piece, 1) for piece in second]
+        routed_near = [routed, line_move(routed, 1)]
+        token = second[:1]
+    else:
+        routed_near = routed_far = line_gather(routed, seq_size)
+        token = ()
     own_picked = pick(picked, seq_at)
     gates = run(
         gates_kernel, [shape_of((own_rows, experts), F32)], info, routed, router, own_picked
     )[0]
-    dy_rows = run(
-        functools.partial(dispatch_with_choices_kernel, steps),
-        [shape_of((members, seq_size * capacity, width + expert_lanes), BF16)],
-        info,
-        table,
-        picked,
-        *cotangent_sources,
-        flops=2 * own_rows * seq_size * plane_slots * width,
-    )[0]
-    dy_rows = swap(after(dy_rows, routed), PLANE)
-    grad_hidden = run(
-        expert_prepare_kernel,
-        [shape_of((members, seq_size * capacity, FFE), F32)],
-        info,
-        dy_rows,
-        w_down,
-        flops=2 * seq_size * plane_slots * width * FFE,
-    )[0]
-    arrived, acts, hiddens, backs = [], [], [], []
-    token = dy_rows
-    for group in groups:
+    arrived = []
+    for group, routed_sources in zip(groups, (routed_near, routed_far)):
         outgoing = run(
             functools.partial(dispatch_kernel, group),
             [shape_of((members, group_slots, width), BF16)],
             info,
             table,
-            *needed(routed_sources, group),
+            *routed_sources,
+            tokens=token,
             flops=2 * own_rows * len(group) * plane_slots * width,
         )[0]
-        arrived.append(swap(after(outgoing, token), PLANE))
-        token = arrived[-1]
-    for at in range(2):
-        act, hidden, back = run(
-            functools.partial(expert_kernel, at * group_slots, experts),
+        arrived.append(swap(outgoing, PLANE))
+        token = arrived[-1:]
+    worked, token = {}, ()
+    for at in (1, 0):
+        worked[at] = run(
+            functools.partial(expert_kernel, experts),
             [
                 shape_of((group_rows, 2 * FFE), BF16),
                 shape_of((group_rows, FFE), BF16),
@@ -975,50 +1030,67 @@
             ],
             info,
             arrived[at],
-            grad_hidden,
-            dy_rows,
+            grad_hidden[at],
+            dy_rows[at],
             router,
             w_gate_up,
+            tokens=token,
             flops=8 * group_rows * width * FFE,
         )
-        acts.append(act)
-        hiddens.append(hidden)
-        backs.append(back)
-    pair_parts = [None] * seq_size
-    token = arrived[-1]
-    for at in (1, 0):
-        returned = swap(after(backs[at], token), PLANE)
-        token = returned
-        kinds = [F32 if step == 0 else BF16 for step in groups[at]]
-        combined = run(
-            functools.partial(combine_kernel, groups[at]),
-            [shape_of((own_rows, width + extra), kind) for kind in kinds],
+        token = (worked[at][2],)
+    acts, hiddens, backs = zip(worked[0], worked[1])
+
+    def combine(at, rows_, columns, held=()):
+        group = groups[at]
+        return run(
+            functools.partial(combine_kernel, group[0]),
+            [shape_of((own_rows, columns), BF16)] * len(group),
             info,
             table,
-            returned,
-            flops=2 * own_rows * len(groups[at]) * plane_slots * (width + extra),
+            rows_,
+            tokens=held,
+            flops=2 * own_rows * len(group) * plane_slots * columns,
         )
-        for step, part in zip(groups[at], combined):
-            pair_parts[step] = part
-    results = run(
-        results_kernel,
-        [shape_of((members, seq_size * capacity, width), BF16)],
-        info,
-        w_down,
-        *hiddens,
-        flops=4 * group_rows * width * FFE,
-    )[0]
-    results = swap(after(results, token), PLANE)
-    pair_terms = line_reduce(pair_parts, seq_at, seq_size)
-    pair_terms = [jnp.zeros(pair_parts[0].shape, BF16) if t is None else t for t in pair_terms]
-    grad_gate_up = gate_up_grad([rows_.reshape(group_rows, width) for rows_ in arrived], acts)
-    grad_down = down_grad(hiddens, dy_rows, width)
-    pair_terms[2] = after(pair_terms[2], grad_gate_up, grad_down)
+
+    def send_groups(near, far):
+        if seq_size != 4:
+            return line_reduce(jnp.stack(list(near) + list(far)), seq_at, seq_size)
+        return [near[0], line_move(far[0], 2), line_move(near[1], 1)]
+
+    pairs_far, pairs_near = swap(backs[1], PLANE), swap(backs[0], PLANE)
+    far_parts = combine(1, pairs_far, width + extra)
+    grad_down = down_grad(hiddens, dy_rows, width, far_parts[:1])
+    if seq_size == 4:
+        far_parts = run(
+            forward_kernel_of_parts,
+            [shape_of((own_rows, width + extra), BF16)],
+            info,
+            far_parts[0],
+            line_move(far_parts[1], 1),
+            tokens=(grad_down,),
+        )
+    results = [
+        run(
+            results_kernel,
+            [shape_of((members, group_slots, width), BF16)],
+            info,
+            w_down,
+            hidden,
+            tokens=far_parts[:1],
+            filler=True,
+        )[0]
+        for hidden in hiddens
+    ]
+    near_parts = combine(0, pairs_near, width + extra, far_parts[:1])
+    pair_terms = send_groups(near_parts, far_parts)
+    grad_gate_up = gate_up_grad(
+        [rows_.reshape(group_rows, width) for rows_ in arrived], acts, near_parts[:1]
+    )
+    results_far = swap(results[1], PLANE)
     grad_middle, grad_branch, grad_moe_gain, grad_router = run(
         token_back_kernel,
         [row_f32, row_bf16, shape_of((1, width), F32), shape_of((width, experts), F32)],
         info,
-        *pair_terms,
         gates,
         router,
         middle,
@@ -1026,32 +1098,51 @@
         second_gain,
         own_cotangent,
         routed,
-    )
-    result_parts = run(
-        combine_all_kernel,
+        *pair_terms,
+        tokens=(grad_gate_up, results_far, grad_down, results[0]),
+    )
+    branch_blocks = plane_gather(grad_branch)
+    far_stacked = run(
+        functools.partial(combine_stacked_kernel, groups[1][0]),
         [shape_of((seq_size, own_rows, width), BF16)],
         info,
         table,
-        results,
-        flops=2 * own_rows * seq_size * plane_slots * width,
+        results_far,
+        tokens=branch_blocks[5:7],
+        flops=2 * own_rows * len(groups[1]) * plane_slots * width,
     )[0]
-    result_sum = lax.psum_scatter(result_parts, "seq", scatter_dimension=0, tiled=False)
-    mixed = (middle + result_sum.astype(F32)).astype(BF16)
-
-    branch_blocks = plane_gather(grad_branch)
     grad_branch, grad_attended = run(
         gradient_spread_kernel,
         [shape_of((plane_rows, width), BF16), shape_of((plane_rows, head_width), BF16)],
         info,
         out_weights,
         *branch_blocks,
+        tokens=(far_stacked,),
         flops=2 * plane_rows * head_width * width,
     )
-    grad_out = dot_tn(attended, grad_branch).astype(BF16)
-    grad_attended = after(grad_attended, grad_out)
+    far_sum = lax.psum_scatter(far_stacked, "seq", scatter_dimension=0, tiled=False)
+    results_near = swap(after(results[0], grad_attended), PLANE)
+    half = dp_size // 2
+    first_call = attention_backward(
+        operands, key_values, totals, grad_attended, 0, half, heads, rows, length
+    )
+    grad_out = dot_tn(after(attended, first_call[0]), grad_branch).astype(BF16)
+    second_call = attention_backward(
+        operands,
+        key_values,
+        totals,
+        grad_attended,
+        half,
+        half,
+        heads,
+        rows,
+        length,
+        (grad_out, far_sum),
+    )
+    query_grads, kept_grads, sent_grads, gain_grads = zip(first_call, second_call)
     if whole_heads:
         grad_out = grad_out.reshape(heads, HEAD_DIM, width)
-        grad_out = lax.psum_scatter(grad_out, "seq", scatter_dimension=0, tiled=False).astype(F32)
+        grad_out = lax.psum_scatter(grad_out, "seq", scatter_dimension=0, tiled=False)
     else:
         group = jnp.zeros((heads, rep_size, HEAD_DIM, width), F32)
         group = lax.dynamic_update_index_in_dim(
@@ -1063,65 +1154,54 @@
             scatter_dimension=0,
             tiled=True,
         )
-    half = dp_size // 2
-    query_grads, kept_grads, sent_grads, gain_grads = zip(
-        *(
-            attention_backward(
-                operands, key_values, totals, grad_attended, first, half, heads, rows, length
+    if seq_size == 4:
+        near_terms = near_parts = combine(0, results_near, width, second_call[:1])
+        near_terms = [near_terms[0], line_move(near_terms[1], 1)]
+    else:
+        near_terms = [
+            lax.psum_scatter(
+                run(
+                    functools.partial(combine_stacked_kernel, 0),
+                    [shape_of((seq_size, own_rows, width), BF16)],
+                    info,
+                    table,
+                    results_near,
+                )[0],
+                "seq",
+                scatter_dimension=0,
+                tiled=False,
             )
-            for first in (0, half)
-        )
-    )
+        ]
+    result_terms = near_terms + [far_sum.reshape(own_rows, width)]
     grad_query_proj = jnp.concatenate(query_grads)
     grad_query_gain = gain_grads[0] + gain_grads[1]
     kept_grads = [
         kept.astype(F32) + plane_move(sent, SIDE).astype(F32)
-        for kept, sent in zip(kept_grads, sent_grads)
+        for kept, sent in zip(kept_grads, (sent_grads[0], after(sent_grads[1], results_near)))
     ]
     grad_key_value = jnp.concatenate(kept_grads, axis=1).astype(BF16)
-    key_value_terms = line_reduce(
-        [pick(grad_key_value, index) for index in order], seq_at, seq_size
-    )
-    key_value_terms = [
-        jnp.zeros((dp_size, rows, HEAD_DIM), BF16) if t is None else t for t in key_value_terms
-    ]
+    key_value_terms = line_reduce(grad_key_value, seq_at, seq_size)
     grad_key_value, grad_key_gain = run(
         functools.partial(key_value_back_kernel, dp_size),
         [shape_of((plane_rows, HEAD_DIM), BF16), shape_of((1, HEAD_DIM), F32)],
         info,
-        *key_value_terms,
         key_proj,
         cosine,
         sine,
         key_norm_gain,
-    )
-
-    def weight_grad(grad, token):
-        parts = dot_tn(units, grad).astype(BF16)
+        *key_value_terms,
+        tokens=near_parts[:1],
+    )
+
+    def weight_parts(left, grad):
+        parts = dot_tn(left, grad).astype(BF16)
         parts = parts.reshape(dp_size, seq_size, rep_size * depth, grad.shape[1])
-        parts = [pick(parts, index, 1) for index in order]
-        total = total_of(line_reduce(parts, seq_at, seq_size)).astype(BF16)
-        return swap(after(total.reshape(members, depth, grad.shape[1]), token), PLANE)
-
-    query_arrived = weight_grad(grad_query_proj, results)
-    grad_query = run(
-        functools.partial(unpack_query_kernel, rep_size),
-        [shape_of(w_query.shape, F32)],
-        info,
-        query_arrived,
-    )[0]
-    key_value_arrived = weight_grad(grad_key_value, query_arrived)
-    grad_key, grad_value = run(
-        functools.partial(unpack_key_value_kernel, rep_size),
-        [shape_of(key_matrix.shape, F32)] * 2,
-        info,
-        key_value_arrived,
-    )
-
-    sums = []
-    parts = []
-    for flip in (CORE, 0):
-        part, column_sums = run(
+        return parts.transpose(1, 0, 2, 3)
+
+    query_parts = weight_parts(units, grad_query_proj)
+
+    def normed_grad(flip, held=()):
+        return run(
             functools.partial(normed_grad_kernel, flip),
             [parts_shape, shape_of((1, width), F32)],
             info,
@@ -1130,34 +1210,54 @@
             query_weights,
             key_value_weights,
             units,
+            tokens=held,
             flops=8 * own_rows * (head_width + HEAD_DIM) * width,
         )
-        parts.append(part)
-        sums.append(column_sums)
+
+    sent, sent_sums = normed_grad(CORE, (grad_out,))
+    kept, kept_sums = normed_grad(0)
+    weights_total = lax.psum_scatter(
+        jnp.concatenate([query_parts, weight_parts(units, grad_key_value)], axis=-1),
+        "seq",
+        scatter_dimension=0,
+        tiled=False,
+    ).reshape(members, depth, head_width + HEAD_DIM)
+    *plane_terms, mark = plane_reduce(info, sent, kept)
+
+    pieces = (grad_router, sent_sums + kept_sums, grad_moe_gain, grad_query_gain, grad_key_gain)
+    small = jnp.concatenate([piece.reshape(devices, -1) for piece in pieces], axis=-1)
+    small = jnp.sum(swap(small, ALL), axis=0)
+    bounds = [0]
+    for piece in pieces:
+        bounds.append(bounds[-1] + piece.size // devices)
+    small = [small[a:b] for a, b in zip(bounds[:-1], bounds[1:])]
+    weights_arrived = swap(weights_total, PLANE)
+    grad_query, grad_key, grad_value = run(
+        functools.partial(unpack_weights_kernel, rep_size),
+        [shape_of(w_query.shape, F32)] + [shape_of(key_matrix.shape, F32)] * 2,
+        info,
+        weights_arrived,
+    )
+    mixed = run(
+        mixed_kernel, [row_bf16], info, middle, *result_terms, tokens=plane_terms[1:]
+    )[0]
     input_grad = run(
         input_grad_kernel,
         [row_f32],
         info,
-        *plane_reduce(info, *parts),
+        *plane_terms,
         own_tokens,
         first_gain,
         grad_middle,
     )[0]
 
-    pieces = (grad_router, sums[0] + sums[1], grad_moe_gain, grad_query_gain, grad_key_gain)
-    small = jnp.concatenate([piece.reshape(devices, -1) for piece in pieces], axis=-1)
-    small = jnp.sum(swap(after(small, key_value_arrived), ALL), axis=0)
-    bounds = [0]
-    for piece in pieces:
-        bounds.append(bounds[-1] + piece.size // devices)
-    small = [small[a:b] for a, b in zip(bounds[:-1], bounds[1:])]
     return (
         mixed[None],
         input_grad[None],
         grad_query,
         grad_key,
         grad_value,
-        grad_out,
+        grad_out.astype(F32),
         small[0].reshape(depth, experts),
         small[1] / attn_gain.astype(F32),
         small[2],

time: 778 us -> 700 us (0.90)
  starting transfers between devices: 185 us -> 93.6 us
  blocking collectives: 0 us -> 30.2 us
  waiting for transfers between devices: 253 us -> 230 us
  Pallas kernels: 232 us -> 243 us
  other arithmetic: 27.5 us -> 17.6 us
  local copies, waits for them, and re-layouts: 36.9 us -> 46.4 us
  between operations: 22.9 us -> 15.1 us
    ppermute x44 -> x15, starting transfers between devices: 96.1 us -> 14.8 us  [line_move(): lax.ppermute(block, 'seq', [(place, place ^ bits) for place in range(4)])]
    all_to_all x13 -> x11, waiting for transfers between devices: 64.3 us -> 28.2 us  [swap(): return lax.all_to_all(blocks, axes, split_axis=0, concat_axis=0, tiled=True)]
    all_to_all x0 -> x1, blocking collectives: none -> 30.2 us  [swap(): return lax.all_to_all(blocks, axes, split_axis=0, concat_axis=0, tiled=True)]
    reduce_scatter x1 -> x2, waiting for transfers between devices: 0.01 us -> 24.3 us  [the longest x1 23.7 us: body(): lax.psum_scatter(jnp.concatenate([query_parts, weight_parts(units, grad_k...]
    ppermute x44 -> x15, waiting for transfers between devices: 118 us -> 98.5 us  [line_move(): lax.ppermute(block, 'seq', [(place, place ^ bits) for place in range(4)])]
    unnamed x162 -> x157, local copies, waits for them, and re-layouts: 17.9 us -> 31.9 us
    all_to_all x13 -> x11, starting transfers between devices: 58 us -> 44.5 us  [swap(): return lax.all_to_all(blocks, axes, split_axis=0, concat_axis=0, tiled=True)]
    pallas_call x32 -> x45, Pallas kernels: 187 us -> 199 us  [the longest x36 166 us: run(): pl.pallas_call(body, in_specs=in_specs, out_specs=[pl.BlockSpec(memory_sp...]
  transfers between devices with their start and end apart: 95 -> 66, of which waited for: 37 -> 37; matrix products, arithmetic and copies ran while one was open for 6% -> 7% of each run, Pallas kernels for 26% -> 29%
where the time goes in v3:
time: 700 us; the launch traced here: 689 us
  Pallas kernels  243 us (35%)
  waiting for transfers between devices  230 us (33%)
  starting transfers between devices  93.6 us (13%)
  local copies, waits for them, and re-layouts  46.4 us (7%)
  blocking collectives  30.2 us (4%)
  other arithmetic  17.6 us (3%)
  between operations  15.1 us (2%)
  matrix products  13.4 us (2%)
    pallas_call x36, Pallas kernels, run(): pl.pallas_call(body, in_specs=in_specs, out_specs=[pl.BlockSpec(memory_sp...  166 us
    ppermute x15, waiting for transfers between devices, line_move(): lax.ppermute(block, 'seq', [(place, place ^ bits) for place in range(4)])  98.5 us
    ppermute x34, waiting for transfers between devices, plane_move(): lax.ppermute(block, PLANE, [(index, index ^ bits) for index in range(8)])  78 us
    all_to_all x11, starting transfers between devices, swap(): return lax.all_to_all(blocks, axes, split_axis=0, concat_axis=0, tiled=True)  44.5 us
    ppermute x34, starting transfers between devices, plane_move(): lax.ppermute(block, PLANE, [(index, index ^ bits) for index in range(8)])  33.4 us
    pallas_call x2, Pallas kernels, attention_backward(): pl.pallas_call(kernel, grid=(sequences, heads), in_specs=attention_specs(...  32.4 us
    unnamed x157, local copies, waits for them, and re-layouts  31.9 us
    all_to_all x1, blocking collectives, swap(): return lax.all_to_all(blocks, axes, split_axis=0, concat_axis=0, tiled=True)  30.2 us
  transfers between devices with their start and end apart: 66, of which 37 were waited for; matrix products, arithmetic and copies ran while one was open for 7% of the time, Pallas kernels for 29%

profile of v3, /device:TPU:0, one launch (start us, length us, event | category | flops | bytes accessed | tf_op | source)
XLA Modules:
  0.0 689.2 jit_solution(1410584023573629645)
XLA Ops:
  46.3 30.2 %all_to_all.64.refs_1_.refs_2_ = bf16[32,96,128]{2,1,0:T(8,128)(2,1)} all-to-all(bf16[32,96,128]{2,1,0:T(8,128)(2,1)} %shard_map.257), channel_id=1, replica_groups=mesh['dp'=4,'seq'=4,'rep'=2] {'dp','seq','rep'}, dimensions={0} | all-to-all | bytes 1572864 | tf_op jit(solution)/shard_map/all_to_all | solution.py:56
  106.6 24.0 %collective-permute-done.10.refs_2_.refs_4_.refs_10_ = bf16[4,256,128]{2,1,0:T(8,128)(2,1)S(1)} collective-permute-done((bf16[4,256,128]{2,1,0:T(8,128)(2,1)S(1)}, bf16[4,256,128]{2,1,0:T(8,128)(2,1)S(1)}, u32[]{:S(2)}, u32[]{:S(2)}) %collective-permute-start.10) | collective-permute-done | bytes 262176 | tf_op jit(solution)/shard_map/ppermute | solution.py:144
  132.0 8.5 %collective-permute-done.11.refs_3_.refs_2_.refs_11_ = bf16[4,256,128]{2,1,0:T(8,128)(2,1)S(1)} collective-permute-done((bf16[4,256,128]{2,1,0:T(8,128)(2,1)}, bf16[4,256,128]{2,1,0:T(8,128)(2,1)S(1)}, u32[]{:S(2)}, u32[]{:S(2)}) %collective-permute-start.11) | collective-permute-done | bytes 262176 | tf_op jit(solution)/shard_map/ppermute | solution.py:144
  151.3 6.7 shard_map.260
  177.8 20.5 %shard_map.263 = (bf16[1024,512]{1,0:T(8,128)(2,1)}, f32[4,4,256,1]{3,2,1,0:T(8,128)}) custom-call(s32[8]{0:T(128)} %compare_select_fusion.4.refs_0_.info, f32[1024,512]{1,0:T(8,128)} %get-tuple-element.82.q_ref.refs_2_.refs_1_, s32[4,256,1]{2,1,0:T(8,128)} %copy.72.qdoc_ref.refs_2_, s32[4,1,1024]{2,1,0:T(1,128)} %bitcast.87, ...), custom_call_target="tpu_custom_call" | custom-call | flops 1000 | bytes 1000 | tf_op jit(solution)/shard_map/pallas_call | solution.py:413
  218.2 6.9 %collective-permute-done.17.refs_3_ = bf16[64,2048]{1,0:T(8,128)(2,1)S(1)} collective-permute-done((bf16[64,2048]{1,0:T(8,128)(2,1)}, bf16[64,2048]{1,0:T(8,128)(2,1)S(1)}, u32[]{:S(2)}, u32[]{:S(2)}) %collective-permute-start.17) | collective-permute-done | bytes 262176 | tf_op jit(solution)/shard_map/ppermute | solution.py:92
  233.1 9.5 %collective-permute-done.19.refs_2_ = bf16[128,2048]{1,0:T(8,128)(2,1)S(1)} collective-permute-done((bf16[128,2048]{1,0:T(8,128)(2,1)}, bf16[128,2048]{1,0:T(8,128)(2,1)S(1)}, u32[]{:S(2)}, u32[]{:S(2)}) %collective-permute-start.19) | collective-permute-done | bytes 524320 | tf_op jit(solution)/shard_map/ppermute | solution.py:92
  250.0 13.1 %collective-permute-done.22.refs_4_.refs_2_ = bf16[64,2048]{1,0:T(8,128)(2,1)S(1)} collective-permute-done((bf16[64,2048]{1,0:T(8,128)(2,1)S(1)}, bf16[64,2048]{1,0:T(8,128)(2,1)S(1)}, u32[]{:S(2)}, u32[]{:S(2)}) %collective-permute-start.22) | collective-permute-done | bytes 262176 | tf_op jit(solution)/shard_map/ppermute | solution.py:144
  275.1 12.9 %collective-permute-done.23.refs_3_ = bf16[64,2048]{1,0:T(8,128)(2,1)S(1)} collective-permute-done((bf16[64,2048]{1,0:T(8,128)(2,1)S(1)}, bf16[64,2048]{1,0:T(8,128)(2,1)S(1)}, u32[]{:S(2)}, u32[]{:S(2)}) %collective-permute-start.23) | collective-permute-done | bytes 262176 | tf_op jit(solution)/shard_map/ppermute | solution.py:144
  290.0 7.2 %collective-permute-done.25.refs_5_ = bf16[64,2048]{1,0:T(8,128)(2,1)S(1)} collective-permute-done((bf16[64,2048]{1,0:T(8,128)(2,1)S(1)}, bf16[64,2048]{1,0:T(8,128)(2,1)S(1)}, u32[]{:S(2)}, u32[]{:S(2)}) %collective-permute-start.25) | collective-permute-done | bytes 262176 | tf_op jit(solution)/shard_map/ppermute | solution.py:144
  318.3 19.1 %all-to-all-done.5.refs_1_ = bf16[8,64,2048]{2,1,0:T(8,128)(2,1)S(1)} async-done(((bf16[8,64,2048]{2,1,0:T(8,128)(2,1)}), bf16[8,64,2048]{2,1,0:T(8,128)(2,1)S(1)}, u32[]{:S(2)}, u32[]{:S(2)}) %all-to-all-start.5) | async-done | bytes 2097184 | tf_op jit(solution)/shard_map/all_to_all | solution.py:56
  338.8 14.7 %shard_map.277 = (bf16[512,1536]{1,0:T(8,128)(2,1)}, bf16[512,768]{1,0:T(8,128)(2,1)}, bf16[8,64,2176]{2,1,0:T(8,128)(2,1)}) custom-call(s32[8]{0:T(128)} %compare_select_fusion.4.refs_0_.info, bf16[8,64,2048]{2,1,0:T(8,128)(2,1)} %copy-done.11, f32[512,768]{1,0:T(8,128)} %shard_map.276.refs_2_, bf16[8,64,2176]{2,1,0:T(8,128)(2,1)} %copy-done.4, ...), custom_call_target="tpu_custom_call" | custom-call | flops 6442450944 | bytes 16908288 | tf_op jit(solution)/shard_map/pallas_call | solution.py:79
  362.9 14.8 %shard_map.278 = (bf16[512,1536]{1,0:T(8,128)(2,1)}, bf16[512,768]{1,0:T(8,128)(2,1)}, bf16[8,64,2176]{2,1,0:T(8,128)(2,1)}) custom-call(s32[8]{0:T(128)} %compare_select_fusion.4.refs_0_.info, bf16[8,64,2048]{2,1,0:T(8,128)(2,1)} %copy-done.5, f32[512,768]{1,0:T(8,128)} %shard_map.274.refs_2_, bf16[8,64,2176]{2,1,0:T(8,128)(2,1)} %copy-done.3, ...), custom_call_target="tpu_custom_call" | custom-call | flops 6442450944 | bytes 16908288 | tf_op jit(solution)/shard_map/pallas_call | solution.py:79
  377.6 6.8 all-to-all-done.6.refs_2_
  392.8 7.8 %shard_map.280.refs_3_.refs_13_ = f32[1,768,2048]{2,1,0:T(8,128)} custom-call(bf16[512,768]{1,0:T(8,128)(2,1)} %get-tuple-element.97.refs_0_.refs_2_, bf16[512,768]{1,0:T(8,128)(2,1)} %get-tuple-element.100.refs_1_.refs_2_, bf16[8,64,2176]{2,1,0:T(8,128)(2,1)} %copy-done.3, bf16[8,64,2176]{2,1,0:T(8,128)(2,1)} %copy-done.4, ...), custom_call_target="tpu_custom_call" | custom-call | flops 1000 | bytes 1000 | tf_op jit(solution)/shard_map/pallas_call | solution.py:717
  400.6 7.1 %collective-permute-done.26.refs_2_ = bf16[128,2176]{1,0:T(8,128)(2,1)S(1)} collective-permute-done((bf16[128,2176]{1,0:T(8,128)(2,1)}, bf16[128,2176]{1,0:T(8,128)(2,1)S(1)}, u32[]{:S(2)}, u32[]{:S(2)}) %collective-permute-start.26) | collective-permute-done | bytes 557088 | tf_op jit(solution)/shard_map/ppermute | solution.py:144
  434.9 11.4 %shard_map.285.refs_11_ = f32[1,2048,1536]{2,1,0:T(8,128)} custom-call(bf16[512,2048]{1,0:T(8,128)(2,1)} %bitcast.60, bf16[512,2048]{1,0:T(8,128)(2,1)} %bitcast.61, bf16[512,1536]{1,0:T(8,128)(2,1)} %get-tuple-element.105.refs_2_, bf16[512,1536]{1,0:T(8,128)(2,1)} %get-tuple-element.106.refs_3_, bf16[128,2176]{1,0:T(8,128)(2,1)} %get-tuple-element.103.refs_4_.refs_8_), custom_call_target="tpu_custom_call" | custom-call | flops 1000 | bytes 1000 | tf_op jit(solution)/shard_map/pallas_call | solution.py:692
  461.9 10.2 %collective-permute-done.32.refs_6_ = bf16[128,2048]{1,0:T(8,128)(2,1)S(1)} collective-permute-done((bf16[128,2048]{1,0:T(8,128)(2,1)}, bf16[128,2048]{1,0:T(8,128)(2,1)S(1)}, u32[]{:S(2)}, u32[]{:S(2)}) %collective-permute-start.32) | collective-permute-done | bytes 524320 | tf_op jit(solution)/shard_map/ppermute | solution.py:92
  501.2 16.2 %shard_map.291 = (bf16[512,512]{1,0:T(8,128)(2,1)}, bf16[4,2,256,128]{3,2,1,0:T(8,128)(2,1)}, bf16[4,2,256,128]{3,2,1,0:T(8,128)(2,1)}, f32[1,128]{1,0:T(1,128)}) custom-call(s32[8]{0:T(128)} %compare_select_fusion.4.refs_0_.info, f32[1024,512]{1,0:T(8,128)} %get-tuple-element.82.q_ref.refs_2_.refs_1_, s32[4,256,1]{2,1,0:T(8,128)} %copy.72.qdoc_ref.refs_2_, ...), custom_call_target="tpu_custom_call" | custom-call | flops 1000 | bytes 1000 | tf_op jit(solution)/shard_map/pallas_call | solution.py:449
  526.5 16.2 %shard_map.293 = (bf16[512,512]{1,0:T(8,128)(2,1)}, bf16[4,2,256,128]{3,2,1,0:T(8,128)(2,1)}, bf16[4,2,256,128]{3,2,1,0:T(8,128)(2,1)}, f32[1,128]{1,0:T(1,128)}) custom-call(s32[8]{0:T(128)} %compare_select_fusion.4.refs_0_.info, f32[1024,512]{1,0:T(8,128)} %get-tuple-element.82.q_ref.refs_2_.refs_1_, s32[4,256,1]{2,1,0:T(8,128)} %copy.72.qdoc_ref.refs_2_, ...), custom_call_target="tpu_custom_call" | custom-call | flops 1000 | bytes 1000 | tf_op jit(solution)/shard_map/pallas_call | solution.py:449
  545.7 12.1 %collective-permute-done.40 = bf16[4,2,256,128]{3,2,1,0:T(8,128)(2,1)S(1)} collective-permute-done((bf16[4,2,256,128]{3,2,1,0:T(8,128)(2,1)}, bf16[4,2,256,128]{3,2,1,0:T(8,128)(2,1)S(1)}, u32[]{:S(2)}, u32[]{:S(2)}) %collective-permute-start.40) | collective-permute-done | bytes 524320 | tf_op jit(solution)/shard_map/ppermute | solution.py:92
  563.1 11.5 %collective-permute-done.41 = bf16[4,256,128]{2,1,0:T(8,128)(2,1)S(1)} collective-permute-done((bf16[4,256,128]{2,1,0:T(8,128)(2,1)}, bf16[4,256,128]{2,1,0:T(8,128)(2,1)S(1)}, u32[]{:S(2)}, u32[]{:S(2)}) %collective-permute-start.41) | collective-permute-done | bytes 262176 | tf_op jit(solution)/shard_map/ppermute | solution.py:144
  594.5 6.6 shard_map.297
  640.3 23.7 %reduce-scatter.8.cloned.1.call-done = bf16[1,4,128,640]{3,2,1,0:T(8,128)(2,1)} async-done(((bf16[4,4,128,640]{3,2,1,0:T(8,128)(2,1)}), bf16[1,4,128,640]{3,2,1,0:T(8,128)(2,1)}) %reduce-scatter.8.cloned.1.call-update) | async-done | bytes 655376 | tf_op jit(solution)/shard_map/reduce_scatter | solution.py:1219
  (389 shorter events, 356.5 us)
Async XLA Ops:
  7.2 69.3 %all-gather.6.cloned.1.call-start = ((), (), s32[]{:S(2)}) async-start(), calls=%async_computation.15 | async-start | bytes 2621440 | tf_op jit(solution)/shard_map/all_gather | solution.py:828
  29.0 122.3 %all-gather.8.cloned.1.call-start = ((), (), s32[]{:S(2)}) async-start(), calls=%async_computation.19 | async-start | bytes 2621440 | tf_op jit(solution)/shard_map/all_gather | solution.py:853
  101.5 66.1 %all-to-all-start.2 = ((bf16[8,64,2176]{2,1,0:T(8,128)(2,1)}), bf16[8,64,2176]{2,1,0:T(8,128)(2,1)S(1)}, u32[]{:S(2)}, u32[]{:S(2)}) async-start(bf16[8,64,2176]{2,1,0:T(8,128)(2,1)} %shard_map.266), calls=%async_computation.2 | async-start | bytes 4456448 | tf_op jit(solution)/shard_map/all_to_all | solution.py:56
  105.3 93.1 %all-gather.10.cloned.1.call-start = ((), (), s32[]{:S(2)}) async-start(), calls=%async_computation.20 | async-start | bytes 2621440 | tf_op jit(solution)/shard_map/all_gather | solution.py:921
  105.3 25.2 %collective-permute-start.10 = (bf16[4,256,128]{2,1,0:T(8,128)(2,1)S(1)}, bf16[4,256,128]{2,1,0:T(8,128)(2,1)S(1)}, u32[]{:S(2)}, u32[]{:S(2)}) collective-permute-start(bf16[4,256,128]{2,1,0:T(8,128)(2,1)S(1)} %copy-done.16), channel_id=1, source_target_pairs={{0,4},{2,6},{4,0},{6,2},{1,5},{3,7},{5,1},{7,3},{8,12},{10,14},{12... | collective-permute-start | bytes 786440 | tf_op jit(solution)/shard_map/ppermute | solution.py:144
  105.4 25.8 %collective-permute-start.9 = (bf16[4,256,128]{2,1,0:T(8,128)(2,1)S(1)}, bf16[4,256,128]{2,1,0:T(8,128)(2,1)S(1)}, u32[]{:S(2)}, u32[]{:S(2)}) collective-permute-start(bf16[4,256,128]{2,1,0:T(8,128)(2,1)S(1)} %copy-done.16), channel_id=1, source_target_pairs={{0,2},{2,0},{4,6},{6,4},{1,3},{3,1},{5,7},{7,5},{8,10},{10,8},{12,... | collective-permute-start | bytes 786440 | tf_op jit(solution)/shard_map/ppermute | solution.py:144
  169.0 31.1 %all-to-all-start.3 = ((bf16[8,64,2176]{2,1,0:T(8,128)(2,1)}), bf16[8,64,2176]{2,1,0:T(8,128)(2,1)S(1)}, u32[]{:S(2)}, u32[]{:S(2)}) async-start(bf16[8,64,2176]{2,1,0:T(8,128)(2,1)} %shard_map.267), calls=%async_computation.3 | async-start | bytes 4456448 | tf_op jit(solution)/shard_map/all_to_all | solution.py:56
  269.1 32.6 %all-to-all-start.4 = ((bf16[8,64,2048]{2,1,0:T(8,128)(2,1)}), bf16[8,64,2048]{2,1,0:T(8,128)(2,1)S(1)}, u32[]{:S(2)}, u32[]{:S(2)}) async-start(bf16[8,64,2048]{2,1,0:T(8,128)(2,1)} %shard_map.273), calls=%async_computation.4 | async-start | bytes 4194304 | tf_op jit(solution)/shard_map/all_to_all | solution.py:56
  307.1 30.3 %all-to-all-start.5 = ((bf16[8,64,2048]{2,1,0:T(8,128)(2,1)}), bf16[8,64,2048]{2,1,0:T(8,128)(2,1)S(1)}, u32[]{:S(2)}, u32[]{:S(2)}) async-start(bf16[8,64,2048]{2,1,0:T(8,128)(2,1)} %shard_map.275), calls=%async_computation.5 | async-start | bytes 4194304 | tf_op jit(solution)/shard_map/all_to_all | solution.py:56
  353.5 30.9 %all-to-all-start.6 = ((bf16[8,64,2176]{2,1,0:T(8,128)(2,1)}), bf16[8,64,2176]{2,1,0:T(8,128)(2,1)S(1)}, u32[]{:S(2)}, u32[]{:S(2)}) async-start(bf16[8,64,2176]{2,1,0:T(8,128)(2,1)} %get-tuple-element.96.refs_6_), calls=%async_computation.6 | async-start | bytes 4456448 | tf_op jit(solution)/shard_map/all_to_all | solution.py:56
  385.8 30.7 %all-to-all-start.7 = ((bf16[8,64,2176]{2,1,0:T(8,128)(2,1)}), bf16[8,64,2176]{2,1,0:T(8,128)(2,1)S(1)}, u32[]{:S(2)}, u32[]{:S(2)}) async-start(bf16[8,64,2176]{2,1,0:T(8,128)(2,1)} %get-tuple-element.102), calls=%async_computation.7 | async-start | bytes 4456448 | tf_op jit(solution)/shard_map/all_to_all | solution.py:56
  417.9 34.9 %all-to-all-start.8 = ((bf16[8,64,2048]{2,1,0:T(8,128)(2,1)}), bf16[8,64,2048]{2,1,0:T(8,128)(2,1)S(1)}, u32[]{:S(2)}, u32[]{:S(2)}) async-start(bf16[8,64,2048]{2,1,0:T(8,128)(2,1)} %shard_map.286), calls=%async_computation.8 | async-start | bytes 4194304 | tf_op jit(solution)/shard_map/all_to_all | solution.py:56
  421.5 105.1 %reduce-scatter.4.cloned.1.call-start = ((), (), s32[]{:S(2)}) async-start(), calls=%async_computation.16 | async-start | bytes 2621440 | tf_op jit(solution)/shard_map/reduce_scatter | solution.py:1123
  424.8 25.3 %collective-permute-start.28 = (bf16[128,2176]{1,0:T(8,128)(2,1)}, bf16[128,2176]{1,0:T(8,128)(2,1)S(1)}, u32[]{:S(2)}, u32[]{:S(2)}) collective-permute-start(bf16[128,2176]{1,0:T(8,128)(2,1)} %get-tuple-element.104), channel_id=1, source_target_pairs={{0,2},{2,0},{4,6},{6,4},{1,3},{3,1},{5,7},{7,5},{8,10},{10,8},{12,... | collective-permute-start | bytes 1671176 | tf_op jit(solution)/shard_map/ppermute | solution.py:144
  425.1 27.6 %collective-permute-start.27 = (bf16[128,2176]{1,0:T(8,128)(2,1)S(1)}, bf16[128,2176]{1,0:T(8,128)(2,1)}, u32[]{:S(2)}, u32[]{:S(2)}) collective-permute-start(bf16[128,2176]{1,0:T(8,128)(2,1)S(1)} %copy-done.10), channel_id=1, source_target_pairs={{0,4},{2,6},{4,0},{6,2},{1,5},{3,7},{5,1},{7,3},{8,12},{10,14},{12... | collective-permute-start | bytes 1671176 | tf_op jit(solution)/shard_map/ppermute | solution.py:144
  497.5 45.2 %all-to-all-start.9 = ((bf16[8,64,2048]{2,1,0:T(8,128)(2,1)}), bf16[8,64,2048]{2,1,0:T(8,128)(2,1)S(1)}, u32[]{:S(2)}, u32[]{:S(2)}) async-start(bf16[8,64,2048]{2,1,0:T(8,128)(2,1)} %shard_map.290), calls=%async_computation.9 | async-start | bytes 4194304 | tf_op jit(solution)/shard_map/all_to_all | solution.py:56
  501.2 93.3 %reduce-scatter.6.cloned.1.call-start = ((), (), s32[]{:S(2)}) async-start(), calls=%async_computation.17 | async-start | bytes 2621440 | tf_op jit(solution)/shard_map/reduce_scatter | solution.py:1145
  523.6 140.4 %reduce-scatter.8.cloned.1.call-start = ((), (), s32[]{:S(2)}) async-start(), calls=%async_computation.18 | async-start | bytes 3276800 | tf_op jit(solution)/shard_map/reduce_scatter | solution.py:1219
  524.1 21.5 %collective-permute-start.39 = (bf16[4,2,256,128]{3,2,1,0:T(8,128)(2,1)}, bf16[4,2,256,128]{3,2,1,0:T(8,128)(2,1)S(1)}, u32[]{:S(2)}, u32[]{:S(2)}) collective-permute-start(bf16[4,2,256,128]{3,2,1,0:T(8,128)(2,1)} %get-tuple-element.118), channel_id=1, source_target_pairs={{0,1},{1,0},{8,9},{9,8},{16,17},{17,16},{24,25},{25,24},{2,3},{3,2... | collective-permute-start | bytes 1572872 | tf_op jit(solution)/shard_map/ppermute | solution.py:92
  561.0 25.6 %collective-permute-start.43 = (bf16[4,256,128]{2,1,0:T(8,128)(2,1)S(1)}, bf16[4,256,128]{2,1,0:T(8,128)(2,1)S(1)}, u32[]{:S(2)}, u32[]{:S(2)}) collective-permute-start(bf16[4,256,128]{2,1,0:T(8,128)(2,1)S(1)} %get-tuple-element.184), channel_id=1, source_target_pairs={{0,2},{2,0},{4,6},{6,4},{1,3},{3,1},{5,7},{7,5},{8,10},{10,8},{12,... | collective-permute-start | bytes 786440 | tf_op jit(solution)/shard_map/ppermute | solution.py:144
  612.2 28.0 %all-to-all-start.11 = ((f32[32,1,2184]{2,1,0:T(1,128)}), f32[32,1,2184]{2,1,0:T(1,128)S(1)}, u32[]{:S(2)}, u32[]{:S(2)}) async-start(f32[32,1,2184]{2,1,0:T(1,128)} %copy.82), calls=%async_computation.14 | async-start | bytes 589824 | tf_op jit(solution)/shard_map/all_to_all | solution.py:56
  627.4 43.5 %collective-permute-start.38 = (bf16[128,2048]{1,0:T(8,128)(2,1)}, bf16[128,2048]{1,0:T(8,128)(2,1)S(1)}, u32[]{:S(2)}, u32[]{:S(2)}) collective-permute-start(bf16[128,2048]{1,0:T(8,128)(2,1)} %get-tuple-element.114), channel_id=1, source_target_pairs={{0,2},{2,0},{4,6},{6,4},{1,3},{3,1},{5,7},{7,5},{8,10},{10,8},{12,... | collective-permute-start | bytes 1572872 | tf_op jit(solution)/shard_map/ppermute | solution.py:144
  638.4 32.5 %collective-permute-start.47 = (bf16[128,2048]{1,0:T(8,128)(2,1)}, bf16[128,2048]{1,0:T(8,128)(2,1)S(1)}, u32[]{:S(2)}, u32[]{:S(2)}) collective-permute-start(bf16[128,2048]{1,0:T(8,128)(2,1)} %get-tuple-element.130), channel_id=1, source_target_pairs={{0,16},{1,17},{8,24},{9,25},{16,0},{17,1},{24,8},{25,9},{2,18},{3,... | collective-permute-start | bytes 1572872 | tf_op jit(solution)/shard_map/ppermute | solution.py:92
  638.9 32.0 %collective-permute-start.48 = (bf16[128,2048]{1,0:T(8,128)(2,1)}, bf16[128,2048]{1,0:T(8,128)(2,1)S(1)}, u32[]{:S(2)}, u32[]{:S(2)}) collective-permute-start(bf16[128,2048]{1,0:T(8,128)(2,1)} %get-tuple-element.131), channel_id=1, source_target_pairs={{0,1},{1,0},{8,9},{9,8},{16,17},{17,16},{24,25},{25,24},{2,3},{3,2... | collective-permute-start | bytes 1572872 | tf_op jit(solution)/shard_map/ppermute | solution.py:92
  (118 other events, 856.6 us)
Sparse Core Ops, SparseCore 0:
  9.6 52.3 all-gather.5
  76.7 53.9 all-gather.7
  143.2 44.4 all-gather.9
  484.6 41.8 reduce-scatter.3
  528.8 49.9 reduce-scatter.5
  594.5 69.4 reduce-scatter.7

commit v4 on v3

--- a/solution.py
+++ b/solution.py
@@ -290,14 +290,18 @@
     return values * cosine + pltpu.roll(values, HEAD_DIM // 2, 1) * sine
 
 
-def key_value_kernel(info, units, packet, cosine, sine, key_proj, out, weights, gain):
+def key_value_kernel(info, units, packet, cosine, sine, key_proj, out, weights, gain, query_gain):
     depth = units.shape[1] // packet.shape[0]
     total = jnp.zeros(gain.shape, F32)
+    query_total = jnp.zeros(gain.shape, F32)
     for index in range(packet.shape[0]):
         weights[index * depth : (index + 1) * depth] = packet[index, :depth]
         row = depth + KEY_GAIN_ROW
         total = total + packet[index, row : row + 1, :].astype(F32)
+        row = depth + QUERY_GAIN_ROW
+        query_total = query_total + packet[index, row : row + 1, :].astype(F32)
     gain[...] = total
+    query_gain[...] = query_total
     projected = dot(units[...], weights[...])
     key_proj[...] = projected
     scale = lax.rsqrt(jnp.mean(projected * projected, axis=-1, keepdims=True) + EPS)
@@ -333,78 +337,104 @@
     return scale, unit, turn(unit * gain, cosine, sine)
 
 
+def windows_of(length, rows):
+    count = length // rows
+    return [max(count * part // 4, 1) * rows for part in (1, 2, 3, 4)]
+
+
+def in_window(info, qdoc_ref, kdoc_ref, rows, work):
+    length = kdoc_ref.shape[2]
+    earlier = jnp.sum((kdoc_ref[0] < qdoc_ref[0, 0:1, 0:1]).astype(jnp.int32))
+    blocks = info[0] + 1 - lax.div(earlier, rows)
+    smaller = 0
+    for size in windows_of(length, rows):
+        start = pl.multiple_of(jnp.maximum(info[0] + 1 - size // rows, 0) * rows, rows)
+        fits = (blocks > smaller) & (blocks <= size // rows)
+        pl.when(fits)(functools.partial(work, start, size))
+        smaller = size // rows
+
+
+def head_columns(head):
+    return slice(head * HEAD_DIM, (head + 1) * HEAD_DIM)
+
+
 def forward_kernel(info, q_ref, qdoc_ref, kdoc_ref, qpos_ref, cos_ref, sin_ref, gain_ref, *refs):
     *sources, out_ref, total_ref, bias, keys, values = refs
-
-    @pl.when(pl.program_id(1) == 0)
-    def _():
-        attention_setup(info, sources, qdoc_ref, kdoc_ref, qpos_ref, bias, keys, values)
-
-    _, _, turned = rotated(q_ref[...], gain_ref[...], cos_ref[...], sin_ref[...])
-    scores = dot_nt(turned.astype(BF16), keys[...]) * (SCALE * LOG2E) + bias[...]
-    highest = jnp.max(scores, axis=-1, keepdims=True)
-    exponent = jnp.exp2(scores - highest)
-    total = jnp.sum(exponent, axis=-1, keepdims=True)
-    probs = (exponent * (1.0 / total)).astype(BF16)
-    out_ref[...] = dot(probs, values[...]).astype(BF16)
-    total_ref[0, 0] = highest + jnp.log2(total)
+    attention_setup(info, sources, qdoc_ref, kdoc_ref, qpos_ref, bias, keys, values)
+    heads = q_ref.shape[1] // HEAD_DIM
+
+    def work(start, size):
+        part = pl.ds(start, size)
+        for head in range(heads):
+            at = head_columns(head)
+            _, _, turned = rotated(q_ref[:, at], gain_ref[...], cos_ref[...], sin_ref[...])
+            scores = dot_nt(turned.astype(BF16), keys[part, :]) * (SCALE * LOG2E) + bias[:, part]
+            highest = jnp.max(scores, axis=-1, keepdims=True)
+            exponent = jnp.exp2(scores - highest)
+            total = jnp.sum(exponent, axis=-1, keepdims=True)
+            probs = (exponent * (1.0 / total)).astype(BF16)
+            out_ref[:, at] = dot(probs, values[part, :]).astype(BF16)
+            total_ref[0, head] = highest + jnp.log2(total)
+
+    in_window(info, qdoc_ref, kdoc_ref, bias.shape[0], work)
 
 
 def backward_kernel(info, q_ref, qdoc_ref, kdoc_ref, qpos_ref, cos_ref, sin_ref, gain_ref, *refs):
     *sources, total_ref, grad_ref, dq_ref, kept_ref, sent_ref, dgain_ref, bias, key_rows, value_rows, dk_sum, dv_sum = refs
-    seq, head = pl.program_id(0), pl.program_id(1)
-
-    @pl.when(head == 0)
-    def _():
-        attention_setup(info, sources, qdoc_ref, kdoc_ref, qpos_ref, bias, key_rows, value_rows)
-        dk_sum[...] = jnp.zeros_like(dk_sum)
-        dv_sum[...] = jnp.zeros_like(dv_sum)
-
-    @pl.when((head == 0) & (seq == 0))
+    seq = pl.program_id(0)
+    attention_setup(info, sources, qdoc_ref, kdoc_ref, qpos_ref, bias, key_rows, value_rows)
+    dk_sum[...] = jnp.zeros_like(dk_sum)
+    dv_sum[...] = jnp.zeros_like(dv_sum)
+
+    @pl.when(seq == 0)
     def _():
         dgain_ref[...] = jnp.zeros_like(dgain_ref)
 
     gain, cosine, sine = gain_ref[...], cos_ref[...], sin_ref[...]
-    scale, unit, turned = rotated(q_ref[...], gain, cosine, sine)
-    turned = turned.astype(BF16)
-    keys, values = key_rows[...], value_rows[...]
-    scores = dot_nt(turned, keys) * (SCALE * LOG2E) + bias[...]
-    probs = jnp.exp2(scores - total_ref[0, 0])
-    grad = grad_ref[...]
-    grad_probs = dot_nt(grad, values)
-    delta = jnp.sum(probs * grad_probs, axis=-1, keepdims=True)
-    grad_scores = (probs * (grad_probs - delta)).astype(BF16)
-    dv_sum[...] += dot_tn(probs.astype(BF16), grad)
-    dk_sum[...] += dot_tn(grad_scores, turned)
-    grad_turned = dot(grad_scores, keys) * SCALE
-    grad_gained = turn(grad_turned, cosine, -sine)
-    dgain_ref[...] += jnp.sum(grad_gained * unit, axis=0, keepdims=True)
-    weighted = grad_gained * gain
-    dq_ref[...] = (
-        scale * (weighted - unit * jnp.mean(weighted * unit, axis=-1, keepdims=True))
-    ).astype(BF16)
-
-    @pl.when(head == pl.num_programs(1) - 1)
-    def _():
-        shape = kept_ref.shape[:1] + kept_ref.shape[2:]
-        dk, dv = dk_sum[...] * SCALE, dv_sum[...]
-        kept_ref[:, 0] = jnp.where(info[3] == 0, dk, dv).astype(BF16).reshape(shape)
-        sent_ref[:, 0] = jnp.where(info[3] == 0, dv, dk).astype(BF16).reshape(shape)
-
-
-def attention_specs(rows, length, sources, first=0):
+
+    def work(start, size):
+        part = pl.ds(start, size)
+        keys, values = key_rows[part, :], value_rows[part, :]
+        for head in range(q_ref.shape[1] // HEAD_DIM):
+            at = head_columns(head)
+            scale, unit, turned = rotated(q_ref[:, at], gain, cosine, sine)
+            turned = turned.astype(BF16)
+            scores = dot_nt(turned, keys) * (SCALE * LOG2E) + bias[:, part]
+            probs = jnp.exp2(scores - total_ref[0, head])
+            grad = grad_ref[:, at]
+            grad_probs = dot_nt(grad, values)
+            delta = jnp.sum(probs * grad_probs, axis=-1, keepdims=True)
+            grad_scores = (probs * (grad_probs - delta)).astype(BF16)
+            dv_sum[part, :] += dot_tn(probs.astype(BF16), grad)
+            dk_sum[part, :] += dot_tn(grad_scores, turned)
+            grad_turned = dot(grad_scores, keys) * SCALE
+            grad_gained = turn(grad_turned, cosine, -sine)
+            dgain_ref[...] += jnp.sum(grad_gained * unit, axis=0, keepdims=True)
+            weighted = grad_gained * gain
+            dq_ref[:, at] = (
+                scale * (weighted - unit * jnp.mean(weighted * unit, axis=-1, keepdims=True))
+            ).astype(BF16)
+
+    in_window(info, qdoc_ref, kdoc_ref, bias.shape[0], work)
+    shape = kept_ref.shape[:1] + kept_ref.shape[2:]
+    dk, dv = dk_sum[...] * SCALE, dv_sum[...]
+    kept_ref[:, 0] = jnp.where(info[3] == 0, dk, dv).astype(BF16).reshape(shape)
+    sent_ref[:, 0] = jnp.where(info[3] == 0, dv, dk).astype(BF16).reshape(shape)
+
+
+def attention_specs(rows, length, width, sources, first=0):
     specs = [
         pl.BlockSpec(memory_space=pltpu.SMEM),
-        pl.BlockSpec((rows, HEAD_DIM), lambda s, h: (first + s, h)),
-        pl.BlockSpec((1, rows, 1), lambda s, h: (first + s, 0, 0)),
-        pl.BlockSpec((1, 1, length), lambda s, h: (first + s, 0, 0)),
-        pl.BlockSpec((rows, 1), lambda s, h: (0, 0)),
-        pl.BlockSpec((rows, HEAD_DIM), lambda s, h: (0, 0)),
-        pl.BlockSpec((rows, HEAD_DIM), lambda s, h: (0, 0)),
-        pl.BlockSpec((1, HEAD_DIM), lambda s, h: (0, 0)),
+        pl.BlockSpec((rows, width), lambda s: (first + s, 0)),
+        pl.BlockSpec((1, rows, 1), lambda s: (first + s, 0, 0)),
+        pl.BlockSpec((1, 1, length), lambda s: (first + s, 0, 0)),
+        pl.BlockSpec((rows, 1), lambda s: (0, 0)),
+        pl.BlockSpec((rows, HEAD_DIM), lambda s: (0, 0)),
+        pl.BlockSpec((rows, HEAD_DIM), lambda s: (0, 0)),
+        pl.BlockSpec((1, HEAD_DIM), lambda s: (0, 0)),
     ]
     return specs + [
-        pl.BlockSpec((1, rows, HEAD_DIM), lambda s, h: (first + s, 0, 0)) for _ in sources
+        pl.BlockSpec((1, rows, HEAD_DIM), lambda s: (first + s, 0, 0)) for _ in sources
     ]
 
 
@@ -412,11 +442,11 @@
     pairs = sequences * heads * rows * length
     return pl.pallas_call(
         forward_kernel,
-        grid=(sequences, heads),
-        in_specs=attention_specs(rows, length, sources),
+        grid=(sequences,),
+        in_specs=attention_specs(rows, length, heads * HEAD_DIM, sources),
         out_specs=[
-            pl.BlockSpec((rows, HEAD_DIM), lambda s, h: (s, h)),
-            pl.BlockSpec((1, 1, rows, 1), lambda s, h: (s, h, 0, 0)),
+            pl.BlockSpec((rows, heads * HEAD_DIM), lambda s: (s, 0)),
+            pl.BlockSpec((1, heads, rows, 1), lambda s: (s, 0, 0, 0)),
         ],
         out_shape=[
             shape_of((sequences * rows, heads * HEAD_DIM), BF16),
@@ -439,7 +469,7 @@
 ):
     pairs = sequences * heads * rows * length
     parts = length // rows
-    key_value_spec = pl.BlockSpec((parts, 1, rows, HEAD_DIM), lambda s, h: (0, s, 0, 0))
+    key_value_spec = pl.BlockSpec((parts, 1, rows, HEAD_DIM), lambda s: (0, s, 0, 0))
     key_value_shape = shape_of((parts, sequences, rows, HEAD_DIM), BF16)
     count = len(operands) + len(sources) + 2
 
@@ -448,18 +478,18 @@
 
     return pl.pallas_call(
         kernel,
-        grid=(sequences, heads),
-        in_specs=attention_specs(rows, length, sources, first)
+        grid=(sequences,),
+        in_specs=attention_specs(rows, length, heads * HEAD_DIM, sources, first)
         + [
-            pl.BlockSpec((1, 1, rows, 1), lambda s, h: (first + s, h, 0, 0)),
-            pl.BlockSpec((rows, HEAD_DIM), lambda s, h: (first + s, h)),
+            pl.BlockSpec((1, heads, rows, 1), lambda s: (first + s, 0, 0, 0)),
+            pl.BlockSpec((rows, heads * HEAD_DIM), lambda s: (first + s, 0)),
         ]
         + [pl.BlockSpec(memory_space=pl.ANY)] * len(tokens),
         out_specs=[
-            pl.BlockSpec((rows, HEAD_DIM), lambda s, h: (s, h)),
+            pl.BlockSpec((rows, heads * HEAD_DIM), lambda s: (s, 0)),
             key_value_spec,
             key_value_spec,
-            pl.BlockSpec((1, HEAD_DIM), lambda s, h: (0, 0)),
+            pl.BlockSpec((1, HEAD_DIM), lambda s: (0, 0)),
         ],
         out_shape=[
             shape_of((sequences * rows, heads * HEAD_DIM), BF16),
@@ -855,7 +885,6 @@
     packet = packet.astype(F32)
     documents = packet[:, DOCUMENT_ROW].reshape(dp_size, length).astype(jnp.int32)
     second_gain = packet[:, MOE_GAIN_ROW, :depth].reshape(1, width)
-    query_norm_gain = jnp.sum(packet[:, QUERY_GAIN_ROW], axis=0, keepdims=True)
     meta = packet.reshape(dp_size, seq_size, rep_size, PACKET_ROWS, LANES)
     meta = pick(pick(meta, dp_at), rep_at, 1).astype(jnp.int32)
     choice_ids, priority_rank = meta[:, :TOPK], meta[:, PRIORITY_ROW]
@@ -886,12 +915,13 @@
     angles = positions.astype(F32)[:, None] * jnp.concatenate([frequency, frequency])[None, :]
     sign = jnp.where(jnp.arange(HEAD_DIM) < HEAD_DIM // 2, -1.0, 1.0)
     cosine, sine = jnp.cos(angles), jnp.sin(angles) * sign[None, :]
-    key_proj, key_value_rows, key_value_weights, key_norm_gain = run(
+    key_proj, key_value_rows, key_value_weights, key_norm_gain, query_norm_gain = run(
         key_value_kernel,
         [
             shape_of((plane_rows, HEAD_DIM), F32),
             shape_of((dp_size, rows, HEAD_DIM), BF16),
             shape_of((width, HEAD_DIM), BF16),
+            shape_of((1, HEAD_DIM), F32),
             shape_of((1, HEAD_DIM), F32),
         ],
         info,
@@ -1108,7 +1138,7 @@
         info,
         table,
         results_far,
-        tokens=branch_blocks[5:7],
+        tokens=(grad_middle,),
         flops=2 * own_rows * len(groups[1]) * plane_slots * width,
     )[0]
     grad_branch, grad_attended = run(
@@ -1137,7 +1167,7 @@
         heads,
         rows,
         length,
-        (grad_out, far_sum),
+        (grad_out,),
     )
     query_grads, kept_grads, sent_grads, gain_grads = zip(first_call, second_call)
     if whole_heads:
@@ -1177,7 +1207,7 @@
     grad_query_gain = gain_grads[0] + gain_grads[1]
     kept_grads = [
         kept.astype(F32) + plane_move(sent, SIDE).astype(F32)
-        for kept, sent in zip(kept_grads, (sent_grads[0], after(sent_grads[1], results_near)))
+        for kept, sent in zip(kept_grads, (sent_grads[0], after(sent_grads[1], results_near, far_sum)))
     ]
     grad_key_value = jnp.concatenate(kept_grads, axis=1).astype(BF16)
     key_value_terms = line_reduce(grad_key_value, seq_at, seq_size)

time: 700 us -> 687 us (0.981)
  Pallas kernels: 243 us -> 225 us
  waiting for transfers between devices: 230 us -> 243 us
    pallas_call x3, Pallas kernels: 52.9 us -> 35 us  [the longest x2 21.5 us: attention_backward(): pl.pallas_call(kernel, grid=(sequences,), in_specs=attention_specs(rows,...]
    all_to_all x11, waiting for transfers between devices: 28.2 us -> 35.9 us  [swap(): return lax.all_to_all(blocks, axes, split_axis=0, concat_axis=0, tiled=True)]
    unnamed x157 -> x153, local copies, waits for them, and re-layouts: 31.9 us -> 30.4 us
  transfers between devices with their start and end apart: 66 -> 66, of which waited for: 37 -> 36; matrix products, arithmetic and copies ran while one was open for 7% -> 7% of each run, Pallas kernels for 29% -> 26%
where the time goes in v4:
time: 687 us; the launch traced here: 677 us
  waiting for transfers between devices  243 us (35%)
  Pallas kernels  225 us (33%)
  starting transfers between devices  88.5 us (13%)
  local copies, waits for them, and re-layouts  44.9 us (7%)
  blocking collectives  30.2 us (4%)
  other arithmetic  17 us (2%)
  between operations  15.3 us (2%)
  matrix products  13.3 us (2%)
    pallas_call x36, Pallas kernels, run(): pl.pallas_call(body, in_specs=in_specs, out_specs=[pl.BlockSpec(memory_sp...  166 us
    ppermute x15, waiting for transfers between devices, line_move(): lax.ppermute(block, 'seq', [(place, place ^ bits) for place in range(4)])  102 us
    ppermute x34, waiting for transfers between devices, plane_move(): lax.ppermute(block, PLANE, [(index, index ^ bits) for index in range(8)])  80.3 us
    all_to_all x11, starting transfers between devices, swap(): return lax.all_to_all(blocks, axes, split_axis=0, concat_axis=0, tiled=True)  42.7 us
    all_to_all x11, waiting for transfers between devices, swap(): return lax.all_to_all(blocks, axes, split_axis=0, concat_axis=0, tiled=True)  35.9 us
    ppermute x34, starting transfers between devices, plane_move(): lax.ppermute(block, PLANE, [(index, index ^ bits) for index in range(8)])  31.5 us
    unnamed x153, local copies, waits for them, and re-layouts  30.4 us
    all_to_all x1, blocking collectives, swap(): return lax.all_to_all(blocks, axes, split_axis=0, concat_axis=0, tiled=True)  30.2 us
  transfers between devices with their start and end apart: 66, of which 36 were waited for; matrix products, arithmetic and copies ran while one was open for 7% of the time, Pallas kernels for 26%

profile of v4, /device:TPU:0, one launch (start us, length us, event | category | flops | bytes accessed | tf_op | source)
XLA Modules:
  0.0 677.1 jit_solution(2174376367474767225)
XLA Ops:
  46.3 30.2 %all_to_all.64.refs_1_.refs_2_ = bf16[32,96,128]{2,1,0:T(8,128)(2,1)} all-to-all(bf16[32,96,128]{2,1,0:T(8,128)(2,1)} %shard_map.257), channel_id=1, replica_groups=mesh['dp'=4,'seq'=4,'rep'=2] {'dp','seq','rep'}, dimensions={0} | all-to-all | bytes 1572864 | tf_op jit(solution)/shard_map/all_to_all | solution.py:56
  106.5 24.0 %collective-permute-done.10.refs_2_.refs_4_.refs_10_ = bf16[4,256,128]{2,1,0:T(8,128)(2,1)S(1)} collective-permute-done((bf16[4,256,128]{2,1,0:T(8,128)(2,1)S(1)}, bf16[4,256,128]{2,1,0:T(8,128)(2,1)S(1)}, u32[]{:S(2)}, u32[]{:S(2)}) %collective-permute-start.10) | collective-permute-done | bytes 262176 | tf_op jit(solution)/shard_map/ppermute | solution.py:144
  132.0 8.5 %collective-permute-done.11.refs_3_.refs_2_.refs_11_ = bf16[4,256,128]{2,1,0:T(8,128)(2,1)S(1)} collective-permute-done((bf16[4,256,128]{2,1,0:T(8,128)(2,1)}, bf16[4,256,128]{2,1,0:T(8,128)(2,1)S(1)}, u32[]{:S(2)}, u32[]{:S(2)}) %collective-permute-start.11) | collective-permute-done | bytes 262176 | tf_op jit(solution)/shard_map/ppermute | solution.py:144
  151.3 6.7 shard_map.260
  177.1 13.4 %shard_map.263 = (bf16[1024,512]{1,0:T(8,128)(2,1)}, f32[4,4,256,1]{3,2,1,0:T(8,128)}) custom-call(s32[8]{0:T(128)} %compare_select_fusion.4.refs_0_.info, f32[1024,512]{1,0:T(8,128)} %get-tuple-element.83.q_ref.refs_2_.refs_1_, s32[4,256,1]{2,1,0:T(8,128)} %copy.72.qdoc_ref.refs_2_, s32[4,1,1024]{2,1,0:T(1,128)} %bitcast.86, ...), custom_call_target="tpu_custom_call" | custom-call | flops 1000 | bytes 1000 | tf_op jit(solution)/shard_map/pallas_call | solution.py:443
  190.6 9.5 %all-to-all-done.3.refs_3_.refs_1_ = bf16[8,64,2176]{2,1,0:T(8,128)(2,1)S(1)} async-done(((bf16[8,64,2176]{2,1,0:T(8,128)(2,1)}), bf16[8,64,2176]{2,1,0:T(8,128)(2,1)S(1)}, u32[]{:S(2)}, u32[]{:S(2)}) %all-to-all-start.3) | async-done | bytes 2228256 | tf_op jit(solution)/shard_map/all_to_all | solution.py:56
  218.1 6.9 %collective-permute-done.17.refs_3_ = bf16[64,2048]{1,0:T(8,128)(2,1)S(1)} collective-permute-done((bf16[64,2048]{1,0:T(8,128)(2,1)}, bf16[64,2048]{1,0:T(8,128)(2,1)S(1)}, u32[]{:S(2)}, u32[]{:S(2)}) %collective-permute-start.17) | collective-permute-done | bytes 262176 | tf_op jit(solution)/shard_map/ppermute | solution.py:92
  233.0 9.5 %collective-permute-done.19.refs_2_ = bf16[128,2048]{1,0:T(8,128)(2,1)S(1)} collective-permute-done((bf16[128,2048]{1,0:T(8,128)(2,1)}, bf16[128,2048]{1,0:T(8,128)(2,1)S(1)}, u32[]{:S(2)}, u32[]{:S(2)}) %collective-permute-start.19) | collective-permute-done | bytes 524320 | tf_op jit(solution)/shard_map/ppermute | solution.py:92
  249.9 13.1 %collective-permute-done.22.refs_4_.refs_2_ = bf16[64,2048]{1,0:T(8,128)(2,1)S(1)} collective-permute-done((bf16[64,2048]{1,0:T(8,128)(2,1)S(1)}, bf16[64,2048]{1,0:T(8,128)(2,1)S(1)}, u32[]{:S(2)}, u32[]{:S(2)}) %collective-permute-start.22) | collective-permute-done | bytes 262176 | tf_op jit(solution)/shard_map/ppermute | solution.py:144
  275.0 12.9 %collective-permute-done.23.refs_3_ = bf16[64,2048]{1,0:T(8,128)(2,1)S(1)} collective-permute-done((bf16[64,2048]{1,0:T(8,128)(2,1)S(1)}, bf16[64,2048]{1,0:T(8,128)(2,1)S(1)}, u32[]{:S(2)}, u32[]{:S(2)}) %collective-permute-start.23) | collective-permute-done | bytes 262176 | tf_op jit(solution)/shard_map/ppermute | solution.py:144
  289.9 7.2 %collective-permute-done.25.refs_5_ = bf16[64,2048]{1,0:T(8,128)(2,1)S(1)} collective-permute-done((bf16[64,2048]{1,0:T(8,128)(2,1)S(1)}, bf16[64,2048]{1,0:T(8,128)(2,1)S(1)}, u32[]{:S(2)}, u32[]{:S(2)}) %collective-permute-start.25) | collective-permute-done | bytes 262176 | tf_op jit(solution)/shard_map/ppermute | solution.py:144
  318.1 19.1 %all-to-all-done.5.refs_1_ = bf16[8,64,2048]{2,1,0:T(8,128)(2,1)S(1)} async-done(((bf16[8,64,2048]{2,1,0:T(8,128)(2,1)}), bf16[8,64,2048]{2,1,0:T(8,128)(2,1)S(1)}, u32[]{:S(2)}, u32[]{:S(2)}) %all-to-all-start.5) | async-done | bytes 2097184 | tf_op jit(solution)/shard_map/all_to_all | solution.py:56
  338.6 14.7 %shard_map.277 = (bf16[512,1536]{1,0:T(8,128)(2,1)}, bf16[512,768]{1,0:T(8,128)(2,1)}, bf16[8,64,2176]{2,1,0:T(8,128)(2,1)}) custom-call(s32[8]{0:T(128)} %compare_select_fusion.4.refs_0_.info, bf16[8,64,2048]{2,1,0:T(8,128)(2,1)} %copy-done.11, f32[512,768]{1,0:T(8,128)} %shard_map.276.refs_2_, bf16[8,64,2176]{2,1,0:T(8,128)(2,1)} %copy-done.4, ...), custom_call_target="tpu_custom_call" | custom-call | flops 6442450944 | bytes 16908288 | tf_op jit(solution)/shard_map/pallas_call | solution.py:79
  362.7 14.8 %shard_map.278 = (bf16[512,1536]{1,0:T(8,128)(2,1)}, bf16[512,768]{1,0:T(8,128)(2,1)}, bf16[8,64,2176]{2,1,0:T(8,128)(2,1)}) custom-call(s32[8]{0:T(128)} %compare_select_fusion.4.refs_0_.info, bf16[8,64,2048]{2,1,0:T(8,128)(2,1)} %copy-done.6, f32[512,768]{1,0:T(8,128)} %shard_map.274.refs_2_, bf16[8,64,2176]{2,1,0:T(8,128)(2,1)} %copy-done.3, ...), custom_call_target="tpu_custom_call" | custom-call | flops 6442450944 | bytes 16908288 | tf_op jit(solution)/shard_map/pallas_call | solution.py:79
  377.4 6.8 all-to-all-done.6.refs_2_
  392.5 7.8 %shard_map.280.refs_3_.refs_13_ = f32[1,768,2048]{2,1,0:T(8,128)} custom-call(bf16[512,768]{1,0:T(8,128)(2,1)} %get-tuple-element.99.refs_0_.refs_2_, bf16[512,768]{1,0:T(8,128)(2,1)} %get-tuple-element.102.refs_1_.refs_2_, bf16[8,64,2176]{2,1,0:T(8,128)(2,1)} %copy-done.3, bf16[8,64,2176]{2,1,0:T(8,128)(2,1)} %copy-done.4, ...), custom_call_target="tpu_custom_call" | custom-call | flops 1000 | bytes 1000 | tf_op jit(solution)/shard_map/pallas_call | solution.py:747
  400.3 7.1 %collective-permute-done.26.refs_2_ = bf16[128,2176]{1,0:T(8,128)(2,1)S(1)} collective-permute-done((bf16[128,2176]{1,0:T(8,128)(2,1)}, bf16[128,2176]{1,0:T(8,128)(2,1)S(1)}, u32[]{:S(2)}, u32[]{:S(2)}) %collective-permute-start.26) | collective-permute-done | bytes 557088 | tf_op jit(solution)/shard_map/ppermute | solution.py:144
  434.7 11.4 %shard_map.285.refs_11_ = f32[1,2048,1536]{2,1,0:T(8,128)} custom-call(bf16[512,2048]{1,0:T(8,128)(2,1)} %bitcast.59, bf16[512,2048]{1,0:T(8,128)(2,1)} %bitcast.60, bf16[512,1536]{1,0:T(8,128)(2,1)} %get-tuple-element.107.refs_2_, bf16[512,1536]{1,0:T(8,128)(2,1)} %get-tuple-element.108.refs_3_, bf16[128,2176]{1,0:T(8,128)(2,1)} %get-tuple-element.105.refs_4_.refs_8_), custom_call_target="tpu_custom_call" | custom-call | flops 1000 | bytes 1000 | tf_op jit(solution)/shard_map/pallas_call | solution.py:722
  466.3 10.0 %collective-permute-done.32.refs_6_ = bf16[128,2048]{1,0:T(8,128)(2,1)S(1)} collective-permute-done((bf16[128,2048]{1,0:T(8,128)(2,1)S(1)}, bf16[128,2048]{1,0:T(8,128)(2,1)S(1)}, u32[]{:S(2)}, u32[]{:S(2)}) %collective-permute-start.32) | collective-permute-done | bytes 524320 | tf_op jit(solution)/shard_map/ppermute | solution.py:92
  497.5 10.8 %shard_map.291 = (bf16[512,512]{1,0:T(8,128)(2,1)}, bf16[4,2,256,128]{3,2,1,0:T(8,128)(2,1)}, bf16[4,2,256,128]{3,2,1,0:T(8,128)(2,1)}, f32[1,128]{1,0:T(1,128)}) custom-call(s32[8]{0:T(128)} %compare_select_fusion.4.refs_0_.info, f32[1024,512]{1,0:T(8,128)} %get-tuple-element.83.q_ref.refs_2_.refs_1_, s32[4,256,1]{2,1,0:T(8,128)} %copy.72.qdoc_ref.refs_2_, ...), custom_call_target="tpu_custom_call" | custom-call | flops 1000 | bytes 1000 | tf_op jit(solution)/shard_map/pallas_call | solution.py:479
  516.5 10.7 %shard_map.293 = (bf16[512,512]{1,0:T(8,128)(2,1)}, bf16[4,2,256,128]{3,2,1,0:T(8,128)(2,1)}, bf16[4,2,256,128]{3,2,1,0:T(8,128)(2,1)}, f32[1,128]{1,0:T(1,128)}) custom-call(s32[8]{0:T(128)} %compare_select_fusion.4.refs_0_.info, f32[1024,512]{1,0:T(8,128)} %get-tuple-element.83.q_ref.refs_2_.refs_1_, s32[4,256,1]{2,1,0:T(8,128)} %copy.72.qdoc_ref.refs_2_, ...), custom_call_target="tpu_custom_call" | custom-call | flops 1000 | bytes 1000 | tf_op jit(solution)/shard_map/pallas_call | solution.py:479
  534.9 10.6 %collective-permute-done.40 = bf16[4,2,256,128]{3,2,1,0:T(8,128)(2,1)S(1)} collective-permute-done((bf16[4,2,256,128]{3,2,1,0:T(8,128)(2,1)}, bf16[4,2,256,128]{3,2,1,0:T(8,128)(2,1)S(1)}, u32[]{:S(2)}, u32[]{:S(2)}) %collective-permute-start.40) | collective-permute-done | bytes 524320 | tf_op jit(solution)/shard_map/ppermute | solution.py:92
  550.8 11.0 %collective-permute-done.41 = bf16[4,256,128]{2,1,0:T(8,128)(2,1)S(1)} collective-permute-done((bf16[4,256,128]{2,1,0:T(8,128)(2,1)}, bf16[4,256,128]{2,1,0:T(8,128)(2,1)S(1)}, u32[]{:S(2)}, u32[]{:S(2)}) %collective-permute-start.41) | collective-permute-done | bytes 262176 | tf_op jit(solution)/shard_map/ppermute | solution.py:144
  627.8 23.9 %reduce-scatter.8.cloned.1.call-done = bf16[1,4,128,640]{3,2,1,0:T(8,128)(2,1)} async-done(((bf16[4,4,128,640]{3,2,1,0:T(8,128)(2,1)}), bf16[1,4,128,640]{3,2,1,0:T(8,128)(2,1)}) %reduce-scatter.8.cloned.1.call-update) | async-done | bytes 655376 | tf_op jit(solution)/shard_map/reduce_scatter | solution.py:1249
  (385 shorter events, 361.3 us)
Async XLA Ops:
  7.2 69.3 %all-gather.6.cloned.1.call-start = ((), (), s32[]{:S(2)}) async-start(), calls=%async_computation.15 | async-start | bytes 2621440 | tf_op jit(solution)/shard_map/all_gather | solution.py:858
  29.0 122.3 %all-gather.8.cloned.1.call-start = ((), (), s32[]{:S(2)}) async-start(), calls=%async_computation.19 | async-start | bytes 2621440 | tf_op jit(solution)/shard_map/all_gather | solution.py:883
  101.5 66.1 %all-to-all-start.2 = ((bf16[8,64,2176]{2,1,0:T(8,128)(2,1)}), bf16[8,64,2176]{2,1,0:T(8,128)(2,1)S(1)}, u32[]{:S(2)}, u32[]{:S(2)}) async-start(bf16[8,64,2176]{2,1,0:T(8,128)(2,1)} %shard_map.266), calls=%async_computation.2 | async-start | bytes 4456448 | tf_op jit(solution)/shard_map/all_to_all | solution.py:56
  105.3 85.3 %all-gather.10.cloned.1.call-start = ((), (), s32[]{:S(2)}) async-start(), calls=%async_computation.20 | async-start | bytes 2621440 | tf_op jit(solution)/shard_map/all_gather | solution.py:951
  105.3 25.2 %collective-permute-start.10 = (bf16[4,256,128]{2,1,0:T(8,128)(2,1)S(1)}, bf16[4,256,128]{2,1,0:T(8,128)(2,1)S(1)}, u32[]{:S(2)}, u32[]{:S(2)}) collective-permute-start(bf16[4,256,128]{2,1,0:T(8,128)(2,1)S(1)} %copy-done.16), channel_id=1, source_target_pairs={{0,4},{2,6},{4,0},{6,2},{1,5},{3,7},{5,1},{7,3},{8,12},{10,14},{12... | collective-permute-start | bytes 786440 | tf_op jit(solution)/shard_map/ppermute | solution.py:144
  105.4 25.9 %collective-permute-start.9 = (bf16[4,256,128]{2,1,0:T(8,128)(2,1)S(1)}, bf16[4,256,128]{2,1,0:T(8,128)(2,1)S(1)}, u32[]{:S(2)}, u32[]{:S(2)}) collective-permute-start(bf16[4,256,128]{2,1,0:T(8,128)(2,1)S(1)} %copy-done.16), channel_id=1, source_target_pairs={{0,2},{2,0},{4,6},{6,4},{1,3},{3,1},{5,7},{7,5},{8,10},{10,8},{12,... | collective-permute-start | bytes 786440 | tf_op jit(solution)/shard_map/ppermute | solution.py:144
  146.7 20.9 %collective-permute-start.15 = (bf16[4,256,128]{2,1,0:T(8,128)(2,1)}, bf16[4,256,128]{2,1,0:T(8,128)(2,1)}, u32[]{:S(2)}, u32[]{:S(2)}) collective-permute-start(bf16[4,256,128]{2,1,0:T(8,128)(2,1)} %copy-done.18), channel_id=1, source_target_pairs={{0,1},{1,0},{8,9},{9,8},{16,17},{17,16},{24,25},{25,24},{2,3},{3,2... | collective-permute-start | bytes 786440 | tf_op jit(solution)/shard_map/ppermute | solution.py:92
  169.0 31.1 %all-to-all-start.3 = ((bf16[8,64,2176]{2,1,0:T(8,128)(2,1)}), bf16[8,64,2176]{2,1,0:T(8,128)(2,1)S(1)}, u32[]{:S(2)}, u32[]{:S(2)}) async-start(bf16[8,64,2176]{2,1,0:T(8,128)(2,1)} %shard_map.267), calls=%async_computation.3 | async-start | bytes 4456448 | tf_op jit(solution)/shard_map/all_to_all | solution.py:56
  269.0 32.6 %all-to-all-start.4 = ((bf16[8,64,2048]{2,1,0:T(8,128)(2,1)}), bf16[8,64,2048]{2,1,0:T(8,128)(2,1)S(1)}, u32[]{:S(2)}, u32[]{:S(2)}) async-start(bf16[8,64,2048]{2,1,0:T(8,128)(2,1)} %shard_map.273), calls=%async_computation.4 | async-start | bytes 4194304 | tf_op jit(solution)/shard_map/all_to_all | solution.py:56
  307.0 30.2 %all-to-all-start.5 = ((bf16[8,64,2048]{2,1,0:T(8,128)(2,1)}), bf16[8,64,2048]{2,1,0:T(8,128)(2,1)S(1)}, u32[]{:S(2)}, u32[]{:S(2)}) async-start(bf16[8,64,2048]{2,1,0:T(8,128)(2,1)} %shard_map.275), calls=%async_computation.5 | async-start | bytes 4194304 | tf_op jit(solution)/shard_map/all_to_all | solution.py:56
  353.3 30.9 %all-to-all-start.6 = ((bf16[8,64,2176]{2,1,0:T(8,128)(2,1)}), bf16[8,64,2176]{2,1,0:T(8,128)(2,1)S(1)}, u32[]{:S(2)}, u32[]{:S(2)}) async-start(bf16[8,64,2176]{2,1,0:T(8,128)(2,1)} %get-tuple-element.98.refs_6_), calls=%async_computation.6 | async-start | bytes 4456448 | tf_op jit(solution)/shard_map/all_to_all | solution.py:56
  385.5 30.7 %all-to-all-start.7 = ((bf16[8,64,2176]{2,1,0:T(8,128)(2,1)}), bf16[8,64,2176]{2,1,0:T(8,128)(2,1)S(1)}, u32[]{:S(2)}, u32[]{:S(2)}) async-start(bf16[8,64,2176]{2,1,0:T(8,128)(2,1)} %get-tuple-element.104), calls=%async_computation.7 | async-start | bytes 4456448 | tf_op jit(solution)/shard_map/all_to_all | solution.py:56
  417.6 34.9 %all-to-all-start.8 = ((bf16[8,64,2048]{2,1,0:T(8,128)(2,1)}), bf16[8,64,2048]{2,1,0:T(8,128)(2,1)S(1)}, u32[]{:S(2)}, u32[]{:S(2)}) async-start(bf16[8,64,2048]{2,1,0:T(8,128)(2,1)} %shard_map.286), calls=%async_computation.8 | async-start | bytes 4194304 | tf_op jit(solution)/shard_map/all_to_all | solution.py:56
  421.3 106.1 %reduce-scatter.4.cloned.1.call-start = ((), (), s32[]{:S(2)}) async-start(), calls=%async_computation.16 | async-start | bytes 2621440 | tf_op jit(solution)/shard_map/reduce_scatter | solution.py:1153
  424.6 25.3 %collective-permute-start.28 = (bf16[128,2176]{1,0:T(8,128)(2,1)}, bf16[128,2176]{1,0:T(8,128)(2,1)S(1)}, u32[]{:S(2)}, u32[]{:S(2)}) collective-permute-start(bf16[128,2176]{1,0:T(8,128)(2,1)} %get-tuple-element.106), channel_id=1, source_target_pairs={{0,2},{2,0},{4,6},{6,4},{1,3},{3,1},{5,7},{7,5},{8,10},{10,8},{12,... | collective-permute-start | bytes 1671176 | tf_op jit(solution)/shard_map/ppermute | solution.py:144
  424.9 27.6 %collective-permute-start.27 = (bf16[128,2176]{1,0:T(8,128)(2,1)S(1)}, bf16[128,2176]{1,0:T(8,128)(2,1)}, u32[]{:S(2)}, u32[]{:S(2)}) collective-permute-start(bf16[128,2176]{1,0:T(8,128)(2,1)S(1)} %copy-done.10), channel_id=1, source_target_pairs={{0,4},{2,6},{4,0},{6,2},{1,5},{3,7},{5,1},{7,3},{8,12},{10,14},{12... | collective-permute-start | bytes 1671176 | tf_op jit(solution)/shard_map/ppermute | solution.py:144
  493.8 33.5 %all-to-all-start.9 = ((bf16[8,64,2048]{2,1,0:T(8,128)(2,1)}), bf16[8,64,2048]{2,1,0:T(8,128)(2,1)S(1)}, u32[]{:S(2)}, u32[]{:S(2)}) async-start(bf16[8,64,2048]{2,1,0:T(8,128)(2,1)} %shard_map.290), calls=%async_computation.9 | async-start | bytes 4194304 | tf_op jit(solution)/shard_map/all_to_all | solution.py:56
  497.4 86.2 %reduce-scatter.6.cloned.1.call-start = ((), (), s32[]{:S(2)}) async-start(), calls=%async_computation.17 | async-start | bytes 2621440 | tf_op jit(solution)/shard_map/reduce_scatter | solution.py:1175
  514.5 137.2 %reduce-scatter.8.cloned.1.call-start = ((), (), s32[]{:S(2)}) async-start(), calls=%async_computation.18 | async-start | bytes 3276800 | tf_op jit(solution)/shard_map/reduce_scatter | solution.py:1249
  548.7 25.4 %collective-permute-start.43 = (bf16[4,256,128]{2,1,0:T(8,128)(2,1)S(1)}, bf16[4,256,128]{2,1,0:T(8,128)(2,1)S(1)}, u32[]{:S(2)}, u32[]{:S(2)}) collective-permute-start(bf16[4,256,128]{2,1,0:T(8,128)(2,1)S(1)} %get-tuple-element.186), channel_id=1, source_target_pairs={{0,2},{2,0},{4,6},{6,4},{1,3},{3,1},{5,7},{7,5},{8,10},{10,8},{12,... | collective-permute-start | bytes 786440 | tf_op jit(solution)/shard_map/ppermute | solution.py:144
  601.4 26.4 %all-to-all-start.11 = ((f32[32,1,2184]{2,1,0:T(1,128)}), f32[32,1,2184]{2,1,0:T(1,128)S(1)}, u32[]{:S(2)}, u32[]{:S(2)}) async-start(f32[32,1,2184]{2,1,0:T(1,128)} %copy.82), calls=%async_computation.14 | async-start | bytes 589824 | tf_op jit(solution)/shard_map/all_to_all | solution.py:56
  614.8 43.8 %collective-permute-start.38 = (bf16[128,2048]{1,0:T(8,128)(2,1)}, bf16[128,2048]{1,0:T(8,128)(2,1)S(1)}, u32[]{:S(2)}, u32[]{:S(2)}) collective-permute-start(bf16[128,2048]{1,0:T(8,128)(2,1)} %get-tuple-element.117), channel_id=1, source_target_pairs={{0,2},{2,0},{4,6},{6,4},{1,3},{3,1},{5,7},{7,5},{8,10},{10,8},{12,... | collective-permute-start | bytes 1572872 | tf_op jit(solution)/shard_map/ppermute | solution.py:144
  625.8 32.8 %collective-permute-start.47 = (bf16[128,2048]{1,0:T(8,128)(2,1)}, bf16[128,2048]{1,0:T(8,128)(2,1)S(1)}, u32[]{:S(2)}, u32[]{:S(2)}) collective-permute-start(bf16[128,2048]{1,0:T(8,128)(2,1)} %get-tuple-element.133), channel_id=1, source_target_pairs={{0,16},{1,17},{8,24},{9,25},{16,0},{17,1},{24,8},{25,9},{2,18},{3,... | collective-permute-start | bytes 1572872 | tf_op jit(solution)/shard_map/ppermute | solution.py:92
  626.4 32.2 %collective-permute-start.48 = (bf16[128,2048]{1,0:T(8,128)(2,1)}, bf16[128,2048]{1,0:T(8,128)(2,1)S(1)}, u32[]{:S(2)}, u32[]{:S(2)}) collective-permute-start(bf16[128,2048]{1,0:T(8,128)(2,1)} %get-tuple-element.134), channel_id=1, source_target_pairs={{0,1},{1,0},{8,9},{9,8},{16,17},{17,16},{24,25},{25,24},{2,3},{3,2... | collective-permute-start | bytes 1572872 | tf_op jit(solution)/shard_map/ppermute | solution.py:92
  (116 other events, 872.6 us)
Sparse Core Ops, SparseCore 0:
  9.6 52.3 all-gather.5
  76.7 53.9 all-gather.7
  143.2 44.4 all-gather.9
  462.3 43.0 reduce-scatter.3
  514.7 52.2 reduce-scatter.5
  583.7 68.0 reduce-scatter.7

commit v5 on v4

--- a/solution.py
+++ b/solution.py
@@ -1186,7 +1186,6 @@
         )
     if seq_size == 4:
         near_terms = near_parts = combine(0, results_near, width, second_call[:1])
-        near_terms = [near_terms[0], line_move(near_terms[1], 1)]
     else:
         near_terms = [
             lax.psum_scatter(
@@ -1202,7 +1201,6 @@
                 tiled=False,
             )
         ]
-    result_terms = near_terms + [far_sum.reshape(own_rows, width)]
     grad_query_proj = jnp.concatenate(query_grads)
     grad_query_gain = gain_grads[0] + gain_grads[1]
     kept_grads = [
@@ -1268,6 +1266,9 @@
         info,
         weights_arrived,
     )
+    if seq_size == 4:
+        near_terms = [near_terms[0], line_move(after(near_terms[1], weights_total), 1)]
+    result_terms = near_terms + [far_sum.reshape(own_rows, width)]
     mixed = run(
         mixed_kernel, [row_bf16], info, middle, *result_terms, tokens=plane_terms[1:]
     )[0]

time: 687 us -> 679 us (0.988)
  waiting for transfers between devices: 243 us -> 233 us
    reduce_scatter x1, waiting for transfers between devices: 23.9 us -> 12.9 us  [body(): lax.psum_scatter(jnp.concatenate([query_parts, weight_parts(units, grad_k...]
  transfers between devices with their start and end apart: 66 -> 66, of which waited for: 36 -> 37; matrix products, arithmetic and copies ran while one was open for 7% -> 7% of each run, Pallas kernels for 26% -> 27%
where the time goes in v5:
time: 679 us; the launch traced here: 669 us
  waiting for transfers between devices  233 us (34%)
  Pallas kernels  225 us (33%)
  starting transfers between devices  89.6 us (13%)
  local copies, waits for them, and re-layouts  44.9 us (7%)
  blocking collectives  30.2 us (4%)
  other arithmetic  17 us (3%)
  between operations  15.3 us (2%)
  matrix products  13.3 us (2%)
    pallas_call x36, Pallas kernels, run(): pl.pallas_call(body, in_specs=in_specs, out_specs=[pl.BlockSpec(memory_sp...  167 us
    ppermute x15, waiting for transfers between devices, line_move(): lax.ppermute(block, 'seq', [(place, place ^ bits) for place in range(4)])  102 us
    ppermute x34, waiting for transfers between devices, plane_move(): lax.ppermute(block, PLANE, [(index, index ^ bits) for index in range(8)])  81.7 us
    all_to_all x11, starting transfers between devices, swap(): return lax.all_to_all(blocks, axes, split_axis=0, concat_axis=0, tiled=True)  42.7 us
    all_to_all x11, waiting for transfers between devices, swap(): return lax.all_to_all(blocks, axes, split_axis=0, concat_axis=0, tiled=True)  35.9 us
    ppermute x34, starting transfers between devices, plane_move(): lax.ppermute(block, PLANE, [(index, index ^ bits) for index in range(8)])  31.5 us
    unnamed x153, local copies, waits for them, and re-layouts  30.4 us
    all_to_all x1, blocking collectives, swap(): return lax.all_to_all(blocks, axes, split_axis=0, concat_axis=0, tiled=True)  30.2 us
  transfers between devices with their start and end apart: 66, of which 37 were waited for; matrix products, arithmetic and copies ran while one was open for 7% of the time, Pallas kernels for 27%

profile of v5, /device:TPU:0, one launch (start us, length us, event | category | flops | bytes accessed | tf_op | source)
XLA Modules:
  0.0 669.0 jit_solution(17158685317947285988)
XLA Ops:
  46.3 30.2 %all_to_all.64.refs_1_.refs_2_ = bf16[32,96,128]{2,1,0:T(8,128)(2,1)} all-to-all(bf16[32,96,128]{2,1,0:T(8,128)(2,1)} %shard_map.257), channel_id=1, replica_groups=mesh['dp'=4,'seq'=4,'rep'=2] {'dp','seq','rep'}, dimensions={0} | all-to-all | bytes 1572864 | tf_op jit(solution)/shard_map/all_to_all | solution.py:56
  106.6 23.8 %collective-permute-done.10.refs_2_.refs_4_.refs_10_ = bf16[4,256,128]{2,1,0:T(8,128)(2,1)S(1)} collective-permute-done((bf16[4,256,128]{2,1,0:T(8,128)(2,1)S(1)}, bf16[4,256,128]{2,1,0:T(8,128)(2,1)S(1)}, u32[]{:S(2)}, u32[]{:S(2)}) %collective-permute-start.10) | collective-permute-done | bytes 262176 | tf_op jit(solution)/shard_map/ppermute | solution.py:144
  131.8 8.5 %collective-permute-done.11.refs_3_.refs_2_.refs_11_ = bf16[4,256,128]{2,1,0:T(8,128)(2,1)S(1)} collective-permute-done((bf16[4,256,128]{2,1,0:T(8,128)(2,1)}, bf16[4,256,128]{2,1,0:T(8,128)(2,1)S(1)}, u32[]{:S(2)}, u32[]{:S(2)}) %collective-permute-start.11) | collective-permute-done | bytes 262176 | tf_op jit(solution)/shard_map/ppermute | solution.py:144
  151.1 6.7 %shard_map.260 = (bf16[2048,512]{1,0:T(8,128)(2,1)}, f32[1024,512]{1,0:T(8,128)}) custom-call(s32[8]{0:T(128)} %compare_select_fusion.4.refs_0_.info, bf16[1024,2048]{1,0:T(8,128)(2,1)} %get-tuple-element.82.refs_1_.refs_5_, bf16[4,512,512]{2,1,0:T(8,128)(2,1)} %bitcast.99), custom_call_target="tpu_custom_call" | custom-call | flops 2147483648 | bytes 10485760 | tf_op jit(solution)/shard_map/pallas_call | solution.py:79
  177.1 13.4 %shard_map.263 = (bf16[1024,512]{1,0:T(8,128)(2,1)}, f32[4,4,256,1]{3,2,1,0:T(8,128)}) custom-call(s32[8]{0:T(128)} %compare_select_fusion.4.refs_0_.info, f32[1024,512]{1,0:T(8,128)} %get-tuple-element.83.q_ref.refs_2_.refs_1_, s32[4,256,1]{2,1,0:T(8,128)} %copy.73.qdoc_ref.refs_2_, s32[4,1,1024]{2,1,0:T(1,128)} %bitcast.87, ...), custom_call_target="tpu_custom_call" | custom-call | flops 1000 | bytes 1000 | tf_op jit(solution)/shard_map/pallas_call | solution.py:443
  190.6 9.5 %all-to-all-done.3.refs_3_.refs_1_ = bf16[8,64,2176]{2,1,0:T(8,128)(2,1)S(1)} async-done(((bf16[8,64,2176]{2,1,0:T(8,128)(2,1)}), bf16[8,64,2176]{2,1,0:T(8,128)(2,1)S(1)}, u32[]{:S(2)}, u32[]{:S(2)}) %all-to-all-start.3) | async-done | bytes 2228256 | tf_op jit(solution)/shard_map/all_to_all | solution.py:56
  218.1 6.9 %collective-permute-done.17.refs_3_ = bf16[64,2048]{1,0:T(8,128)(2,1)S(1)} collective-permute-done((bf16[64,2048]{1,0:T(8,128)(2,1)}, bf16[64,2048]{1,0:T(8,128)(2,1)S(1)}, u32[]{:S(2)}, u32[]{:S(2)}) %collective-permute-start.17) | collective-permute-done | bytes 262176 | tf_op jit(solution)/shard_map/ppermute | solution.py:92
  233.0 9.5 %collective-permute-done.19.refs_2_ = bf16[128,2048]{1,0:T(8,128)(2,1)S(1)} collective-permute-done((bf16[128,2048]{1,0:T(8,128)(2,1)}, bf16[128,2048]{1,0:T(8,128)(2,1)S(1)}, u32[]{:S(2)}, u32[]{:S(2)}) %collective-permute-start.19) | collective-permute-done | bytes 524320 | tf_op jit(solution)/shard_map/ppermute | solution.py:92
  249.9 13.1 %collective-permute-done.22.refs_4_.refs_2_ = bf16[64,2048]{1,0:T(8,128)(2,1)S(1)} collective-permute-done((bf16[64,2048]{1,0:T(8,128)(2,1)S(1)}, bf16[64,2048]{1,0:T(8,128)(2,1)S(1)}, u32[]{:S(2)}, u32[]{:S(2)}) %collective-permute-start.22) | collective-permute-done | bytes 262176 | tf_op jit(solution)/shard_map/ppermute | solution.py:144
  275.0 12.9 %collective-permute-done.23.refs_3_ = bf16[64,2048]{1,0:T(8,128)(2,1)S(1)} collective-permute-done((bf16[64,2048]{1,0:T(8,128)(2,1)S(1)}, bf16[64,2048]{1,0:T(8,128)(2,1)S(1)}, u32[]{:S(2)}, u32[]{:S(2)}) %collective-permute-start.23) | collective-permute-done | bytes 262176 | tf_op jit(solution)/shard_map/ppermute | solution.py:144
  290.0 7.2 %collective-permute-done.25.refs_5_ = bf16[64,2048]{1,0:T(8,128)(2,1)S(1)} collective-permute-done((bf16[64,2048]{1,0:T(8,128)(2,1)S(1)}, bf16[64,2048]{1,0:T(8,128)(2,1)S(1)}, u32[]{:S(2)}, u32[]{:S(2)}) %collective-permute-start.25) | collective-permute-done | bytes 262176 | tf_op jit(solution)/shard_map/ppermute | solution.py:144
  318.1 19.1 %all-to-all-done.5.refs_1_ = bf16[8,64,2048]{2,1,0:T(8,128)(2,1)S(1)} async-done(((bf16[8,64,2048]{2,1,0:T(8,128)(2,1)}), bf16[8,64,2048]{2,1,0:T(8,128)(2,1)S(1)}, u32[]{:S(2)}, u32[]{:S(2)}) %all-to-all-start.5) | async-done | bytes 2097184 | tf_op jit(solution)/shard_map/all_to_all | solution.py:56
  338.6 14.7 %shard_map.277 = (bf16[512,1536]{1,0:T(8,128)(2,1)}, bf16[512,768]{1,0:T(8,128)(2,1)}, bf16[8,64,2176]{2,1,0:T(8,128)(2,1)}) custom-call(s32[8]{0:T(128)} %compare_select_fusion.4.refs_0_.info, bf16[8,64,2048]{2,1,0:T(8,128)(2,1)} %copy-done.11, f32[512,768]{1,0:T(8,128)} %shard_map.276.refs_2_, bf16[8,64,2176]{2,1,0:T(8,128)(2,1)} %copy-done.4, ...), custom_call_target="tpu_custom_call" | custom-call | flops 6442450944 | bytes 16908288 | tf_op jit(solution)/shard_map/pallas_call | solution.py:79
  362.7 14.8 %shard_map.278 = (bf16[512,1536]{1,0:T(8,128)(2,1)}, bf16[512,768]{1,0:T(8,128)(2,1)}, bf16[8,64,2176]{2,1,0:T(8,128)(2,1)}) custom-call(s32[8]{0:T(128)} %compare_select_fusion.4.refs_0_.info, bf16[8,64,2048]{2,1,0:T(8,128)(2,1)} %copy-done.6, f32[512,768]{1,0:T(8,128)} %shard_map.274.refs_2_, bf16[8,64,2176]{2,1,0:T(8,128)(2,1)} %copy-done.3, ...), custom_call_target="tpu_custom_call" | custom-call | flops 6442450944 | bytes 16908288 | tf_op jit(solution)/shard_map/pallas_call | solution.py:79
  377.4 6.8 %all-to-all-done.6.refs_2_ = bf16[8,64,2176]{2,1,0:T(8,128)(2,1)S(1)} async-done(((bf16[8,64,2176]{2,1,0:T(8,128)(2,1)}), bf16[8,64,2176]{2,1,0:T(8,128)(2,1)S(1)}, u32[]{:S(2)}, u32[]{:S(2)}) %all-to-all-start.6) | async-done | bytes 2228256 | tf_op jit(solution)/shard_map/all_to_all | solution.py:56
  392.6 7.8 %shard_map.280.refs_3_.refs_13_ = f32[1,768,2048]{2,1,0:T(8,128)} custom-call(bf16[512,768]{1,0:T(8,128)(2,1)} %get-tuple-element.99.refs_0_.refs_2_, bf16[512,768]{1,0:T(8,128)(2,1)} %get-tuple-element.102.refs_1_.refs_2_, bf16[8,64,2176]{2,1,0:T(8,128)(2,1)} %copy-done.3, bf16[8,64,2176]{2,1,0:T(8,128)(2,1)} %copy-done.4, ...), custom_call_target="tpu_custom_call" | custom-call | flops 1000 | bytes 1000 | tf_op jit(solution)/shard_map/pallas_call | solution.py:747
  400.4 7.1 %collective-permute-done.26.refs_2_ = bf16[128,2176]{1,0:T(8,128)(2,1)S(1)} collective-permute-done((bf16[128,2176]{1,0:T(8,128)(2,1)}, bf16[128,2176]{1,0:T(8,128)(2,1)S(1)}, u32[]{:S(2)}, u32[]{:S(2)}) %collective-permute-start.26) | collective-permute-done | bytes 557088 | tf_op jit(solution)/shard_map/ppermute | solution.py:144
  434.7 11.4 %shard_map.285.refs_11_ = f32[1,2048,1536]{2,1,0:T(8,128)} custom-call(bf16[512,2048]{1,0:T(8,128)(2,1)} %bitcast.59, bf16[512,2048]{1,0:T(8,128)(2,1)} %bitcast.60, bf16[512,1536]{1,0:T(8,128)(2,1)} %get-tuple-element.107.refs_2_, bf16[512,1536]{1,0:T(8,128)(2,1)} %get-tuple-element.108.refs_3_, bf16[128,2176]{1,0:T(8,128)(2,1)} %get-tuple-element.105.refs_4_.refs_8_), custom_call_target="tpu_custom_call" | custom-call | flops 1000 | bytes 1000 | tf_op jit(solution)/shard_map/pallas_call | solution.py:722
  466.4 10.0 %collective-permute-done.32.refs_6_ = bf16[128,2048]{1,0:T(8,128)(2,1)S(1)} collective-permute-done((bf16[128,2048]{1,0:T(8,128)(2,1)S(1)}, bf16[128,2048]{1,0:T(8,128)(2,1)S(1)}, u32[]{:S(2)}, u32[]{:S(2)}) %collective-permute-start.32) | collective-permute-done | bytes 524320 | tf_op jit(solution)/shard_map/ppermute | solution.py:92
  497.5 10.9 %shard_map.291 = (bf16[512,512]{1,0:T(8,128)(2,1)}, bf16[4,2,256,128]{3,2,1,0:T(8,128)(2,1)}, bf16[4,2,256,128]{3,2,1,0:T(8,128)(2,1)}, f32[1,128]{1,0:T(1,128)}) custom-call(s32[8]{0:T(128)} %compare_select_fusion.4.refs_0_.info, f32[1024,512]{1,0:T(8,128)} %get-tuple-element.83.q_ref.refs_2_.refs_1_, s32[4,256,1]{2,1,0:T(8,128)} %copy.73.qdoc_ref.refs_2_, ...), custom_call_target="tpu_custom_call" | custom-call | flops 1000 | bytes 1000 | tf_op jit(solution)/shard_map/pallas_call | solution.py:479
  516.6 10.7 %shard_map.293 = (bf16[512,512]{1,0:T(8,128)(2,1)}, bf16[4,2,256,128]{3,2,1,0:T(8,128)(2,1)}, bf16[4,2,256,128]{3,2,1,0:T(8,128)(2,1)}, f32[1,128]{1,0:T(1,128)}) custom-call(s32[8]{0:T(128)} %compare_select_fusion.4.refs_0_.info, f32[1024,512]{1,0:T(8,128)} %get-tuple-element.83.q_ref.refs_2_.refs_1_, s32[4,256,1]{2,1,0:T(8,128)} %copy.73.qdoc_ref.refs_2_, ...), custom_call_target="tpu_custom_call" | custom-call | flops 1000 | bytes 1000 | tf_op jit(solution)/shard_map/pallas_call | solution.py:479
  534.9 10.6 %collective-permute-done.39 = bf16[4,2,256,128]{3,2,1,0:T(8,128)(2,1)S(1)} collective-permute-done((bf16[4,2,256,128]{3,2,1,0:T(8,128)(2,1)}, bf16[4,2,256,128]{3,2,1,0:T(8,128)(2,1)S(1)}, u32[]{:S(2)}, u32[]{:S(2)}) %collective-permute-start.39) | collective-permute-done | bytes 524320 | tf_op jit(solution)/shard_map/ppermute | solution.py:92
  550.8 11.0 %collective-permute-done.40 = bf16[4,256,128]{2,1,0:T(8,128)(2,1)S(1)} collective-permute-done((bf16[4,256,128]{2,1,0:T(8,128)(2,1)}, bf16[4,256,128]{2,1,0:T(8,128)(2,1)S(1)}, u32[]{:S(2)}, u32[]{:S(2)}) %collective-permute-start.40) | collective-permute-done | bytes 262176 | tf_op jit(solution)/shard_map/ppermute | solution.py:144
  627.8 12.9 %reduce-scatter.6.cloned.1.call-done = bf16[1,4,128,640]{3,2,1,0:T(8,128)(2,1)} async-done(((bf16[4,4,128,640]{3,2,1,0:T(8,128)(2,1)}), bf16[1,4,128,640]{3,2,1,0:T(8,128)(2,1)}) %reduce-scatter.6.cloned.1.call-update) | async-done | bytes 655376 | tf_op jit(solution)/shard_map/reduce_scatter | solution.py:1247
  (386 shorter events, 364.3 us)
Async XLA Ops:
  7.2 69.3 %all-gather.6.cloned.1.call-start = ((), (), s32[]{:S(2)}) async-start(), calls=%async_computation.15 | async-start | bytes 2621440 | tf_op jit(solution)/shard_map/all_gather | solution.py:858
  29.0 122.2 %all-gather.8.cloned.1.call-start = ((), (), s32[]{:S(2)}) async-start(), calls=%async_computation.19 | async-start | bytes 2621440 | tf_op jit(solution)/shard_map/all_gather | solution.py:883
  101.6 65.9 %all-to-all-start.2 = ((bf16[8,64,2176]{2,1,0:T(8,128)(2,1)}), bf16[8,64,2176]{2,1,0:T(8,128)(2,1)S(1)}, u32[]{:S(2)}, u32[]{:S(2)}) async-start(bf16[8,64,2176]{2,1,0:T(8,128)(2,1)} %shard_map.266), calls=%async_computation.2 | async-start | bytes 4456448 | tf_op jit(solution)/shard_map/all_to_all | solution.py:56
  105.3 85.3 %all-gather.10.cloned.1.call-start = ((), (), s32[]{:S(2)}) async-start(), calls=%async_computation.20 | async-start | bytes 2621440 | tf_op jit(solution)/shard_map/all_gather | solution.py:951
  105.4 25.0 %collective-permute-start.10 = (bf16[4,256,128]{2,1,0:T(8,128)(2,1)S(1)}, bf16[4,256,128]{2,1,0:T(8,128)(2,1)S(1)}, u32[]{:S(2)}, u32[]{:S(2)}) collective-permute-start(bf16[4,256,128]{2,1,0:T(8,128)(2,1)S(1)} %copy-done.16), channel_id=1, source_target_pairs={{0,4},{2,6},{4,0},{6,2},{1,5},{3,7},{5,1},{7,3},{8,12},{10,14},{12... | collective-permute-start | bytes 786440 | tf_op jit(solution)/shard_map/ppermute | solution.py:144
  105.4 25.6 %collective-permute-start.9 = (bf16[4,256,128]{2,1,0:T(8,128)(2,1)S(1)}, bf16[4,256,128]{2,1,0:T(8,128)(2,1)S(1)}, u32[]{:S(2)}, u32[]{:S(2)}) collective-permute-start(bf16[4,256,128]{2,1,0:T(8,128)(2,1)S(1)} %copy-done.16), channel_id=1, source_target_pairs={{0,2},{2,0},{4,6},{6,4},{1,3},{3,1},{5,7},{7,5},{8,10},{10,8},{12,... | collective-permute-start | bytes 786440 | tf_op jit(solution)/shard_map/ppermute | solution.py:144
  146.7 20.8 %collective-permute-start.15 = (bf16[4,256,128]{2,1,0:T(8,128)(2,1)}, bf16[4,256,128]{2,1,0:T(8,128)(2,1)}, u32[]{:S(2)}, u32[]{:S(2)}) collective-permute-start(bf16[4,256,128]{2,1,0:T(8,128)(2,1)} %copy-done.18), channel_id=1, source_target_pairs={{0,1},{1,0},{8,9},{9,8},{16,17},{17,16},{24,25},{25,24},{2,3},{3,2... | collective-permute-start | bytes 786440 | tf_op jit(solution)/shard_map/ppermute | solution.py:92
  168.8 31.2 %all-to-all-start.3 = ((bf16[8,64,2176]{2,1,0:T(8,128)(2,1)}), bf16[8,64,2176]{2,1,0:T(8,128)(2,1)S(1)}, u32[]{:S(2)}, u32[]{:S(2)}) async-start(bf16[8,64,2176]{2,1,0:T(8,128)(2,1)} %shard_map.267), calls=%async_computation.3 | async-start | bytes 4456448 | tf_op jit(solution)/shard_map/all_to_all | solution.py:56
  269.0 32.6 %all-to-all-start.4 = ((bf16[8,64,2048]{2,1,0:T(8,128)(2,1)}), bf16[8,64,2048]{2,1,0:T(8,128)(2,1)S(1)}, u32[]{:S(2)}, u32[]{:S(2)}) async-start(bf16[8,64,2048]{2,1,0:T(8,128)(2,1)} %shard_map.273), calls=%async_computation.4 | async-start | bytes 4194304 | tf_op jit(solution)/shard_map/all_to_all | solution.py:56
  307.0 30.2 %all-to-all-start.5 = ((bf16[8,64,2048]{2,1,0:T(8,128)(2,1)}), bf16[8,64,2048]{2,1,0:T(8,128)(2,1)S(1)}, u32[]{:S(2)}, u32[]{:S(2)}) async-start(bf16[8,64,2048]{2,1,0:T(8,128)(2,1)} %shard_map.275), calls=%async_computation.5 | async-start | bytes 4194304 | tf_op jit(solution)/shard_map/all_to_all | solution.py:56
  353.3 30.9 %all-to-all-start.6 = ((bf16[8,64,2176]{2,1,0:T(8,128)(2,1)}), bf16[8,64,2176]{2,1,0:T(8,128)(2,1)S(1)}, u32[]{:S(2)}, u32[]{:S(2)}) async-start(bf16[8,64,2176]{2,1,0:T(8,128)(2,1)} %get-tuple-element.98.refs_6_), calls=%async_computation.6 | async-start | bytes 4456448 | tf_op jit(solution)/shard_map/all_to_all | solution.py:56
  385.6 30.7 %all-to-all-start.7 = ((bf16[8,64,2176]{2,1,0:T(8,128)(2,1)}), bf16[8,64,2176]{2,1,0:T(8,128)(2,1)S(1)}, u32[]{:S(2)}, u32[]{:S(2)}) async-start(bf16[8,64,2176]{2,1,0:T(8,128)(2,1)} %get-tuple-element.104), calls=%async_computation.7 | async-start | bytes 4456448 | tf_op jit(solution)/shard_map/all_to_all | solution.py:56
  417.6 34.9 %all-to-all-start.8 = ((bf16[8,64,2048]{2,1,0:T(8,128)(2,1)}), bf16[8,64,2048]{2,1,0:T(8,128)(2,1)S(1)}, u32[]{:S(2)}, u32[]{:S(2)}) async-start(bf16[8,64,2048]{2,1,0:T(8,128)(2,1)} %shard_map.286), calls=%async_computation.8 | async-start | bytes 4194304 | tf_op jit(solution)/shard_map/all_to_all | solution.py:56
  421.3 106.1 %reduce-scatter.4.cloned.1.call-start = ((), (), s32[]{:S(2)}) async-start(), calls=%async_computation.16 | async-start | bytes 2621440 | tf_op jit(solution)/shard_map/reduce_scatter | solution.py:1153
  424.6 25.3 %collective-permute-start.28 = (bf16[128,2176]{1,0:T(8,128)(2,1)}, bf16[128,2176]{1,0:T(8,128)(2,1)S(1)}, u32[]{:S(2)}, u32[]{:S(2)}) collective-permute-start(bf16[128,2176]{1,0:T(8,128)(2,1)} %get-tuple-element.106), channel_id=1, source_target_pairs={{0,2},{2,0},{4,6},{6,4},{1,3},{3,1},{5,7},{7,5},{8,10},{10,8},{12,... | collective-permute-start | bytes 1671176 | tf_op jit(solution)/shard_map/ppermute | solution.py:144
  424.9 27.6 %collective-permute-start.27 = (bf16[128,2176]{1,0:T(8,128)(2,1)S(1)}, bf16[128,2176]{1,0:T(8,128)(2,1)}, u32[]{:S(2)}, u32[]{:S(2)}) collective-permute-start(bf16[128,2176]{1,0:T(8,128)(2,1)S(1)} %copy-done.10), channel_id=1, source_target_pairs={{0,4},{2,6},{4,0},{6,2},{1,5},{3,7},{5,1},{7,3},{8,12},{10,14},{12... | collective-permute-start | bytes 1671176 | tf_op jit(solution)/shard_map/ppermute | solution.py:144
  493.8 33.5 %all-to-all-start.9 = ((bf16[8,64,2048]{2,1,0:T(8,128)(2,1)}), bf16[8,64,2048]{2,1,0:T(8,128)(2,1)S(1)}, u32[]{:S(2)}, u32[]{:S(2)}) async-start(bf16[8,64,2048]{2,1,0:T(8,128)(2,1)} %shard_map.290), calls=%async_computation.9 | async-start | bytes 4194304 | tf_op jit(solution)/shard_map/all_to_all | solution.py:56
  497.4 86.2 %reduce-scatter.8.cloned.1.call-start = ((), (), s32[]{:S(2)}) async-start(), calls=%async_computation.18 | async-start | bytes 2621440 | tf_op jit(solution)/shard_map/reduce_scatter | solution.py:1175
  514.6 126.1 %reduce-scatter.6.cloned.1.call-start = ((), (), s32[]{:S(2)}) async-start(), calls=%async_computation.17 | async-start | bytes 3276800 | tf_op jit(solution)/shard_map/reduce_scatter | solution.py:1247
  514.6 20.1 %collective-permute-start.38 = (bf16[4,2,256,128]{3,2,1,0:T(8,128)(2,1)}, bf16[4,2,256,128]{3,2,1,0:T(8,128)(2,1)S(1)}, u32[]{:S(2)}, u32[]{:S(2)}) collective-permute-start(bf16[4,2,256,128]{3,2,1,0:T(8,128)(2,1)} %get-tuple-element.121), channel_id=1, source_target_pairs={{0,1},{1,0},{8,9},{9,8},{16,17},{17,16},{24,25},{25,24},{2,3},{3,2... | collective-permute-start | bytes 1572872 | tf_op jit(solution)/shard_map/ppermute | solution.py:92
  548.7 25.3 %collective-permute-start.42 = (bf16[4,256,128]{2,1,0:T(8,128)(2,1)S(1)}, bf16[4,256,128]{2,1,0:T(8,128)(2,1)S(1)}, u32[]{:S(2)}, u32[]{:S(2)}) collective-permute-start(bf16[4,256,128]{2,1,0:T(8,128)(2,1)S(1)} %get-tuple-element.186), channel_id=1, source_target_pairs={{0,2},{2,0},{4,6},{6,4},{1,3},{3,1},{5,7},{7,5},{8,10},{10,8},{12,... | collective-permute-start | bytes 786440 | tf_op jit(solution)/shard_map/ppermute | solution.py:144
  601.5 41.5 %all-to-all-start.11 = ((f32[32,1,2184]{2,1,0:T(1,128)}), f32[32,1,2184]{2,1,0:T(1,128)S(1)}, u32[]{:S(2)}, u32[]{:S(2)}) async-start(f32[32,1,2184]{2,1,0:T(1,128)} %copy.83), calls=%async_computation.14 | async-start | bytes 589824 | tf_op jit(solution)/shard_map/all_to_all | solution.py:56
  625.9 24.0 %collective-permute-start.47 = (bf16[128,2048]{1,0:T(8,128)(2,1)}, bf16[128,2048]{1,0:T(8,128)(2,1)S(1)}, u32[]{:S(2)}, u32[]{:S(2)}) collective-permute-start(bf16[128,2048]{1,0:T(8,128)(2,1)} %get-tuple-element.133), channel_id=1, source_target_pairs={{0,16},{1,17},{8,24},{9,25},{16,0},{17,1},{24,8},{25,9},{2,18},{3,... | collective-permute-start | bytes 1572872 | tf_op jit(solution)/shard_map/ppermute | solution.py:92
  626.4 23.5 %collective-permute-start.48 = (bf16[128,2048]{1,0:T(8,128)(2,1)}, bf16[128,2048]{1,0:T(8,128)(2,1)S(1)}, u32[]{:S(2)}, u32[]{:S(2)}) collective-permute-start(bf16[128,2048]{1,0:T(8,128)(2,1)} %get-tuple-element.134), channel_id=1, source_target_pairs={{0,1},{1,0},{8,9},{9,8},{16,17},{17,16},{24,25},{25,24},{2,3},{3,2... | collective-permute-start | bytes 1572872 | tf_op jit(solution)/shard_map/ppermute | solution.py:92
  (116 other events, 825.1 us)
Sparse Core Ops, SparseCore 0:
  9.6 52.3 all-gather.5
  76.7 53.4 all-gather.7
  143.1 44.5 all-gather.9
  462.3 43.0 reduce-scatter.3
  514.7 52.4 reduce-scatter.7
  583.8 56.8 reduce-scatter.5
